TPU v7x, 32 devices: a whole 2x2x4 slice. The times are simulated.
32 devices in a mesh: row: 8 (over z, x), col: 4 (over y, core).
Axes of the slice: x: 2, y: 2, z: 4, core: 2. Of those that a mesh axis runs over, the one named last changes fastest.
Arguments:
- traces: bfloat16 [32, 512, 512], P(None, 'row', 'col'), may hold values from -6 to 6
- source_pos: int32 [512], P('row'), may hold values from 0 to 4095
- receiver_pos: int32 [512], replicated, may hold values from 0 to 4095
- aperture_list: int32 [32, 256], P('row'), may hold values from 0 to 511, as said below
- band_index: int32 [4096], P('row'), may hold values from 0 to 31
- weight_tiles: bfloat16 [32, 8, 128], replicated, may hold values from -2 to 2
Outputs:
- primaries: bfloat16 [32, 512, 512], P(None, 'row', 'col')
- image: float32 [512, 4096], P('col', 'row')
Inputs may be any that keep to these rules, and one draw needn't show every extreme that they name: `aperture_list`: the 256 receivers listed for one tile are distinct.
All inputs are finite; a program needn't handle non-finite values.
Results may differ from a plain program's by a relative error of at most 0.012.
Values may be sent and summed in bfloat16 or wider, within the bound.
No kernel may reach another device: no remote copies, remote signals or barrier semaphores. Data moves between devices by JAX's collectives and lax.ppermute only.
A program may use at most 64 MiB of HBM per device.

v0:
```python
import math

import jax
import jax.numpy as jnp
from jax import lax
from jax.sharding import PartitionSpec as P

NFFT = 4096
NF = 4


def phase_tables(samples):
    freq_bins = (2 * jnp.arange(NF, dtype=jnp.int32) + 1) * (NFFT // (4 * NF))
    sample_ticks = jnp.arange(samples, dtype=jnp.int32)
    phase_turns = freq_bins[:, None] * sample_ticks[None, :] % NFFT
    phase_angle = phase_turns.astype(jnp.float32) * (2.0 * math.pi / NFFT)
    return (jnp.cos(phase_angle), jnp.sin(phase_angle))


def aperture_matrix(tile_index_lists, positions, columns, first_row, row_count, spread_len):
    tile_count, listed = tile_index_lists.shape
    col_width = columns.shape[0]
    inside = (tile_index_lists >= first_row) & (tile_index_lists < first_row + row_count)
    local_index = jnp.where(inside, tile_index_lists - first_row, row_count)
    tile_rows = jnp.broadcast_to(
        jnp.arange(tile_count, dtype=jnp.int32)[:, None], tile_index_lists.shape
    )
    member = (
        jnp.zeros((tile_count, row_count), jnp.float32)
        .at[tile_rows, local_index]
        .add(1.0, mode="drop")
    )
    widened = jnp.repeat(member.T, col_width // tile_count, axis=1)
    offset = (positions[:, None] - columns[None, :]).astype(jnp.float32) / spread_len
    taper_weight = 1.0 / (1.0 + offset * offset)
    return (widened * taper_weight * (2.0 / math.sqrt(listed))).astype(jnp.bfloat16)


def shot_weights(positions, columns, spread_len):
    offset = (positions[:, None] - columns[None, :]).astype(jnp.float32) / spread_len
    return 1.0 / (1.0 + offset * offset)


def complex_product(left_section, right_section):
    real_real = jnp.einsum(
        "qju,quy->qjy", left_section[0], right_section[0], preferred_element_type=jnp.float32
    )
    imag_imag = jnp.einsum(
        "qju,quy->qjy", left_section[1], right_section[1], preferred_element_type=jnp.float32
    )
    real_imag = jnp.einsum(
        "qju,quy->qjy", left_section[0], right_section[1], preferred_element_type=jnp.float32
    )
    imag_real = jnp.einsum(
        "qju,quy->qjy", left_section[1], right_section[0], preferred_element_type=jnp.float32
    )
    return jnp.stack([real_real - imag_imag, real_imag + imag_real])


def slab_stack(slab_block, aperture, stacking_weights):
    depth_slab_samples, shot_count, listed_rows = slab_block.shape
    stacked = jnp.dot(
        slab_block.reshape(depth_slab_samples * shot_count, listed_rows),
        aperture,
        preferred_element_type=jnp.float32,
    )
    stacked = stacked.reshape(depth_slab_samples, shot_count, aperture.shape[1])
    return jnp.sum(stacked * stacking_weights[None], axis=1)


def per_device(traces, source_pos, receiver_pos, aperture_list, band_index, weight_tiles):
    samples, shot_count, recv_count = traces.shape
    col_count = lax.axis_size("col")
    surface_count = recv_count * col_count
    image_panel_width = band_index.shape[0]
    depth_slab_samples = samples // col_count
    cosine, sine_table = phase_tables(samples)
    forward = (jnp.concatenate([cosine, -sine_table], 0) / math.sqrt(samples)).astype(jnp.bfloat16)
    spectra = jnp.dot(
        forward,
        traces.reshape(samples, shot_count * recv_count),
        preferred_element_type=jnp.float32,
    )
    spectra = spectra.astype(jnp.bfloat16).reshape(2, NF, shot_count, recv_count)
    columns_whole = lax.all_gather(spectra, "row", axis=2, tiled=True)
    summed = complex_product(lax.all_gather(spectra, "col", axis=3, tiled=True), columns_whole)
    multiples = -summed / math.sqrt(surface_count)
    inverse = jnp.concatenate([cosine, -sine_table], 0).T / math.sqrt(NF)
    wave_field = jnp.dot(
        inverse,
        multiples.reshape(2 * NF, shot_count * recv_count),
        precision=lax.Precision.HIGHEST,
        preferred_element_type=jnp.float32,
    )
    primaries = (
        traces.astype(jnp.float32) - wave_field.reshape(samples, shot_count, recv_count)
    ).astype(jnp.bfloat16)
    columns = lax.axis_index("row") * image_panel_width + jnp.arange(
        image_panel_width, dtype=jnp.int32
    )
    spread_len = image_panel_width * lax.axis_size("row") // 4
    stacking_weights = shot_weights(source_pos, columns, spread_len)
    slab_block = lax.all_to_all(primaries, "col", split_axis=0, concat_axis=2, tiled=True)
    aperture = aperture_matrix(aperture_list, receiver_pos, columns, 0, surface_count, spread_len)
    stacked = slab_stack(slab_block, aperture, stacking_weights)
    column_stack = (stacked / math.sqrt(shot_count)).astype(jnp.bfloat16)
    tile_kinds = weight_tiles.shape[0]
    select = band_index[None, :] == jnp.arange(tile_kinds, dtype=jnp.int32)[:, None]
    widened = jnp.where(select[:, None, :], column_stack[None], jnp.zeros((), jnp.bfloat16))
    image_out = jnp.einsum(
        "kz,kx->zx",
        weight_tiles.reshape(tile_kinds * depth_slab_samples, weight_tiles.shape[2]),
        widened.reshape(tile_kinds * depth_slab_samples, image_panel_width),
        preferred_element_type=jnp.float32,
    )
    return (primaries, image_out)


def solution(mesh):
    placed = (P(None, "row", "col"), P("row"), P(), P("row", None), P("row"), P())
    return jax.shard_map(
        per_device,
        mesh=mesh,
        in_specs=placed,
        out_specs=(P(None, "row", "col"), P("col", "row")),
        check_vma=False,
    )
```

profile of v0, /device:TPU:0, one launch (start us, length us, event | category | flops | bytes accessed | tf_op | source)
XLA Modules:
  0.0 81.6 jit_solution(6389623279304152867)
XLA Ops:
  7.2 0.0 copy-start
  7.2 0.0 all-gather.2.cloned.1.call-start
  7.2 0.1 fusion.26
  7.4 1.4 %fusion.4 = bf16[1,8,64,128]{3,1,2,0:T(8,128)(2,1)S(1)} fusion(bf16[4,8,64,128]{3,2,1,0:T(8,128)(2,1)} %bitcast.57, f32[4,32]{1,0:T(4,128)S(1)} %get-tuple-element.11, f32[4,32]{1,0:T(4,128)S(1)} %get-tuple-element.10), kind=kOutput, calls=%fused_computation.11 | convolution fusion | flops 4260608 | bytes 656384 | tf_op jit(solution)/shard_map/dot_general | solution.py:79
  8.8 0.7 copy.33
  9.5 0.0 copy-start.4
  9.5 0.0 all-gather.2.cloned.1.call-update
  9.5 0.7 copy-done.4
  10.2 0.0 copy-start.8
  10.2 0.6 copy-done.8
  10.8 0.0 copy-start.9
  10.8 0.1 multiply_reduce_fusion
  10.9 0.6 copy-done.9
  11.5 0.1 and_reduce_fusion
  11.6 7.6 %scatter_custom_fusion = f32[2048]{0:T(1024)S(1)} fusion(s32[1024]{0:T(1024)S(1)} %bitcast.64, f32[1024]{0:T(1024)S(1)} %broadcast.205, f32[]{:T(128)} %constant.55.clone.1), kind=kCustom, calls=%fused_computation.41 | custom fusion | flops 1024 | bytes 8196
  19.2 0.0 copy-start.2
  19.2 0.2 copy.28
  19.4 0.7 copy-done.2
  20.1 0.0 copy-start.5
  20.1 8.8 %all_gather.6 = bf16[2,4,64,512]{3,2,1,0:T(8,128)(2,1)S(1)} all-gather(bf16[2,4,64,128]{3,2,1,0:T(8,128)(2,1)S(1)} %bitcast.61), channel_id=1, replica_groups=mesh['row'=8,'col'=4] {'col'}, dimensions={3}, use_global_device_ids=true | all-gather | bytes 655360 | tf_op jit(solution)/shard_map/all_gather | solution.py:86
  28.9 0.0 copy-done.5
  28.9 1.9 %multiply_convert_fusion = bf16[512,4,128]{2,1,0:T(4,128)(2,1)S(1)} fusion(s32[4,128]{1,0:T(4,128)S(1)} %add_add_fusion, s32[512]{0:T(512)S(1)} %copy-done.5, f32[512,4]{1,0:T(8,128)S(1)} %copy.28), kind=kLoop, calls=%fused_computation.12 | loop fusion | flops 2359296 | bytes 536576 | tf_op jit(solution)/shard_map/convert_element_type | solution.py:36
  30.8 22.9 %all-gather.2.cloned.1.call-done = bf16[2,4,512,128]{3,2,1,0:T(8,128)(2,1)} async-done(((bf16[2,4,64,128]{3,2,1,0:T(8,128)(2,1)}), bf16[2,4,512,128]{3,2,1,0:T(8,128)(2,1)}) %all-gather.2.cloned.1.call-update) | async-done | bytes 1048592 | tf_op jit(solution)/shard_map/all_gather | solution.py:85
  53.7 0.0 copy-start.3
  53.7 1.3 %fusion.7 = f32[4,64,128]{2,1,0:T(8,128)S(1)} fusion(bf16[2,4,512,128]{3,2,1,0:T(8,128)(2,1)} %all-gather.2.cloned.1.call-done, bf16[2,4,64,512]{3,2,1,0:T(8,128)(2,1)S(1)} %all_gather.6), kind=kOutput, calls=%fused_computation.18 | convolution fusion | flops 33554432 | bytes 917504 | tf_op jit(solution)/shard_map/qju,quy->qjy/dot_general | solution.py:45
  55.1 1.3 %fusion.8 = f32[4,64,128]{2,1,0:T(8,128)S(1)} fusion(bf16[2,4,512,128]{3,2,1,0:T(8,128)(2,1)} %all-gather.2.cloned.1.call-done, bf16[2,4,64,512]{3,2,1,0:T(8,128)(2,1)S(1)} %all_gather.6), kind=kOutput, calls=%fused_computation.19 | convolution fusion | flops 33554432 | bytes 917504 | tf_op jit(solution)/shard_map/qju,quy->qjy/dot_general | solution.py:51
  56.3 0.0 copy-done.3
  56.3 0.2 fusion.3
  56.6 0.2 fusion.2
  56.8 0.0 copy-start.1
  56.8 1.0 %copy-done.1 = bf16[32,64,128]{2,1,0:T(8,128)(2,1)S(1)} copy-done((bf16[32,64,128]{2,1,0:T(8,128)(2,1)S(1)}, bf16[32,64,128]{2,1,0:T(8,128)(2,1)}, u32[]{:S(2)}) %copy-start.1) | copy-done | bytes 524312
  57.8 1.3 %fusion = bf16[32,64,128]{2,0,1:T(8,128)(2,1)S(1)} fusion(bf16[32,64,128]{2,1,0:T(8,128)(2,1)S(1)} %copy-done.1, f32[1,8,64,128]{3,2,1,0:T(8,128)S(1)} %bitcast.62, f32[4,32]{1,0:T(4,128)S(1)} %get-tuple-element.11, f32[4,32]{1,0:T(4,128)S(1)} %get-tuple-element.10), kind=kOutput, calls=%fused_computation.4 | convolution fusion | flops 25952768 | bytes 1311744 | tf_op jit(solution)/shard_map/dot_general | solution.py:89
  59.1 1.0 %copy.30 = bf16[32,64,128]{2,1,0:T(8,128)(2,1)} copy(bf16[32,64,128]{2,0,1:T(8,128)(2,1)S(1)} %fusion) | data formatting | bytes 1048576
  60.1 0.0 copy-start.6
  60.1 3.6 %all-to-all-start = ((bf16[32,64,128]{2,1,0:T(8,128)(2,1)}), bf16[32,64,128]{2,1,0:T(8,128)(2,1)S(1)}, u32[]{:S(2)}, u32[]{:S(2)}) async-start(bf16[32,64,128]{2,1,0:T(8,128)(2,1)} %copy.30), calls=%async_computation | async-start | bytes 1048576 | tf_op jit(solution)/shard_map/all_to_all | solution.py:103
  63.7 0.0 copy-done.6
  63.8 0.2 reshape.161
  64.0 0.0 copy-start.7
  64.0 0.6 copy-done.7
  64.6 0.1 add_divide_fusion
  64.7 7.8 %all-to-all-done = bf16[32,64,128]{2,1,0:T(8,128)(2,1)S(1)} async-done(((bf16[32,64,128]{2,1,0:T(8,128)(2,1)}), bf16[32,64,128]{2,1,0:T(8,128)(2,1)S(1)}, u32[]{:S(2)}, u32[]{:S(2)}) %all-to-all-start) | async-done | bytes 524320 | tf_op jit(solution)/shard_map/all_to_all | solution.py:103
  72.5 0.4 copy.48
  73.0 0.2 dot_general.40
  73.2 0.4 fusion.1
  73.6 0.0 copy-done
  73.6 0.3 convolution_bitcast_fusion
  73.9 0.8 %copy.31 = f32[128,512]{1,0:T(8,128)} copy(f32[128,512]{0,1:T(8,128)S(1)} %convolution_bitcast_fusion) | data formatting | bytes 524288
  (12 shorter events, 0.1 us)
Async XLA Ops:
  7.2 66.5 %copy-start = (bf16[32,8,128]{2,1,0:T(8,128)(2,1)S(1)}, bf16[32,8,128]{2,1,0:T(8,128)(2,1)}, u32[]{:S(2)}) copy-start(bf16[32,8,128]{2,1,0:T(8,128)(2,1)} %param.11) | copy-start | bytes 196612
  7.2 46.5 %all-gather.2.cloned.1.call-start = ((), (), s32[]{:S(2)}) async-start(), calls=%async_computation.1 | async-start | bytes 1179648 | tf_op jit(solution)/shard_map/all_gather | solution.py:85
  9.5 0.7 copy-start.4
  10.2 0.7 copy-start.8
  10.8 0.7 copy-start.9
  19.2 0.9 %copy-start.2 = (bf16[1,8,64,128]{3,2,1,0:T(8,128)(2,1)S(1)}, bf16[1,8,64,128]{3,2,1,0:T(8,128)(2,1)}, u32[]{:S(2)}) copy-start(bf16[1,8,64,128]{3,2,1,0:T(8,128)(2,1)} %copy.33) | copy-start | bytes 393220
  20.1 8.8 %copy-start.5 = (s32[512]{0:T(512)S(1)}, s32[512]{0:T(512)}, u32[]{:S(2)}) copy-start(s32[512]{0:T(512)} %param.8) | copy-start | bytes 6148
  53.7 2.6 %copy-start.3 = (bf16[2,4,512,128]{3,2,1,0:T(8,128)(2,1)S(1)}, bf16[2,4,512,128]{3,2,1,0:T(8,128)(2,1)}, u32[]{:S(2)}) copy-start(bf16[2,4,512,128]{3,2,1,0:T(8,128)(2,1)} %all-gather.2.cloned.1.call-done) | copy-start | bytes 3145732
  56.8 1.0 %copy-start.1 = (bf16[32,64,128]{2,1,0:T(8,128)(2,1)S(1)}, bf16[32,64,128]{2,1,0:T(8,128)(2,1)}, u32[]{:S(2)}) copy-start(bf16[32,64,128]{2,1,0:T(8,128)(2,1)} %param.6) | copy-start | bytes 1572868
  60.1 3.6 %copy-start.6 = (s32[512]{0:T(512)S(1)}, s32[512]{0:T(512)}, u32[]{:S(2)}) copy-start(s32[512]{0:T(512)} %param.10) | copy-start | bytes 6148
  60.1 12.4 %all-to-all-start = ((bf16[32,64,128]{2,1,0:T(8,128)(2,1)}), bf16[32,64,128]{2,1,0:T(8,128)(2,1)S(1)}, u32[]{:S(2)}, u32[]{:S(2)}) async-start(bf16[32,64,128]{2,1,0:T(8,128)(2,1)} %copy.30), calls=%async_computation | async-start | bytes 1048576 | tf_op jit(solution)/shard_map/all_to_all | solution.py:103
  64.0 0.7 copy-start.7
Sparse Core Ops, SparseCore 0:
  10.8 42.8 all-gather.1
where the time goes:
time: 82 us; the launch traced here: 81.6 us
  waiting for transfers between devices  30.7 us (37%)
  between operations  14.2 us (17%)
  other arithmetic  9.99 us (12%)
  blocking collectives  8.77 us (11%)
  local copies, waits for them, and re-layouts  7.79 us (10%)
  matrix products  6.48 us (8%)
  starting transfers between devices  3.64 us (4%)
    all_gather x1, waiting for transfers between devices, per_device(): columns_whole = lax.all_gather(spectra, 'row', axis=2, tiled=True)  22.9 us
    all_gather x1, blocking collectives, per_device(): lax.all_gather(spectra, 'col', axis=3, tiled=True)  8.77 us
    all_to_all x1, waiting for transfers between devices, per_device(): lax.all_to_all(primaries, 'col', split_axis=0, concat_axis=2, tiled=True)  7.81 us
    unnamed x4, other arithmetic  7.8 us
    unnamed x25, local copies, waits for them, and re-layouts  6.8 us
    all_to_all x1, starting transfers between devices, per_device(): lax.all_to_all(primaries, 'col', split_axis=0, concat_axis=2, tiled=True)  3.6 us
    convert_element_type x1, other arithmetic, aperture_matrix(): (widened * taper_weight * (2.0 / math.sqrt(listed))).astype(jnp.bfloat16)  1.91 us
  transfers between devices with their start and end apart: 2, of which 2 were waited for; matrix products, arithmetic and copies ran while one was open for 13% of the time, Pallas kernels for 0%

commit v1 on v0

v1 whole, which is shorter than its diff:
```python
import functools
import math

import jax
import jax.numpy as jnp
import ml_dtypes
import numpy as np
from jax import lax
from jax.experimental import pallas as pl
from jax.experimental.pallas import tpu as pltpu
from jax.sharding import PartitionSpec as P

NFFT = 4096
NF = 4
STEP = NFFT // (4 * NF)
HALF_TURN = NFFT // (2 * STEP)
F32 = jnp.float32
BF16 = jnp.bfloat16
VMEM_BYTES = 48 * 1024 * 1024


def angle(freq, sample):
    return 2.0 * math.pi * (((2 * freq + 1) * STEP * sample) % NFFT) / NFFT


def forward_weight(freq, part, sample, samples):
    value = (math.cos, lambda a: -math.sin(a))[part](angle(freq, sample)) / math.sqrt(samples)
    return float(np.float32(value).astype(ml_dtypes.bfloat16)) if abs(value) > 1e-6 else 0.0


def weighted_sum(weights, arrays):
    total = None
    for weight, array in zip(weights, arrays):
        if abs(weight) > 1e-6:
            total = weight * array if total is None else total + weight * array
    return total


def dot(left, right):
    return jnp.dot(left, right, preferred_element_type=F32)


def member_index():
    return lax.rem(lax.axis_index("row"), NF)


def spectra_kernel(traces, held, own, send_1, send_2, send_3, planes, arrived):
    samples, shots, _ = held.shape
    rows = shots // 4
    copies = []
    for part in range(4):
        piece = (slice(None), pl.ds(part * rows, rows))
        copies.append(pltpu.make_async_copy(traces.at[piece], held.at[piece], arrived.at[part]))
        copies[-1].start()
    for part in range(4):
        copies[part].wait()
        here = slice(part * rows, (part + 1) * rows)
        folded = []
        for sample in range(HALF_TURN):
            total = held[sample, here].astype(F32)
            for turn in range(1, samples // HALF_TURN):
                term = held[sample + turn * HALF_TURN, here].astype(F32)
                total = total - term if turn % 2 else total + term
            folded.append(total)
        for freq in range(NF):
            for piece in range(2):
                weights = [forward_weight(freq, piece, t, samples) for t in range(HALF_TURN)]
                planes[freq, piece, here] = weighted_sum(weights, folded).astype(BF16)
    me = member_index()
    for offset, out in enumerate((own, send_1, send_2, send_3)):
        out[...] = planes[me ^ offset]


def rows_kernel(own, got_1, got_2, got_3, block):
    me = member_index()
    for offset, got in enumerate((own, got_1, got_2, got_3)):
        for piece in range(2):
            block[piece, me ^ offset] = got[piece]


def product_kernel(left_offsets, groups, *refs):
    n_left = len(left_offsets)
    lefts, rights = refs[:n_left], refs[n_left : n_left + groups]
    outs = refs[n_left + groups : n_left + groups + NF]
    left, right, product = refs[n_left + groups + NF :]
    me, group = member_index(), lax.axis_index("row") // NF
    col = lax.axis_index("col")
    for offset, got in zip(left_offsets, lefts):
        left[col ^ offset] = got[...]
    for offset, got in enumerate(rights):
        right[group ^ offset] = got[...]
    rows = left.shape[2] * left.shape[3]
    lanes = left.shape[4]
    ratio = n_left // groups
    total = None
    for index in range(groups):
        real, imag = (right[index, piece].reshape(rows, lanes) for piece in range(2))
        left_real, left_imag = (
            jnp.concatenate(
                [left[index * ratio + k, piece].reshape(rows, lanes) for k in range(ratio)], axis=1
            )
            for piece in range(2)
        )
        term = dot(left_real, jnp.concatenate([real, imag], axis=1))
        term = term + dot(left_imag, jnp.concatenate([-imag, real], axis=1))
        total = term if total is None else total + term
    scale = -1.0 / math.sqrt(rows * groups)
    product[...] = (total * scale).reshape(product.shape).astype(BF16)
    for offset, out in enumerate(outs):
        out[...] = product[me ^ offset]


def tables_kernel(
    spread_len, held, block, receiver_pos, aperture_list, source_pos, band_index, weight_tiles,
    aperture, shot_weight, stacked, tiles_turned, chosen,
):
    del block
    samples, shots, receivers = held.shape
    panel = aperture.shape[1]
    tiles, listed = aperture_list.shape
    width = panel // tiles
    col = lax.axis_index("col")
    first = lax.axis_index("row") * panel

    def upright(row, length):
        at_row = lax.broadcasted_iota(jnp.int32, (length, length), 0)
        at_lane = lax.broadcasted_iota(jnp.int32, (length, length), 1)
        return jnp.sum(jnp.where(at_row == at_lane, row.astype(F32), 0.0), axis=1, keepdims=True)

    def taper(positions, length):
        columns = (lax.broadcasted_iota(jnp.int32, (length, panel), 1) + first).astype(F32)
        offset = (positions - columns) / spread_len
        return 1.0 / (1.0 + offset * offset)

    position = upright(receiver_pos[pl.ds(col, 1)], receivers)
    near = taper(position, receivers)
    receiver = lax.broadcasted_iota(jnp.int32, (receivers, listed), 0) + col * receivers
    ones = jnp.ones((listed, width), BF16)
    for tile in range(tiles):
        hits = jnp.where(aperture_list[tile : tile + 1] == receiver, 1.0, 0.0).astype(BF16)
        counts = dot(hits, ones)
        here = slice(tile * width, (tile + 1) * width)
        aperture[:, here] = (counts * near[:, here] * (2.0 / math.sqrt(listed))).astype(BF16)
    shot_weight[...] = taper(upright(source_pos[...], shots), shots)
    bands, steps, _ = stacked.shape
    for band in range(bands):
        lines = []
        for step in range(steps):
            line = dot(held[band * steps + step], aperture[...])
            lines.append(jnp.sum(line * shot_weight[...], axis=0, keepdims=True))
        stacked[band] = jnp.concatenate(lines, axis=0)
    tiles_turned[...] = weight_tiles[...].astype(F32).T.astype(BF16)
    kinds = chosen.shape[0]
    kind = lax.broadcasted_iota(jnp.int32, (kinds, panel), 0)
    chosen[...] = jnp.where(band_index[...] == kind, 1.0, 0.0)


def stack_kernel(own, got_1, got_2, got_3, aperture, shot_weight, stacked, keep, send, multiples, columns):
    me, col = member_index(), lax.axis_index("col")
    for offset, got in enumerate((own, got_1, got_2, got_3)):
        multiples[me ^ offset] = got[...]
    shots, receivers = multiples.shape[1], multiples.shape[2] // 2
    lines = []
    for freq in range(NF):
        for piece in range(2):
            part = multiples[freq, :, piece * receivers : (piece + 1) * receivers]
            line = dot(part, aperture[...]) * shot_weight[...]
            lines.append(jnp.sum(line, axis=0, keepdims=True))
    waves = []
    for sample in range(HALF_TURN):
        weights = []
        for freq in range(NF):
            weights += [math.cos(angle(freq, sample)), -math.sin(angle(freq, sample))]
        waves.append(weighted_sum([w / math.sqrt(NF) for w in weights], lines))
    bands, steps, _ = stacked.shape
    for band in range(bands):
        start = band * steps
        wave = jnp.concatenate([waves[(start + k) % HALF_TURN] for k in range(steps)], axis=0)
        sign = -1.0 if (start // HALF_TURN) % 2 else 1.0
        columns[band] = stacked[band] - sign * wave
    half = keep.shape[0]
    for offset in range(half):
        keep[offset] = columns[col ^ offset]
        send[offset] = columns[col ^ (offset + half)]


def halve_kernel(kept, got, keep, send):
    half = keep.shape[0]
    for offset in range(half):
        keep[offset] = kept[offset] + got[offset]
        send[offset] = kept[offset + half] + got[offset + half]


def primaries_kernel(own, got_1, got_2, got_3, held, out, multiples):
    me = member_index()
    for offset, got in enumerate((own, got_1, got_2, got_3)):
        multiples[me ^ offset] = got[...]
    samples, shots, receivers = held.shape
    rows = 16
    for start in range(0, shots, rows):
        here = slice(start, start + rows)
        parts = []
        for freq in range(NF):
            for piece in range(2):
                lanes = slice(piece * receivers, (piece + 1) * receivers)
                parts.append(multiples[freq, here, lanes].astype(F32))
        for sample in range(HALF_TURN):
            weights = []
            for freq in range(NF):
                weights += [math.cos(angle(freq, sample)), -math.sin(angle(freq, sample))]
            wave = weighted_sum([w / math.sqrt(NF) for w in weights], parts)
            for turn in range(samples // HALF_TURN):
                at = sample + turn * HALF_TURN
                trace = held[at, here].astype(F32)
                out[at, here] = (trace + wave if turn % 2 else trace - wave).astype(BF16)


def image_kernel(shots, kept, got, tiles_turned, chosen, primaries, image):
    del primaries
    column_stack = (kept[0] + got[0]) / math.sqrt(shots)
    steps, panel = column_stack.shape
    kinds = chosen.shape[0]
    rounded = column_stack.astype(BF16).astype(F32)
    widened = jnp.where(chosen[...][:, None, :] > 0.5, rounded[None], 0.0)
    image[...] = dot(tiles_turned[...], widened.reshape(kinds * steps, panel).astype(BF16))


WHOLE = pl.BlockSpec(memory_space=pltpu.VMEM)
ANYWHERE = pl.BlockSpec(memory_space=pl.ANY)


def in_vmem(*arrays):
    return [pltpu.with_memory_space_constraint(a, pltpu.VMEM) for a in arrays]


def call(body, out_shape, in_specs, out_specs, scratch=(), flops=0, moved=0):
    return pl.pallas_call(
        body,
        out_shape=out_shape,
        in_specs=in_specs,
        out_specs=out_specs,
        scratch_shapes=list(scratch),
        compiler_params=pltpu.CompilerParams(vmem_limit_bytes=VMEM_BYTES),
        cost_estimate=pl.CostEstimate(flops=flops, bytes_accessed=moved, transcendentals=0),
    )


def swap(array, axis, size, offset):
    return lax.ppermute(array, axis, [(i, i ^ offset) for i in range(size)])


def per_device(traces, source_pos, receiver_pos, aperture_list, band_index, weight_tiles):
    samples, shots, receivers = traces.shape
    rows, cols = lax.axis_size("row"), lax.axis_size("col")
    panel = band_index.shape[0]
    steps = samples // cols
    kinds, _, depth = weight_tiles.shape
    spread_len = panel * rows // 4
    groups = rows // NF

    plane_pair = pltpu.VMEM((2, shots, receivers), BF16)
    held, own, *sends = call(
        spectra_kernel,
        [pltpu.VMEM(traces.shape, BF16)] + [plane_pair] * NF,
        [ANYWHERE],
        [WHOLE] * (1 + NF),
        [pltpu.VMEM((NF, 2, shots, receivers), BF16), pltpu.SemaphoreType.DMA((4,))],
    )(traces)
    gots = [swap(s, "row", rows, d + 1) for d, s in enumerate(sends)]
    block_shape = (2, NF, shots, receivers)
    block = call(
        rows_kernel, pltpu.VMEM(block_shape, BF16), [WHOLE] * NF, WHOLE
    )(*in_vmem(own, *gots))

    rights = [block] + [swap(block, "row", rows, d * NF) for d in range(1, groups)]
    aperture, shot_weight, stacked, tiles_turned, chosen = call(
        functools.partial(tables_kernel, float(spread_len)),
        [
            pltpu.VMEM((receivers, panel), BF16),
            pltpu.VMEM((shots, panel), F32),
            pltpu.VMEM((cols, steps, panel), F32),
            pltpu.VMEM((depth, kinds * steps), BF16),
            pltpu.VMEM((kinds, panel), F32),
        ],
        [WHOLE, ANYWHERE] + [WHOLE] * 5,
        [WHOLE] * 5,
        flops=2 * samples * shots * receivers * panel,
        moved=8 << 20,
    )(
        *in_vmem(held),
        block,
        receiver_pos.reshape(cols, receivers),
        aperture_list,
        source_pos.reshape(1, shots),
        band_index.reshape(1, panel),
        weight_tiles.reshape(kinds * steps, depth),
    )

    lefts, offsets, bit = [block], [0], cols // 2
    while bit:
        lefts += [swap(a, "col", cols, bit) for a in lefts]
        offsets += [o ^ bit for o in offsets]
        bit //= 2
    part = pltpu.VMEM((shots, 2 * receivers), BF16)
    own, *sends = call(
        functools.partial(product_kernel, tuple(offsets), groups),
        [part] * NF,
        [WHOLE] * (cols + groups),
        [WHOLE] * NF,
        [
            pltpu.VMEM((cols,) + block_shape, BF16),
            pltpu.VMEM((groups,) + block_shape, BF16),
            pltpu.VMEM((NF, shots, 2 * receivers), BF16),
        ],
    )(*in_vmem(*lefts, *rights))
    parts = in_vmem(own, *[swap(s, "row", rows, d + 1) for d, s in enumerate(sends)])

    half = cols // 2
    piece = pltpu.VMEM((half, steps, panel), F32)
    gathered = pltpu.VMEM((NF, shots, 2 * receivers), BF16)
    keep, send = call(
        stack_kernel,
        [piece, piece],
        [WHOLE] * (NF + 3),
        [WHOLE] * 2,
        [gathered, pltpu.VMEM((cols, steps, panel), F32)],
    )(*parts, *in_vmem(aperture, shot_weight, stacked))
    got = swap(send, "col", cols, half)
    primaries = call(
        primaries_kernel,
        jax.ShapeDtypeStruct(traces.shape, BF16),
        [WHOLE] * (NF + 1),
        WHOLE,
        [gathered],
        flops=1 << 20,
        moved=3 << 20,
    )(*parts, *in_vmem(held))
    while half > 1:
        half //= 2
        piece = pltpu.VMEM((half, steps, panel), F32)
        keep, send = call(halve_kernel, [piece, piece], [WHOLE] * 2, [WHOLE] * 2)(
            *in_vmem(keep, got)
        )
        got = swap(send, "col", cols, half)
    image = call(
        functools.partial(image_kernel, shots),
        jax.ShapeDtypeStruct((depth, panel), F32),
        [WHOLE] * 4 + [ANYWHERE],
        WHOLE,
    )(*in_vmem(keep, got, tiles_turned, chosen), primaries)
    return primaries, image


def solution(mesh):
    placed = (P(None, "row", "col"), P("row"), P(), P("row", None), P("row"), P())
    return jax.shard_map(
        per_device,
        mesh=mesh,
        in_specs=placed,
        out_specs=(P(None, "row", "col"), P("col", "row")),
        check_vma=False,
    )
```

time: 82 us -> 36.4 us (0.44)
  waiting for transfers between devices: 30.7 us -> 15.9 us
  between operations: 14.2 us -> 0.73 us
  other arithmetic: 9.99 us -> 0 us
  starting transfers between devices: 3.64 us -> 12.9 us
  blocking collectives: 8.77 us -> 0 us
  matrix products: 6.48 us -> 0 us
  local copies, waits for them, and re-layouts: 7.79 us -> 2.77 us
  Pallas kernels: 0 us -> 3.87 us
    all_gather x1 -> x0, waiting for transfers between devices: 22.9 us -> none  [per_device(): columns_whole = lax.all_gather(spectra, 'row', axis=2, tiled=True)]
    ppermute x0 -> x12, waiting for transfers between devices: none -> 15.9 us  [swap(): return lax.ppermute(array, axis, [(i, i ^ offset) for i in range(size)])]
    ppermute x0 -> x12, starting transfers between devices: none -> 12.9 us  [swap(): return lax.ppermute(array, axis, [(i, i ^ offset) for i in range(size)])]
    all_gather x1 -> x0, blocking collectives: 8.77 us -> none  [per_device(): lax.all_gather(spectra, 'col', axis=3, tiled=True)]
    all_to_all x1 -> x0, waiting for transfers between devices: 7.81 us -> none  [per_device(): lax.all_to_all(primaries, 'col', split_axis=0, concat_axis=2, tiled=True)]
    unnamed x4 -> x0, other arithmetic: 7.8 us -> none
    dot_general x8 -> x0, matrix products: 6.48 us -> none  [the longest x1 1.43 us: per_device(): jnp.dot(forward, traces.reshape(samples, shot_count * recv_count), prefer...]
    unnamed x25 -> x14, local copies, waits for them, and re-layouts: 6.8 us -> 2.77 us
  transfers between devices with their start and end apart: 2 -> 12, of which waited for: 2 -> 8; matrix products, arithmetic and copies ran while one was open for 13% -> 0% of each run, Pallas kernels for 0% -> 5%
where the time goes in v1:
time: 36.4 us; the launch traced here: 36.1 us
  waiting for transfers between devices  15.9 us (44%)
  starting transfers between devices  12.9 us (35%)
  Pallas kernels  3.87 us (11%)
  local copies, waits for them, and re-layouts  2.77 us (8%)
  between operations  0.73 us (2%)
    ppermute x12, waiting for transfers between devices, swap(): return lax.ppermute(array, axis, [(i, i ^ offset) for i in range(size)])  15.9 us
    ppermute x12, starting transfers between devices, swap(): return lax.ppermute(array, axis, [(i, i ^ offset) for i in range(size)])  12.9 us
    unnamed x14, local copies, waits for them, and re-layouts  2.77 us
    pallas_call x1, Pallas kernels, per_device(): call(primaries_kernel, jax.ShapeDtypeStruct(traces.shape, BF16), [WHOLE]...  1.03 us
    pallas_call x1, Pallas kernels, per_device(): call(functools.partial(tables_kernel, float(spread_len)), [pltpu.VMEM((re...  0.92 us
    pallas_call x1, Pallas kernels, per_device(): call(functools.partial(image_kernel, shots), jax.ShapeDtypeStruct((depth,...  0.91 us
  transfers between devices with their start and end apart: 12, of which 8 were waited for; matrix products, arithmetic and copies ran while one was open for 0% of the time, Pallas kernels for 5%

profile of v1, /device:TPU:0, one launch (start us, length us, event | category | flops | bytes accessed | tf_op | source)
XLA Modules:
  0.0 36.1 jit_solution(12245784097074121334)
XLA Ops:
  0.6 0.0 copy-start.1
  0.6 1.0 %copy-done.1 = bf16[32,64,128]{2,1,0:T(8,128)(2,1)S(1)} copy-done((bf16[32,64,128]{2,1,0:T(8,128)(2,1)S(1)}, bf16[32,64,128]{2,1,0:T(8,128)(2,1)}, u32[]{:S(2)}) %copy-start.1) | copy-done | bytes 524312
  1.7 0.3 shard_map.77
  2.0 3.0 %collective-permute-start = (bf16[2,64,128]{2,1,0:T(8,128)(2,1)S(1)}, bf16[2,64,128]{2,1,0:T(8,128)(2,1)S(1)}, u32[]{:S(2)}, u32[]{:S(2)}) collective-permute-start(bf16[2,64,128]{2,1,0:T(8,128)(2,1)S(1)} %get-tuple-element.21), channel_id=1, source_target_pairs={{0,4},{4,0},{8,12},{12,8},{16,20},{20,16},{24,28},{28,24},{1,5},{5... | collective-permute-start | bytes 98312 | tf_op jit(solution)/shard_map/ppermute | solution.py:249
  5.0 1.6 %collective-permute-start.1 = (bf16[2,64,128]{2,1,0:T(8,128)(2,1)S(1)}, bf16[2,64,128]{2,1,0:T(8,128)(2,1)S(1)}, u32[]{:S(2)}, u32[]{:S(2)}) collective-permute-start(bf16[2,64,128]{2,1,0:T(8,128)(2,1)S(1)} %get-tuple-element.22), channel_id=1, source_target_pairs={{0,8},{4,12},{8,0},{12,4},{16,24},{20,28},{24,16},{28,20},{1,9},{5... | collective-permute-start | bytes 98312 | tf_op jit(solution)/shard_map/ppermute | solution.py:249
  6.5 0.0 collective-permute-start.2
  6.6 0.3 collective-permute-done.got_1
  6.9 2.2 %collective-permute-done.1.got_2 = bf16[2,64,128]{2,1,0:T(8,128)(2,1)S(1)} collective-permute-done((bf16[2,64,128]{2,1,0:T(8,128)(2,1)S(1)}, bf16[2,64,128]{2,1,0:T(8,128)(2,1)S(1)}, u32[]{:S(2)}, u32[]{:S(2)}) %collective-permute-start.1) | collective-permute-done | bytes 32800 | tf_op jit(solution)/shard_map/ppermute | solution.py:249
  9.1 2.3 %collective-permute-done.2.got_3 = bf16[2,64,128]{2,1,0:T(8,128)(2,1)S(1)} collective-permute-done((bf16[2,64,128]{2,1,0:T(8,128)(2,1)S(1)}, bf16[2,64,128]{2,1,0:T(8,128)(2,1)S(1)}, u32[]{:S(2)}, u32[]{:S(2)}) %collective-permute-start.2) | collective-permute-done | bytes 32800 | tf_op jit(solution)/shard_map/ppermute | solution.py:249
  11.4 0.0 copy-start.2
  11.4 1.6 %collective-permute-start.3 = (bf16[2,4,64,128]{3,2,1,0:T(8,128)(2,1)S(1)}, bf16[2,4,64,128]{3,2,1,0:T(8,128)(2,1)S(1)}, u32[]{:S(2)}, u32[]{:S(2)}) collective-permute-start(bf16[2,4,64,128]{3,2,1,0:T(8,128)(2,1)S(1)} %shard_map.78.refs_0_.refs_4_.block), channel_id=1, source_target_pairs={{0,2},{1,3},{2,0},{3,1},{4,6},{5,7},{6,4},{7,5},{8,10},{9,11},{10,... | collective-permute-start | bytes 393224 | tf_op jit(solution)/shard_map/ppermute | solution.py:249
  13.0 0.0 collective-permute-start.4
  13.0 2.6 %collective-permute-start.6 = (bf16[2,4,64,128]{3,2,1,0:T(8,128)(2,1)S(1)}, bf16[2,4,64,128]{3,2,1,0:T(8,128)(2,1)S(1)}, u32[]{:S(2)}, u32[]{:S(2)}) collective-permute-start(bf16[2,4,64,128]{3,2,1,0:T(8,128)(2,1)S(1)} %shard_map.78.refs_0_.refs_4_.block), channel_id=1, source_target_pairs={{0,16},{4,20},{8,24},{12,28},{16,0},{20,4},{24,8},{28,12},{1,17},{... | collective-permute-start | bytes 393224 | tf_op jit(solution)/shard_map/ppermute | solution.py:249
  15.6 0.9 %collective-permute-done.3.refs_1_ = bf16[2,4,64,128]{3,2,1,0:T(8,128)(2,1)S(1)} collective-permute-done((bf16[2,4,64,128]{3,2,1,0:T(8,128)(2,1)S(1)}, bf16[2,4,64,128]{3,2,1,0:T(8,128)(2,1)S(1)}, u32[]{:S(2)}, u32[]{:S(2)}) %collective-permute-start.3) | collective-permute-done | bytes 131104 | tf_op jit(solution)/shard_map/ppermute | solution.py:249
  16.4 0.0 collective-permute-start.5
  16.4 0.0 collective-permute-done.4.refs_2_
  16.4 6.0 %collective-permute-done.6.refs_5_ = bf16[2,4,64,128]{3,2,1,0:T(8,128)(2,1)S(1)} collective-permute-done((bf16[2,4,64,128]{3,2,1,0:T(8,128)(2,1)S(1)}, bf16[2,4,64,128]{3,2,1,0:T(8,128)(2,1)S(1)}, u32[]{:S(2)}, u32[]{:S(2)}) %collective-permute-start.6) | collective-permute-done | bytes 131104 | tf_op jit(solution)/shard_map/ppermute | solution.py:249
  22.5 0.0 collective-permute-done.5.refs_3_
  22.5 0.0 copy-start.5
  22.5 0.4 %shard_map.79 = (bf16[64,256]{1,0:T(8,128)(2,1)S(1)}, bf16[64,256]{1,0:T(8,128)(2,1)S(1)}, bf16[64,256]{1,0:T(8,128)(2,1)S(1)}, bf16[64,256]{1,0:T(8,128)(2,1)S(1)}) custom-call(bf16[2,4,64,128]{3,2,1,0:T(8,128)(2,1)S(1)} %shard_map.78.refs_0_.refs_4_.block, bf16[2,4,64,128]{3,2,1,0:T(8,128)(2,1)S(1)} %collective-permute-done.3.refs_1_, ...), custom_call_target="tpu_custom_call" | custom-call | tf_op jit(solution)/shard_map/pallas_call | solution.py:305
  22.9 0.6 %collective-permute-start.7 = (bf16[64,256]{1,0:T(8,128)(2,1)S(1)}, bf16[64,256]{1,0:T(8,128)(2,1)S(1)}, u32[]{:S(2)}, u32[]{:S(2)}) collective-permute-start(bf16[64,256]{1,0:T(8,128)(2,1)S(1)} %get-tuple-element.25), channel_id=1, source_target_pairs={{0,4},{4,0},{8,12},{12,8},{16,20},{20,16},{24,28},{28,24},{1,5},{5... | collective-permute-start | bytes 98312 | tf_op jit(solution)/shard_map/ppermute | solution.py:249
  23.5 0.0 collective-permute-start.8
  23.5 3.0 %collective-permute-start.9 = (bf16[64,256]{1,0:T(8,128)(2,1)S(1)}, bf16[64,256]{1,0:T(8,128)(2,1)S(1)}, u32[]{:S(2)}, u32[]{:S(2)}) collective-permute-start(bf16[64,256]{1,0:T(8,128)(2,1)S(1)} %get-tuple-element.27), channel_id=1, source_target_pairs={{0,12},{4,8},{8,4},{12,0},{16,28},{20,24},{24,20},{28,16},{1,13},{... | collective-permute-start | bytes 98312 | tf_op jit(solution)/shard_map/ppermute | solution.py:249
  26.4 0.0 copy-start.3
  26.4 0.0 copy-start.4
  26.4 0.0 copy-start.6
  26.4 0.0 copy-done.2
  26.4 0.0 copy-done.5
  26.4 0.7 %copy-done.3 = s32[4,256]{1,0:T(4,128)S(1)} copy-done((s32[4,256]{1,0:T(4,128)S(1)}, s32[4,256]{1,0:T(4,128)}, u32[]{:S(2)}) %copy-start.3) | copy-done | bytes 4120
  27.1 0.0 copy-done.4
  27.1 0.0 copy-done.6
  27.1 0.9 %shard_map.81 = (bf16[128,512]{1,0:T(8,128)(2,1)S(1)}, f32[64,512]{1,0:T(8,128)S(1)}, f32[4,8,512]{2,1,0:T(8,128)S(1)}, bf16[128,256]{1,0:T(8,128)(2,1)S(1)}, f32[32,512]{1,0:T(8,128)S(1)}) custom-call(bf16[32,64,128]{2,1,0:T(8,128)(2,1)S(1)} %get-tuple-element.28.held, bf16[2,4,64,128]{3,2,1,0:T(8,128)(2,1)S(1)} %shard_map.78.refs_0_.refs_4_.block, ...), custom_call_target="tpu_custom_call" | custom-call | flops 268435456 | bytes 8388608 | tf_op jit(solution)/shard_map/pallas_call | solution.py:276
  28.1 0.0 collective-permute-done.7.got_1
  28.1 0.0 collective-permute-done.8.got_2
  28.1 0.6 %collective-permute-done.9.got_3 = bf16[64,256]{1,0:T(8,128)(2,1)S(1)} collective-permute-done((bf16[64,256]{1,0:T(8,128)(2,1)S(1)}, bf16[64,256]{1,0:T(8,128)(2,1)S(1)}, u32[]{:S(2)}, u32[]{:S(2)}) %collective-permute-start.9) | collective-permute-done | bytes 32800 | tf_op jit(solution)/shard_map/ppermute | solution.py:249
  28.7 0.3 shard_map.82
  29.0 0.6 %collective-permute-start.10 = (f32[2,8,512]{2,1,0:T(8,128)S(1)}, f32[2,8,512]{2,1,0:T(8,128)S(1)}, u32[]{:S(2)}, u32[]{:S(2)}) collective-permute-start(f32[2,8,512]{2,1,0:T(8,128)S(1)} %get-tuple-element.33), channel_id=1, source_target_pairs={{0,2},{1,3},{2,0},{3,1},{4,6},{5,7},{6,4},{7,5},{8,10},{9,11},{10,... | collective-permute-start | bytes 98312 | tf_op jit(solution)/shard_map/ppermute | solution.py:249
  29.6 3.4 %collective-permute-done.10.got = f32[2,8,512]{2,1,0:T(8,128)S(1)} collective-permute-done((f32[2,8,512]{2,1,0:T(8,128)S(1)}, f32[2,8,512]{2,1,0:T(8,128)S(1)}, u32[]{:S(2)}, u32[]{:S(2)}) %collective-permute-start.10) | collective-permute-done | bytes 32800 | tf_op jit(solution)/shard_map/ppermute | solution.py:249
  33.0 0.0 collective-permute-start.11
  33.0 1.0 %shard_map.80.primaries = bf16[32,64,128]{2,1,0:T(8,128)(2,1)} custom-call(bf16[64,256]{1,0:T(8,128)(2,1)S(1)} %get-tuple-element.24.own, bf16[64,256]{1,0:T(8,128)(2,1)S(1)} %collective-permute-done.7.got_1, bf16[64,256]{1,0:T(8,128)(2,1)S(1)} %collective-permute-done.8.got_2, bf16[64,256]{1,0:T(8,128)(2,1)S(1)} %collective-permute-done.9.got_3, ...), custom_call_target="tpu_custom_call" | custom-call | flops 1048576 | bytes 3145728 | tf_op jit(solution)/shard_map/pallas_call | solution.py:329
  34.0 0.1 collective-permute-done.11.got
  34.2 0.0 copy-start
  34.2 1.0 %copy-done = bf16[32,64,128]{2,1,0:T(8,128)(2,1)S(1)} copy-done((bf16[32,64,128]{2,1,0:T(8,128)(2,1)S(1)}, bf16[32,64,128]{2,1,0:T(8,128)(2,1)}, u32[]{:S(2)}) %copy-start) | copy-done | bytes 524312
  35.2 0.9 %shard_map.84 = f32[128,512]{1,0:T(8,128)} custom-call(f32[1,8,512]{2,1,0:T(8,128)S(1)} %get-tuple-element.34.kept, f32[1,8,512]{2,1,0:T(8,128)S(1)} %collective-permute-done.11.got, bf16[128,256]{1,0:T(8,128)(2,1)S(1)} %get-tuple-element.36.tiles_turned, f32[32,512]{1,0:T(8,128)S(1)} %get-tuple-element.37.chosen, bf16[32,64,128]{2,1,0:T(8,128)(2,1)S(1)} %copy-done), custom_call_target="tpu_custom_call" | custom-call | tf_op jit(solution)/shard_map/pallas_call | solution.py:345
  (2 shorter events, 0.0 us)
Async XLA Ops:
  0.6 1.0 %copy-start.1 = (bf16[32,64,128]{2,1,0:T(8,128)(2,1)S(1)}, bf16[32,64,128]{2,1,0:T(8,128)(2,1)}, u32[]{:S(2)}) copy-start(bf16[32,64,128]{2,1,0:T(8,128)(2,1)} %traces.1) | copy-start | bytes 1572868
  2.0 4.9 %collective-permute-start = (bf16[2,64,128]{2,1,0:T(8,128)(2,1)S(1)}, bf16[2,64,128]{2,1,0:T(8,128)(2,1)S(1)}, u32[]{:S(2)}, u32[]{:S(2)}) collective-permute-start(bf16[2,64,128]{2,1,0:T(8,128)(2,1)S(1)} %get-tuple-element.21), channel_id=1, source_target_pairs={{0,4},{4,0},{8,12},{12,8},{16,20},{20,16},{24,28},{28,24},{1,5},{5... | collective-permute-start | bytes 98312 | tf_op jit(solution)/shard_map/ppermute | solution.py:249
  5.0 4.1 %collective-permute-start.1 = (bf16[2,64,128]{2,1,0:T(8,128)(2,1)S(1)}, bf16[2,64,128]{2,1,0:T(8,128)(2,1)S(1)}, u32[]{:S(2)}, u32[]{:S(2)}) collective-permute-start(bf16[2,64,128]{2,1,0:T(8,128)(2,1)S(1)} %get-tuple-element.22), channel_id=1, source_target_pairs={{0,8},{4,12},{8,0},{12,4},{16,24},{20,28},{24,16},{28,20},{1,9},{5... | collective-permute-start | bytes 98312 | tf_op jit(solution)/shard_map/ppermute | solution.py:249
  6.5 4.8 %collective-permute-start.2 = (bf16[2,64,128]{2,1,0:T(8,128)(2,1)S(1)}, bf16[2,64,128]{2,1,0:T(8,128)(2,1)S(1)}, u32[]{:S(2)}, u32[]{:S(2)}) collective-permute-start(bf16[2,64,128]{2,1,0:T(8,128)(2,1)S(1)} %get-tuple-element.23), channel_id=1, source_target_pairs={{0,12},{4,8},{8,4},{12,0},{16,28},{20,24},{24,20},{28,16},{1,13},{... | collective-permute-start | bytes 98312 | tf_op jit(solution)/shard_map/ppermute | solution.py:249
  11.4 15.1 %copy-start.2 = (bf16[32,8,128]{2,1,0:T(8,128)(2,1)S(1)}, bf16[32,8,128]{2,1,0:T(8,128)(2,1)}, u32[]{:S(2)}) copy-start(bf16[32,8,128]{2,1,0:T(8,128)(2,1)} %param.11) | copy-start | bytes 196612
  11.4 5.0 %collective-permute-start.3 = (bf16[2,4,64,128]{3,2,1,0:T(8,128)(2,1)S(1)}, bf16[2,4,64,128]{3,2,1,0:T(8,128)(2,1)S(1)}, u32[]{:S(2)}, u32[]{:S(2)}) collective-permute-start(bf16[2,4,64,128]{3,2,1,0:T(8,128)(2,1)S(1)} %shard_map.78.refs_0_.refs_4_.block), channel_id=1, source_target_pairs={{0,2},{1,3},{2,0},{3,1},{4,6},{5,7},{6,4},{7,5},{8,10},{9,11},{10,... | collective-permute-start | bytes 393224 | tf_op jit(solution)/shard_map/ppermute | solution.py:249
  13.0 3.5 %collective-permute-start.4 = (bf16[2,4,64,128]{3,2,1,0:T(8,128)(2,1)S(1)}, bf16[2,4,64,128]{3,2,1,0:T(8,128)(2,1)S(1)}, u32[]{:S(2)}, u32[]{:S(2)}) collective-permute-start(bf16[2,4,64,128]{3,2,1,0:T(8,128)(2,1)S(1)} %shard_map.78.refs_0_.refs_4_.block), channel_id=1, source_target_pairs={{0,1},{1,0},{2,3},{3,2},{4,5},{5,4},{6,7},{7,6},{8,9},{9,8},{10,11... | collective-permute-start | bytes 393224 | tf_op jit(solution)/shard_map/ppermute | solution.py:249
  13.0 9.5 %collective-permute-start.6 = (bf16[2,4,64,128]{3,2,1,0:T(8,128)(2,1)S(1)}, bf16[2,4,64,128]{3,2,1,0:T(8,128)(2,1)S(1)}, u32[]{:S(2)}, u32[]{:S(2)}) collective-permute-start(bf16[2,4,64,128]{3,2,1,0:T(8,128)(2,1)S(1)} %shard_map.78.refs_0_.refs_4_.block), channel_id=1, source_target_pairs={{0,16},{4,20},{8,24},{12,28},{16,0},{20,4},{24,8},{28,12},{1,17},{... | collective-permute-start | bytes 393224 | tf_op jit(solution)/shard_map/ppermute | solution.py:249
  16.4 6.1 %collective-permute-start.5 = (bf16[2,4,64,128]{3,2,1,0:T(8,128)(2,1)S(1)}, bf16[2,4,64,128]{3,2,1,0:T(8,128)(2,1)S(1)}, u32[]{:S(2)}, u32[]{:S(2)}) collective-permute-start(bf16[2,4,64,128]{3,2,1,0:T(8,128)(2,1)S(1)} %collective-permute-done.3.refs_1_), channel_id=1, source_target_pairs={{0,1},{1,0},{2,3},{3,2},{4,5},{5,4},{6,7},{7,6},{8,9},{9,8},{10,11... | collective-permute-start | bytes 393224 | tf_op jit(solution)/shard_map/ppermute | solution.py:249
  22.5 4.0 %copy-start.5 = (s32[512]{0:T(512)S(1)}, s32[512]{0:T(512)}, u32[]{:S(2)}) copy-start(s32[512]{0:T(512)} %param.10) | copy-start | bytes 6148
  22.9 5.2 %collective-permute-start.7 = (bf16[64,256]{1,0:T(8,128)(2,1)S(1)}, bf16[64,256]{1,0:T(8,128)(2,1)S(1)}, u32[]{:S(2)}, u32[]{:S(2)}) collective-permute-start(bf16[64,256]{1,0:T(8,128)(2,1)S(1)} %get-tuple-element.25), channel_id=1, source_target_pairs={{0,4},{4,0},{8,12},{12,8},{16,20},{20,16},{24,28},{28,24},{1,5},{5... | collective-permute-start | bytes 98312 | tf_op jit(solution)/shard_map/ppermute | solution.py:249
  23.5 4.6 %collective-permute-start.8 = (bf16[64,256]{1,0:T(8,128)(2,1)S(1)}, bf16[64,256]{1,0:T(8,128)(2,1)S(1)}, u32[]{:S(2)}, u32[]{:S(2)}) collective-permute-start(bf16[64,256]{1,0:T(8,128)(2,1)S(1)} %get-tuple-element.26), channel_id=1, source_target_pairs={{0,8},{4,12},{8,0},{12,4},{16,24},{20,28},{24,16},{28,20},{1,9},{5... | collective-permute-start | bytes 98312 | tf_op jit(solution)/shard_map/ppermute | solution.py:249
  23.5 5.2 %collective-permute-start.9 = (bf16[64,256]{1,0:T(8,128)(2,1)S(1)}, bf16[64,256]{1,0:T(8,128)(2,1)S(1)}, u32[]{:S(2)}, u32[]{:S(2)}) collective-permute-start(bf16[64,256]{1,0:T(8,128)(2,1)S(1)} %get-tuple-element.27), channel_id=1, source_target_pairs={{0,12},{4,8},{8,4},{12,0},{16,28},{20,24},{24,20},{28,16},{1,13},{... | collective-permute-start | bytes 98312 | tf_op jit(solution)/shard_map/ppermute | solution.py:249
  26.4 0.7 %copy-start.3 = (s32[4,256]{1,0:T(4,128)S(1)}, s32[4,256]{1,0:T(4,128)}, u32[]{:S(2)}) copy-start(s32[4,256]{1,0:T(4,128)} %aperture_list.1) | copy-start | bytes 12292
  26.4 0.7 %copy-start.4 = (s32[512]{0:T(512)S(1)}, s32[512]{0:T(512)}, u32[]{:S(2)}) copy-start(s32[512]{0:T(512)} %param.8) | copy-start | bytes 6148
  26.4 0.7 %copy-start.6 = (s32[64]{0:T(128)S(1)}, s32[64]{0:T(128)}, u32[]{:S(2)}) copy-start(s32[64]{0:T(128)} %param.7) | copy-start | bytes 772
  29.0 4.0 %collective-permute-start.10 = (f32[2,8,512]{2,1,0:T(8,128)S(1)}, f32[2,8,512]{2,1,0:T(8,128)S(1)}, u32[]{:S(2)}, u32[]{:S(2)}) collective-permute-start(f32[2,8,512]{2,1,0:T(8,128)S(1)} %get-tuple-element.33), channel_id=1, source_target_pairs={{0,2},{1,3},{2,0},{3,1},{4,6},{5,7},{6,4},{7,5},{8,10},{9,11},{10,... | collective-permute-start | bytes 98312 | tf_op jit(solution)/shard_map/ppermute | solution.py:249
  33.0 1.2 %collective-permute-start.11 = (f32[1,8,512]{2,1,0:T(8,128)S(1)}, f32[1,8,512]{2,1,0:T(8,128)S(1)}, u32[]{:S(2)}, u32[]{:S(2)}) collective-permute-start(f32[1,8,512]{2,1,0:T(8,128)S(1)} %get-tuple-element.35), channel_id=1, source_target_pairs={{0,1},{1,0},{2,3},{3,2},{4,5},{5,4},{6,7},{7,6},{8,9},{9,8},{10,11... | collective-permute-start | bytes 49160 | tf_op jit(solution)/shard_map/ppermute | solution.py:249
  34.2 1.0 %copy-start = (bf16[32,64,128]{2,1,0:T(8,128)(2,1)S(1)}, bf16[32,64,128]{2,1,0:T(8,128)(2,1)}, u32[]{:S(2)}) copy-start(bf16[32,64,128]{2,1,0:T(8,128)(2,1)} %shard_map.80.primaries) | copy-start | bytes 1572868

commit v2 on v1

v2 whole, which is shorter than its diff:
```python
import functools
import math

import jax
import jax.numpy as jnp
import ml_dtypes
import numpy as np
from jax import lax
from jax.experimental import pallas as pl
from jax.experimental.pallas import tpu as pltpu
from jax.sharding import PartitionSpec as P

NFFT = 4096
NF = 4
STEP = NFFT // (4 * NF)
HALF_TURN = NFFT // (2 * STEP)
F32 = jnp.float32
BF16 = jnp.bfloat16
VMEM_BYTES = 48 * 1024 * 1024


def angle(freq, sample):
    return 2.0 * math.pi * (((2 * freq + 1) * STEP * sample) % NFFT) / NFFT


def forward_weight(freq, part, sample, samples):
    value = (math.cos, lambda a: -math.sin(a))[part](angle(freq, sample)) / math.sqrt(samples)
    return float(np.float32(value).astype(ml_dtypes.bfloat16)) if abs(value) > 1e-6 else 0.0


def weighted_sum(weights, arrays):
    total = None
    for weight, array in zip(weights, arrays):
        if abs(weight) > 1e-6:
            total = weight * array if total is None else total + weight * array
    return total


def dot(left, right):
    return jnp.dot(left, right, preferred_element_type=F32)


def wave_weights(sample):
    weights = []
    for freq in range(NF):
        weights += [math.cos(angle(freq, sample)), -math.sin(angle(freq, sample))]
    return [w / math.sqrt(NF) for w in weights]


def spectra_kernel(
    traces, aperture_list, source_pos, held, planes, mine, theirs, lists, halves, listing, places, arrived
):
    samples, shots, receivers = held.shape
    rows = shots // 4
    copies = []
    for part in range(4):
        piece = (slice(None), pl.ds(part * rows, rows))
        copies.append(pltpu.make_async_copy(traces.at[piece], held.at[piece], arrived.at[part]))
        copies[-1].start()
    for index, (given, near) in enumerate(((aperture_list, listing), (source_pos, places))):
        copies.append(pltpu.make_async_copy(given, near, arrived.at[4 + index]))
        copies[-1].start()
    lane = lax.broadcasted_iota(jnp.int32, (rows, receivers), 1)
    low = lane < receivers // 2
    for part in range(4):
        copies[part].wait()
        here = slice(part * rows, (part + 1) * rows)
        folded = []
        for sample in range(HALF_TURN):
            total = held[sample, here].astype(F32)
            for turn in range(1, samples // HALF_TURN):
                term = held[sample + turn * HALF_TURN, here].astype(F32)
                total = total - term if turn % 2 else total + term
            folded.append(total)
        for freq in range(NF):
            pair = []
            for piece in range(2):
                weights = [forward_weight(freq, piece, t, samples) for t in range(HALF_TURN)]
                pair.append(weighted_sum(weights, folded))
                planes[freq, piece, here] = pair[piece].astype(BF16)
            real, imag = pair
            turned = [pltpu.roll(p, receivers // 2, 1) for p in pair]
            halves[0, freq, here] = jnp.where(low, real, turned[1]).astype(BF16)
            halves[1, freq, here] = jnp.where(low, turned[0], imag).astype(BF16)
    copies[4].wait()
    copies[5].wait()
    tiles = listing.shape[0]
    lists[0:tiles] = listing[...]
    lists[tiles : tiles + 1, 0:shots] = places[...]
    side = lax.rem(lax.axis_index("row"), 2)
    mine[...] = halves[side]
    theirs[...] = halves[1 - side]


def pair_kernel(mine, got, both):
    both[0] = mine[...]
    both[1] = got[...]


def panel_stack(parts, aperture, shot_weight):
    lines = []
    receivers = aperture.shape[0]
    for freq in range(NF):
        for piece in range(2):
            part = parts[freq, :, piece * receivers : (piece + 1) * receivers]
            line = dot(part, aperture[...]) * shot_weight[...]
            lines.append(jnp.sum(line, axis=0, keepdims=True))
    waves = [weighted_sum(wave_weights(sample), lines) for sample in range(HALF_TURN)]
    return jnp.concatenate(waves, axis=0)


def product_kernel(levels, left, *refs):
    rights = refs[:levels]
    apertures, shot_weights, mine, theirs, waves, right = refs[levels:]
    level = lax.axis_index("row") // 2
    for offset, got in enumerate(rights):
        right[level ^ offset] = got[...]
    _, _, _, shots, lanes = left.shape
    scale = -1.0 / math.sqrt(2 * levels * shots)
    step = min(2, levels)
    for freq in range(NF):
        total = None
        for first in range(0, levels, step):
            inner = range(first, first + step)
            near = jnp.concatenate(
                [left[k, :, freq].reshape(2 * shots, lanes) for k in inner], axis=1
            )
            far = []
            for k in inner:
                real, imag = right[k, freq, 0], right[k, freq, 1]
                far.append(jnp.concatenate([real, imag], axis=1))
                far.append(jnp.concatenate([-imag, real], axis=1))
            term = dot(near, jnp.concatenate(far, axis=0))
            total = term if total is None else total + term
        total = total * scale
        mine[freq] = total[:shots].astype(BF16)
        theirs[freq] = total[shots:].astype(BF16)
    waves[...] = panel_stack(theirs, apertures.at[1], shot_weights.at[1])


def tables_kernel(
    spread_len, left, got_lists, receiver_pos, aperture_list, source_pos, apertures, shot_weights
):
    del left
    _, receivers, panel = apertures.shape
    shots = shot_weights.shape[1]
    tiles, listed = aperture_list.shape
    width = panel // tiles
    row, col = lax.axis_index("row"), lax.axis_index("col")

    def upright(line, length):
        at_row = lax.broadcasted_iota(jnp.int32, (length, length), 0)
        at_lane = lax.broadcasted_iota(jnp.int32, (length, length), 1)
        return jnp.sum(jnp.where(at_row == at_lane, line.astype(F32), 0.0), axis=1, keepdims=True)

    def taper(positions, length, first):
        columns = (lax.broadcasted_iota(jnp.int32, (length, panel), 1) + first).astype(F32)
        offset = (positions - columns) / spread_len
        return 1.0 / (1.0 + offset * offset)

    position = upright(receiver_pos[pl.ds(col, 1)], receivers)
    receiver = lax.broadcasted_iota(jnp.int32, (receivers, listed), 0) + col * receivers
    ones = jnp.ones((listed, width), BF16)
    sources = (source_pos[...], got_lists[tiles : tiles + 1, 0:shots])
    for index, lists in enumerate((aperture_list, got_lists)):
        first = (row ^ index) * panel
        near = taper(position, receivers, first)
        for tile in range(tiles):
            hits = jnp.where(lists[tile : tile + 1] == receiver, 1.0, 0.0).astype(BF16)
            counts = dot(hits, ones)
            here = slice(tile * width, (tile + 1) * width)
            weighted = counts * near[:, here] * (2.0 / math.sqrt(listed))
            apertures[index, :, here] = weighted.astype(BF16)
        shot_weights[index] = taper(upright(sources[index], shots), shots, first)


def subtract_waves(band, columns, waves):
    steps = columns.shape[0]
    start = band * steps
    sign = -1.0 if (start // HALF_TURN) % 2 else 1.0
    first = start % HALF_TURN
    return columns - sign * waves[first : first + steps]


def own_stack_kernel(
    mine, held, apertures, shot_weights, band_index, weight_tiles, columns, tiles_turned, chosen
):
    waves = panel_stack(mine, apertures.at[0], shot_weights.at[0])
    bands, steps, _ = columns.shape
    for band in range(bands):
        lines = []
        for step in range(steps):
            line = dot(held[band * steps + step], apertures[0])
            lines.append(jnp.sum(line * shot_weights[0], axis=0, keepdims=True))
        columns[band] = subtract_waves(band, jnp.concatenate(lines, axis=0), waves)
    tiles_turned[...] = weight_tiles[...].astype(F32).T.astype(BF16)
    kind = lax.broadcasted_iota(jnp.int32, chosen.shape, 0)
    chosen[...] = jnp.where(band_index[...] == kind, 1.0, 0.0)


def column_kernel(columns, got, *refs):
    total = refs[-1]
    col = lax.axis_index("col")
    waves = got[...]
    for band in range(columns.shape[0]):
        total[band] = subtract_waves(band, columns[band], waves)
    for offset, out in enumerate(refs[:-1]):
        out[...] = total[col ^ offset]


def primaries_kernel(mine, got, held, out, token):
    samples, shots, receivers = held.shape
    rows = 16
    for start in range(0, shots, rows):
        here = slice(start, start + rows)
        parts = []
        for freq in range(NF):
            both = mine[freq, here].astype(F32) + got[freq, here].astype(F32)
            parts += [both[:, :receivers], both[:, receivers:]]
        for sample in range(HALF_TURN):
            wave = weighted_sum(wave_weights(sample), parts)
            for turn in range(samples // HALF_TURN):
                at = sample + turn * HALF_TURN
                trace = held[at, here].astype(F32)
                out[at, here] = (trace + wave if turn % 2 else trace - wave).astype(BF16)
    token[...] = jnp.zeros_like(token)


def image_kernel(shots, bands, *refs):
    parts = refs[:bands]
    tiles_turned, chosen, _, image = refs[bands:]
    total = parts[0][...]
    for part in parts[1:]:
        total = total + part[...]
    column_stack = total / math.sqrt(shots)
    steps, panel = column_stack.shape
    kinds = chosen.shape[0]
    rounded = column_stack.astype(BF16).astype(F32)
    widened = jnp.where(chosen[...][:, None, :] > 0.5, rounded[None], 0.0)
    image[...] = dot(tiles_turned[...], widened.reshape(kinds * steps, panel).astype(BF16))


WHOLE = pl.BlockSpec(memory_space=pltpu.VMEM)
IN_HBM = pl.BlockSpec(memory_space=pltpu.HBM)


def in_vmem(*arrays):
    return [pltpu.with_memory_space_constraint(a, pltpu.VMEM) for a in arrays]


def call(body, out_shape, in_specs, out_specs, scratch=(), flops=0, moved=0):
    return pl.pallas_call(
        body,
        out_shape=out_shape,
        in_specs=in_specs,
        out_specs=out_specs,
        scratch_shapes=list(scratch),
        compiler_params=pltpu.CompilerParams(vmem_limit_bytes=VMEM_BYTES),
        cost_estimate=pl.CostEstimate(flops=flops, bytes_accessed=moved, transcendentals=0),
    )


def swap(array, axis, size, offset):
    return lax.ppermute(array, axis, [(i, i ^ offset) for i in range(size)])


def per_device(traces, source_pos, receiver_pos, aperture_list, band_index, weight_tiles):
    samples, shots, receivers = traces.shape
    rows, cols = lax.axis_size("row"), lax.axis_size("col")
    panel = band_index.shape[0]
    steps = samples // cols
    kinds, _, depth = weight_tiles.shape
    spread_len = panel * rows // 4
    levels = rows // 2
    tiles, listed = aperture_list.shape
    assert receivers == 2 * shots and levels == cols

    plane_shape = (NF, 2, shots, receivers)
    half_shape = (NF, shots, receivers)
    part = pltpu.VMEM((NF, shots, 2 * receivers), BF16)
    positions = source_pos.reshape(1, shots)
    held, planes, mine, theirs, lists = call(
        spectra_kernel,
        [
            pltpu.VMEM(traces.shape, BF16),
            pltpu.VMEM(plane_shape, BF16),
            pltpu.VMEM(half_shape, BF16),
            pltpu.VMEM(half_shape, BF16),
            pltpu.VMEM((2 * tiles, listed), jnp.int32),
        ],
        [IN_HBM] * 3,
        [WHOLE] * 5,
        [
            pltpu.VMEM((2,) + half_shape, BF16),
            pltpu.VMEM(aperture_list.shape, jnp.int32),
            pltpu.VMEM(positions.shape, jnp.int32),
            pltpu.SemaphoreType.DMA((6,)),
        ],
    )(*[pltpu.with_memory_space_constraint(a, pltpu.HBM) for a in (traces, aperture_list, positions)])
    rights = [planes] + [swap(planes, "row", rows, 2 * d) for d in range(1, levels)]
    both = call(pair_kernel, pltpu.VMEM((2,) + half_shape, BF16), [WHOLE] * 2, WHOLE)(
        *in_vmem(mine, swap(theirs, "row", rows, 1))
    )
    left = lax.all_gather(both, "col")
    apertures, shot_weights = call(
        functools.partial(tables_kernel, float(spread_len)),
        [pltpu.VMEM((2, receivers, panel), BF16), pltpu.VMEM((2, shots, panel), F32)],
        [WHOLE] * 5,
        [WHOLE] * 2,
        moved=2 << 20,
    )(
        *in_vmem(left, swap(lists, "row", rows, 1)),
        receiver_pos.reshape(cols, receivers),
        aperture_list,
        positions,
    )
    mine, theirs, waves = call(
        functools.partial(product_kernel, levels),
        [part, part, pltpu.VMEM((HALF_TURN, panel), F32)],
        [WHOLE] * (levels + 3),
        [WHOLE] * 3,
        [pltpu.VMEM((levels,) + plane_shape, BF16)],
    )(*in_vmem(left, *rights, apertures, shot_weights))
    got_waves = swap(waves, "row", rows, 1)
    got_part = swap(theirs, "row", rows, 1)
    columns, tiles_turned, chosen = call(
        own_stack_kernel,
        [
            pltpu.VMEM((cols, steps, panel), F32),
            pltpu.VMEM((depth, kinds * steps), BF16),
            pltpu.VMEM((kinds, panel), F32),
        ],
        [WHOLE] * 6,
        [WHOLE] * 3,
        flops=2 * samples * shots * receivers * panel,
        moved=1 << 20,
    )(
        *in_vmem(mine, held, apertures, shot_weights),
        band_index.reshape(1, panel),
        weight_tiles.reshape(kinds * steps, depth),
    )
    band = pltpu.VMEM((steps, panel), F32)
    own, *sends = call(
        column_kernel,
        [band] * cols,
        [WHOLE] * 2,
        [WHOLE] * cols,
        [pltpu.VMEM((cols, steps, panel), F32)],
    )(*in_vmem(columns, got_waves))
    bands = [own] + [swap(s, "col", cols, d + 1) for d, s in enumerate(sends)]
    primaries, token = call(
        primaries_kernel,
        [jax.ShapeDtypeStruct(traces.shape, BF16), pltpu.VMEM((8, 128), F32)],
        [WHOLE] * 3,
        [WHOLE] * 2,
        flops=1 << 20,
        moved=3 << 20,
    )(*in_vmem(mine, got_part, held))
    image = call(
        functools.partial(image_kernel, shots, cols),
        jax.ShapeDtypeStruct((depth, panel), F32),
        [WHOLE] * (cols + 3),
        WHOLE,
    )(*in_vmem(*bands, tiles_turned, chosen, token))
    return primaries, image


def solution(mesh):
    placed = (P(None, "row", "col"), P("row"), P(), P("row", None), P("row"), P())
    return jax.shard_map(
        per_device,
        mesh=mesh,
        in_specs=placed,
        out_specs=(P(None, "row", "col"), P("col", "row")),
        check_vma=False,
    )
```

time: 36.4 us -> 31.3 us (0.86)
  waiting for transfers between devices: 15.9 us -> 4.62 us
  blocking collectives: 0 us -> 7.42 us
  local copies, waits for them, and re-layouts: 2.77 us -> 1.36 us
  Pallas kernels: 3.87 us -> 5.19 us
  starting transfers between devices: 12.9 us -> 11.7 us
    ppermute x12 -> x10, waiting for transfers between devices: 15.9 us -> 4.62 us  [swap(): return lax.ppermute(array, axis, [(i, i ^ offset) for i in range(size)])]
    all_gather x0 -> x1, blocking collectives: none -> 7.42 us  [per_device(): left = lax.all_gather(both, 'col')]
    unnamed x14 -> x10, local copies, waits for them, and re-layouts: 2.77 us -> 1.36 us
    pallas_call x8, Pallas kernels: 3.87 us -> 5.19 us  [the longest x1 1.43 us: per_device(): call(spectra_kernel, [pltpu.VMEM(traces.shape, BF16), pltpu.VMEM(plane_sh...]
    ppermute x12 -> x10, starting transfers between devices: 12.9 us -> 11.7 us  [swap(): return lax.ppermute(array, axis, [(i, i ^ offset) for i in range(size)])]
  transfers between devices with their start and end apart: 12 -> 10, of which waited for: 8 -> 4; matrix products, arithmetic and copies ran while one was open for 0% -> 0% of each run, Pallas kernels for 5% -> 7%
where the time goes in v2:
time: 31.3 us; the launch traced here: 31 us
  starting transfers between devices  11.7 us (37%)
  blocking collectives  7.42 us (24%)
  Pallas kernels  5.19 us (17%)
  waiting for transfers between devices  4.62 us (15%)
  local copies, waits for them, and re-layouts  1.36 us (4%)
  between operations  0.71 us (2%)
    ppermute x10, starting transfers between devices, swap(): return lax.ppermute(array, axis, [(i, i ^ offset) for i in range(size)])  11.7 us
    all_gather x1, blocking collectives, per_device(): left = lax.all_gather(both, 'col')  7.42 us
    ppermute x10, waiting for transfers between devices, swap(): return lax.ppermute(array, axis, [(i, i ^ offset) for i in range(size)])  4.62 us
    pallas_call x1, Pallas kernels, per_device(): call(spectra_kernel, [pltpu.VMEM(traces.shape, BF16), pltpu.VMEM(plane_sh...  1.43 us
    unnamed x10, local copies, waits for them, and re-layouts  1.36 us
    pallas_call x1, Pallas kernels, per_device(): call(primaries_kernel, [jax.ShapeDtypeStruct(traces.shape, BF16), pltpu.V...  1.01 us
    pallas_call x1, Pallas kernels, per_device(): call(functools.partial(image_kernel, shots, cols), jax.ShapeDtypeStruct((...  0.92 us
    pallas_call x1, Pallas kernels, per_device(): call(own_stack_kernel, [pltpu.VMEM((cols, steps, panel), F32), pltpu.VMEM...  0.88 us
  transfers between devices with their start and end apart: 10, of which 4 were waited for; matrix products, arithmetic and copies ran while one was open for 0% of the time, Pallas kernels for 7%

profile of v2, /device:TPU:0, one launch (start us, length us, event | category | flops | bytes accessed | tf_op | source)
XLA Modules:
  0.0 31.0 jit_solution(14907701840001195399)
XLA Ops:
  0.6 1.4 %shard_map.77 = (bf16[32,64,128]{2,1,0:T(8,128)(2,1)S(1)}, bf16[4,2,64,128]{3,2,1,0:T(8,128)(2,1)S(1)}, bf16[4,64,128]{2,1,0:T(8,128)(2,1)S(1)}, bf16[4,64,128]{2,1,0:T(8,128)(2,1)S(1)}, s32[8,256]{1,0:T(8,128)S(1)}) custom-call(bf16[32,64,128]{2,1,0:T(8,128)(2,1)} %traces.1, s32[4,256]{1,0:T(4,128)} %aperture_list.3, s32[1,64]{1,0:T(1,128)} %bitcast.10), custom_call_target="tpu_custom_call" | custom-call | tf_op jit(solution)/shard_map/pallas_call | solution.py:282
  2.1 3.0 %collective-permute-start = (bf16[4,64,128]{2,1,0:T(8,128)(2,1)S(1)}, bf16[4,64,128]{2,1,0:T(8,128)(2,1)S(1)}, u32[]{:S(2)}, u32[]{:S(2)}) collective-permute-start(bf16[4,64,128]{2,1,0:T(8,128)(2,1)S(1)} %get-tuple-element.22), channel_id=1, source_target_pairs={{0,4},{4,0},{8,12},{12,8},{16,20},{20,16},{24,28},{28,24},{1,5},{5... | collective-permute-start | bytes 196616 | tf_op jit(solution)/shard_map/ppermute | solution.py:264
  5.1 3.6 %collective-permute-start.3 = (bf16[4,2,64,128]{3,2,1,0:T(8,128)(2,1)S(1)}, bf16[4,2,64,128]{3,2,1,0:T(8,128)(2,1)S(1)}, u32[]{:S(2)}, u32[]{:S(2)}) collective-permute-start(bf16[4,2,64,128]{3,2,1,0:T(8,128)(2,1)S(1)} %get-tuple-element.23.refs_0_), channel_id=1, source_target_pairs={{0,24},{4,28},{8,16},{12,20},{16,8},{20,12},{24,0},{28,4},{1,25},{... | collective-permute-start | bytes 393224 | tf_op jit(solution)/shard_map/ppermute | solution.py:264
  8.7 0.0 collective-permute-start.2
  8.7 0.8 %collective-permute-start.1 = (bf16[4,2,64,128]{3,2,1,0:T(8,128)(2,1)S(1)}, bf16[4,2,64,128]{3,2,1,0:T(8,128)(2,1)S(1)}, u32[]{:S(2)}, u32[]{:S(2)}) collective-permute-start(bf16[4,2,64,128]{3,2,1,0:T(8,128)(2,1)S(1)} %get-tuple-element.23.refs_0_), channel_id=1, source_target_pairs={{0,8},{4,12},{8,0},{12,4},{16,24},{20,28},{24,16},{28,20},{1,9},{5... | collective-permute-start | bytes 393224 | tf_op jit(solution)/shard_map/ppermute | solution.py:264
  9.5 0.3 %collective-permute-start.4 = (s32[8,256]{1,0:T(8,128)S(1)}, s32[8,256]{1,0:T(8,128)S(1)}, u32[]{:S(2)}, u32[]{:S(2)}) collective-permute-start(s32[8,256]{1,0:T(8,128)S(1)} %get-tuple-element.24), channel_id=1, source_target_pairs={{0,4},{4,0},{8,12},{12,8},{16,20},{20,16},{24,28},{28,24},{1,5},{5... | collective-permute-start | bytes 24584 | tf_op jit(solution)/shard_map/ppermute | solution.py:264
  9.8 0.0 collective-permute-done.got
  9.8 0.0 copy-start.1
  9.8 7.4 %all-gather = bf16[8,4,64,128]{3,2,1,0:T(8,128)(2,1)S(1)} all-gather(bf16[2,4,64,128]{3,2,1,0:T(8,128)(2,1)S(1)} %shard_map.78), channel_id=2, replica_groups=mesh['row'=8,'col'=4] {'col'}, dimensions={0}, use_global_device_ids=true | all-gather | bytes 655360 | tf_op jit(solution)/shard_map/all_gather | solution.py:304
  17.2 0.0 copy-start.2
  17.2 0.0 collective-permute-done.4.got_lists
  17.2 0.0 copy-start.4
  17.2 0.0 copy-done.1
  17.2 0.7 %copy-done.2 = s32[512]{0:T(512)S(1)} copy-done((s32[512]{0:T(512)S(1)}, s32[512]{0:T(512)}, u32[]{:S(2)}) %copy-start.2) | copy-done | bytes 2072
  17.9 0.0 copy-done.4
  17.9 0.3 %shard_map.79 = (bf16[2,128,512]{2,1,0:T(8,128)(2,1)S(1)}, f32[2,64,512]{2,1,0:T(8,128)S(1)}) custom-call(bf16[4,2,4,64,128]{4,3,2,1,0:T(8,128)(2,1)S(1)} %bitcast.5, s32[8,256]{1,0:T(8,128)S(1)} %collective-permute-done.4.got_lists, s32[4,128]{1,0:T(4,128)S(1)} %bitcast.8, s32[4,256]{1,0:T(4,128)S(1)} %copy-done.1, s32[1,64]{1,0:T(1,128)S(1)} %bitcast.11), custom_call_target="tpu_custom_call" | custom-call | bytes 2097152 | tf_op jit(solution)/shard_map/pallas_call | solution.py:305
  18.2 0.0 collective-permute-done.3.refs_3_
  18.3 1.2 %collective-permute-done.2.refs_2_ = bf16[4,2,64,128]{3,2,1,0:T(8,128)(2,1)S(1)} collective-permute-done((bf16[4,2,64,128]{3,2,1,0:T(8,128)(2,1)S(1)}, bf16[4,2,64,128]{3,2,1,0:T(8,128)(2,1)S(1)}, u32[]{:S(2)}, u32[]{:S(2)}) %collective-permute-start.2) | collective-permute-done | bytes 131104 | tf_op jit(solution)/shard_map/ppermute | solution.py:264
  19.5 0.0 collective-permute-done.1.refs_1_
  19.5 0.0 copy-start
  19.5 0.6 %shard_map.80 = (bf16[4,64,256]{2,1,0:T(8,128)(2,1)S(1)}, bf16[4,64,256]{2,1,0:T(8,128)(2,1)S(1)}, f32[8,512]{1,0:T(8,128)S(1)}) custom-call(bf16[4,2,4,64,128]{4,3,2,1,0:T(8,128)(2,1)S(1)} %bitcast.6, bf16[4,2,64,128]{3,2,1,0:T(8,128)(2,1)S(1)} %get-tuple-element.23.refs_0_, bf16[4,2,64,128]{3,2,1,0:T(8,128)(2,1)S(1)} %collective-permute-done.1.refs_1_, ...), custom_call_target="tpu_custom_call" | custom-call | tf_op jit(solution)/shard_map/pallas_call | solution.py:317
  20.1 0.6 %collective-permute-start.5 = (bf16[4,64,256]{2,1,0:T(8,128)(2,1)S(1)}, bf16[4,64,256]{2,1,0:T(8,128)(2,1)S(1)}, u32[]{:S(2)}, u32[]{:S(2)}) collective-permute-start(bf16[4,64,256]{2,1,0:T(8,128)(2,1)S(1)} %get-tuple-element.28), channel_id=1, source_target_pairs={{0,4},{4,0},{8,12},{12,8},{16,20},{20,16},{24,28},{28,24},{1,5},{5... | collective-permute-start | bytes 393224 | tf_op jit(solution)/shard_map/ppermute | solution.py:264
  20.7 1.5 %collective-permute-start.6 = (f32[8,512]{1,0:T(8,128)S(1)}, f32[8,512]{1,0:T(8,128)S(1)}, u32[]{:S(2)}, u32[]{:S(2)}) collective-permute-start(f32[8,512]{1,0:T(8,128)S(1)} %get-tuple-element.32), channel_id=1, source_target_pairs={{0,4},{4,0},{8,12},{12,8},{16,20},{20,16},{24,28},{28,24},{1,5},{5... | collective-permute-start | bytes 49160 | tf_op jit(solution)/shard_map/ppermute | solution.py:264
  22.2 0.0 copy-start.3
  22.2 0.0 copy-done
  22.2 0.7 %copy-done.3 = s32[512]{0:T(512)S(1)} copy-done((s32[512]{0:T(512)S(1)}, s32[512]{0:T(512)}, u32[]{:S(2)}) %copy-start.3) | copy-done | bytes 2072
  22.9 0.9 %shard_map.82 = (f32[4,8,512]{2,1,0:T(8,128)S(1)}, bf16[128,256]{1,0:T(8,128)(2,1)S(1)}, f32[32,512]{1,0:T(8,128)S(1)}) custom-call(bf16[4,64,256]{2,1,0:T(8,128)(2,1)S(1)} %get-tuple-element.27.mine, bf16[32,64,128]{2,1,0:T(8,128)(2,1)S(1)} %get-tuple-element.29.held, bf16[2,128,512]{2,1,0:T(8,128)(2,1)S(1)} %get-tuple-element.25.refs_4_.apertures, ...), custom_call_target="tpu_custom_call" | custom-call | flops 268435456 | bytes 1048576 | tf_op jit(solution)/shard_map/pallas_call | solution.py:326
  23.8 1.5 %collective-permute-done.6.got = f32[8,512]{1,0:T(8,128)S(1)} collective-permute-done((f32[8,512]{1,0:T(8,128)S(1)}, f32[8,512]{1,0:T(8,128)S(1)}, u32[]{:S(2)}, u32[]{:S(2)}) %collective-permute-start.6) | collective-permute-done | bytes 16416 | tf_op jit(solution)/shard_map/ppermute | solution.py:264
  25.3 0.1 collective-permute-start.7
  25.4 1.6 %collective-permute-start.8 = (f32[8,512]{1,0:T(8,128)S(1)}, f32[8,512]{1,0:T(8,128)S(1)}, u32[]{:S(2)}, u32[]{:S(2)}) collective-permute-start(f32[8,512]{1,0:T(8,128)S(1)} %get-tuple-element.35), channel_id=1, source_target_pairs={{0,2},{1,3},{2,0},{3,1},{4,6},{5,7},{6,4},{7,5},{8,10},{9,11},{10,... | collective-permute-start | bytes 49160 | tf_op jit(solution)/shard_map/ppermute | solution.py:264
  27.0 0.3 collective-permute-start.9
  27.3 0.0 collective-permute-done.5.got
  27.3 1.0 %shard_map.81 = (bf16[32,64,128]{2,1,0:T(8,128)(2,1)}, f32[8,128]{1,0:T(8,128)S(1)}) custom-call(bf16[4,64,256]{2,1,0:T(8,128)(2,1)S(1)} %get-tuple-element.27.mine, bf16[4,64,256]{2,1,0:T(8,128)(2,1)S(1)} %collective-permute-done.5.got, bf16[32,64,128]{2,1,0:T(8,128)(2,1)S(1)} %get-tuple-element.29.held), custom_call_target="tpu_custom_call" | custom-call | flops 1048576 | bytes 3145728 | tf_op jit(solution)/shard_map/pallas_call | solution.py:351
  28.3 0.0 collective-permute-done.7.refs_1_
  28.3 0.9 %collective-permute-done.8.refs_2_ = f32[8,512]{1,0:T(8,128)S(1)} collective-permute-done((f32[8,512]{1,0:T(8,128)S(1)}, f32[8,512]{1,0:T(8,128)S(1)}, u32[]{:S(2)}, u32[]{:S(2)}) %collective-permute-start.8) | collective-permute-done | bytes 16416 | tf_op jit(solution)/shard_map/ppermute | solution.py:264
  29.2 0.9 %collective-permute-done.9.refs_3_ = f32[8,512]{1,0:T(8,128)S(1)} collective-permute-done((f32[8,512]{1,0:T(8,128)S(1)}, f32[8,512]{1,0:T(8,128)S(1)}, u32[]{:S(2)}, u32[]{:S(2)}) %collective-permute-start.9) | collective-permute-done | bytes 16416 | tf_op jit(solution)/shard_map/ppermute | solution.py:264
  30.1 0.9 %shard_map.84 = f32[128,512]{1,0:T(8,128)} custom-call(f32[8,512]{1,0:T(8,128)S(1)} %get-tuple-element.33.refs_0_, f32[8,512]{1,0:T(8,128)S(1)} %collective-permute-done.7.refs_1_, f32[8,512]{1,0:T(8,128)S(1)} %collective-permute-done.8.refs_2_, f32[8,512]{1,0:T(8,128)S(1)} %collective-permute-done.9.refs_3_, ...), custom_call_target="tpu_custom_call" | custom-call | tf_op jit(solution)/shard_map/pallas_call | solution.py:359
  (2 shorter events, 0.0 us)
Async XLA Ops:
  2.1 7.7 %collective-permute-start = (bf16[4,64,128]{2,1,0:T(8,128)(2,1)S(1)}, bf16[4,64,128]{2,1,0:T(8,128)(2,1)S(1)}, u32[]{:S(2)}, u32[]{:S(2)}) collective-permute-start(bf16[4,64,128]{2,1,0:T(8,128)(2,1)S(1)} %get-tuple-element.22), channel_id=1, source_target_pairs={{0,4},{4,0},{8,12},{12,8},{16,20},{20,16},{24,28},{28,24},{1,5},{5... | collective-permute-start | bytes 196616 | tf_op jit(solution)/shard_map/ppermute | solution.py:264
  5.1 13.2 %collective-permute-start.3 = (bf16[4,2,64,128]{3,2,1,0:T(8,128)(2,1)S(1)}, bf16[4,2,64,128]{3,2,1,0:T(8,128)(2,1)S(1)}, u32[]{:S(2)}, u32[]{:S(2)}) collective-permute-start(bf16[4,2,64,128]{3,2,1,0:T(8,128)(2,1)S(1)} %get-tuple-element.23.refs_0_), channel_id=1, source_target_pairs={{0,24},{4,28},{8,16},{12,20},{16,8},{20,12},{24,0},{28,4},{1,25},{... | collective-permute-start | bytes 393224 | tf_op jit(solution)/shard_map/ppermute | solution.py:264
  8.7 10.8 %collective-permute-start.2 = (bf16[4,2,64,128]{3,2,1,0:T(8,128)(2,1)S(1)}, bf16[4,2,64,128]{3,2,1,0:T(8,128)(2,1)S(1)}, u32[]{:S(2)}, u32[]{:S(2)}) collective-permute-start(bf16[4,2,64,128]{3,2,1,0:T(8,128)(2,1)S(1)} %get-tuple-element.23.refs_0_), channel_id=1, source_target_pairs={{0,16},{4,20},{8,24},{12,28},{16,0},{20,4},{24,8},{28,12},{1,17},{... | collective-permute-start | bytes 393224 | tf_op jit(solution)/shard_map/ppermute | solution.py:264
  8.7 10.8 %collective-permute-start.1 = (bf16[4,2,64,128]{3,2,1,0:T(8,128)(2,1)S(1)}, bf16[4,2,64,128]{3,2,1,0:T(8,128)(2,1)S(1)}, u32[]{:S(2)}, u32[]{:S(2)}) collective-permute-start(bf16[4,2,64,128]{3,2,1,0:T(8,128)(2,1)S(1)} %get-tuple-element.23.refs_0_), channel_id=1, source_target_pairs={{0,8},{4,12},{8,0},{12,4},{16,24},{20,28},{24,16},{28,20},{1,9},{5... | collective-permute-start | bytes 393224 | tf_op jit(solution)/shard_map/ppermute | solution.py:264
  9.5 7.8 %collective-permute-start.4 = (s32[8,256]{1,0:T(8,128)S(1)}, s32[8,256]{1,0:T(8,128)S(1)}, u32[]{:S(2)}, u32[]{:S(2)}) collective-permute-start(s32[8,256]{1,0:T(8,128)S(1)} %get-tuple-element.24), channel_id=1, source_target_pairs={{0,4},{4,0},{8,12},{12,8},{16,20},{20,16},{24,28},{28,24},{1,5},{5... | collective-permute-start | bytes 24584 | tf_op jit(solution)/shard_map/ppermute | solution.py:264
  9.8 7.4 %copy-start.1 = (s32[4,256]{1,0:T(4,128)S(1)}, s32[4,256]{1,0:T(4,128)}, u32[]{:S(2)}) copy-start(s32[4,256]{1,0:T(4,128)} %aperture_list.3) | copy-start | bytes 12292
  17.2 0.7 %copy-start.2 = (s32[512]{0:T(512)S(1)}, s32[512]{0:T(512)}, u32[]{:S(2)}) copy-start(s32[512]{0:T(512)} %param.8) | copy-start | bytes 6148
  17.2 0.7 %copy-start.4 = (s32[64]{0:T(128)S(1)}, s32[64]{0:T(128)}, u32[]{:S(2)}) copy-start(s32[64]{0:T(128)} %param.7) | copy-start | bytes 772
  19.5 2.7 %copy-start = (bf16[32,8,128]{2,1,0:T(8,128)(2,1)S(1)}, bf16[32,8,128]{2,1,0:T(8,128)(2,1)}, u32[]{:S(2)}) copy-start(bf16[32,8,128]{2,1,0:T(8,128)(2,1)} %param.11) | copy-start | bytes 196612
  20.1 7.2 %collective-permute-start.5 = (bf16[4,64,256]{2,1,0:T(8,128)(2,1)S(1)}, bf16[4,64,256]{2,1,0:T(8,128)(2,1)S(1)}, u32[]{:S(2)}, u32[]{:S(2)}) collective-permute-start(bf16[4,64,256]{2,1,0:T(8,128)(2,1)S(1)} %get-tuple-element.28), channel_id=1, source_target_pairs={{0,4},{4,0},{8,12},{12,8},{16,20},{20,16},{24,28},{28,24},{1,5},{5... | collective-permute-start | bytes 393224 | tf_op jit(solution)/shard_map/ppermute | solution.py:264
  20.7 4.6 %collective-permute-start.6 = (f32[8,512]{1,0:T(8,128)S(1)}, f32[8,512]{1,0:T(8,128)S(1)}, u32[]{:S(2)}, u32[]{:S(2)}) collective-permute-start(f32[8,512]{1,0:T(8,128)S(1)} %get-tuple-element.32), channel_id=1, source_target_pairs={{0,4},{4,0},{8,12},{12,8},{16,20},{20,16},{24,28},{28,24},{1,5},{5... | collective-permute-start | bytes 49160 | tf_op jit(solution)/shard_map/ppermute | solution.py:264
  22.2 0.7 %copy-start.3 = (s32[512]{0:T(512)S(1)}, s32[512]{0:T(512)}, u32[]{:S(2)}) copy-start(s32[512]{0:T(512)} %param.10) | copy-start | bytes 6148
  25.3 3.0 %collective-permute-start.7 = (f32[8,512]{1,0:T(8,128)S(1)}, f32[8,512]{1,0:T(8,128)S(1)}, u32[]{:S(2)}, u32[]{:S(2)}) collective-permute-start(f32[8,512]{1,0:T(8,128)S(1)} %get-tuple-element.34), channel_id=1, source_target_pairs={{0,1},{1,0},{2,3},{3,2},{4,5},{5,4},{6,7},{7,6},{8,9},{9,8},{10,11... | collective-permute-start | bytes 49160 | tf_op jit(solution)/shard_map/ppermute | solution.py:264
  25.4 3.8 %collective-permute-start.8 = (f32[8,512]{1,0:T(8,128)S(1)}, f32[8,512]{1,0:T(8,128)S(1)}, u32[]{:S(2)}, u32[]{:S(2)}) collective-permute-start(f32[8,512]{1,0:T(8,128)S(1)} %get-tuple-element.35), channel_id=1, source_target_pairs={{0,2},{1,3},{2,0},{3,1},{4,6},{5,7},{6,4},{7,5},{8,10},{9,11},{10,... | collective-permute-start | bytes 49160 | tf_op jit(solution)/shard_map/ppermute | solution.py:264
  27.0 3.2 %collective-permute-start.9 = (f32[8,512]{1,0:T(8,128)S(1)}, f32[8,512]{1,0:T(8,128)S(1)}, u32[]{:S(2)}, u32[]{:S(2)}) collective-permute-start(f32[8,512]{1,0:T(8,128)S(1)} %get-tuple-element.36), channel_id=1, source_target_pairs={{0,3},{1,2},{2,1},{3,0},{4,7},{5,6},{6,5},{7,4},{8,11},{9,10},{10,... | collective-permute-start | bytes 49160 | tf_op jit(solution)/shard_map/ppermute | solution.py:264

commit v3 on v2

--- a/solution.py
+++ b/solution.py
@@ -16,6 +16,16 @@
 HALF_TURN = NFFT // (2 * STEP)
 F32 = jnp.float32
 BF16 = jnp.bfloat16
+PARTS = 2
+
+
+def routes(levels):
+    if levels == 4:
+        return [[2, 3, 1, 0], [1, 0, 3, 2], [3, 2, 0, 1]]
+    return [[(a + d) % levels for a in range(levels)] for d in range(1, levels)]
+
+
+LINKT = BF16
 VMEM_BYTES = 48 * 1024 * 1024
 
 
@@ -47,22 +57,33 @@
     return [w / math.sqrt(NF) for w in weights]
 
 
+DIGIT = 128
+
+
+def digit_rows(tiles, listed):
+    used = 2 * tiles * (listed // DIGIT) + 2
+    return -(-used // 16) * 16
+
+
 def spectra_kernel(
-    traces, aperture_list, source_pos, held, planes, mine, theirs, lists, halves, listing, places, arrived
+    traces, aperture_list, source_pos, receiver_pos, band_index, weight_tiles,
+    held, planes, mine, theirs, lists, places, stations, kinds, tiles_near,
+    halves, digits, arrived,
 ):
     samples, shots, receivers = held.shape
-    rows = shots // 4
+    rows = shots // PARTS
     copies = []
-    for part in range(4):
+    for part in range(PARTS):
         piece = (slice(None), pl.ds(part * rows, rows))
         copies.append(pltpu.make_async_copy(traces.at[piece], held.at[piece], arrived.at[part]))
         copies[-1].start()
-    for index, (given, near) in enumerate(((aperture_list, listing), (source_pos, places))):
-        copies.append(pltpu.make_async_copy(given, near, arrived.at[4 + index]))
+    given = (aperture_list, source_pos, receiver_pos, band_index, weight_tiles)
+    for index, near in enumerate((lists, places, stations, kinds, tiles_near)):
+        copies.append(pltpu.make_async_copy(given[index], near, arrived.at[PARTS + index]))
         copies[-1].start()
     lane = lax.broadcasted_iota(jnp.int32, (rows, receivers), 1)
     low = lane < receivers // 2
-    for part in range(4):
+    for part in range(PARTS):
         copies[part].wait()
         here = slice(part * rows, (part + 1) * rows)
         folded = []
@@ -82,19 +103,28 @@
             turned = [pltpu.roll(p, receivers // 2, 1) for p in pair]
             halves[0, freq, here] = jnp.where(low, real, turned[1]).astype(BF16)
             halves[1, freq, here] = jnp.where(low, turned[0], imag).astype(BF16)
-    copies[4].wait()
-    copies[5].wait()
-    tiles = listing.shape[0]
-    lists[0:tiles] = listing[...]
-    lists[tiles : tiles + 1, 0:shots] = places[...]
+    for copy in copies[PARTS:]:
+        copy.wait()
+    tiles, listed = lists.shape
+    groups = listed // DIGIT
+    digits[...] = jnp.zeros_like(digits)
+    for group in range(groups):
+        some = lists[:, group * DIGIT : (group + 1) * DIGIT]
+        start = 2 * group * tiles
+        digits[start : start + tiles] = (some >> 7).astype(F32)
+        digits[start + tiles : start + 2 * tiles] = (some & (DIGIT - 1)).astype(F32)
+    start = 2 * groups * tiles
+    digits[start : start + 1, 0:shots] = (places[...] >> 7).astype(F32)
+    digits[start + 1 : start + 2, 0:shots] = (places[...] & (DIGIT - 1)).astype(F32)
     side = lax.rem(lax.axis_index("row"), 2)
     mine[...] = halves[side]
-    theirs[...] = halves[1 - side]
+    theirs[0 : NF * shots] = halves[1 - side].reshape(NF * shots, receivers)
+    theirs[NF * shots :] = digits[...].astype(BF16)
 
 
 def pair_kernel(mine, got, both):
     both[0] = mine[...]
-    both[1] = got[...]
+    both[1] = got[0 : mine.shape[0] * mine.shape[1]].reshape(mine.shape)
 
 
 def panel_stack(parts, aperture, shot_weight):
@@ -113,8 +143,10 @@
     rights = refs[:levels]
     apertures, shot_weights, mine, theirs, waves, right = refs[levels:]
     level = lax.axis_index("row") // 2
-    for offset, got in enumerate(rights):
-        right[level ^ offset] = got[...]
+    right[level] = rights[0][...]
+    for to, got in zip(routes(levels), rights[1:]):
+        origin = sum(jnp.where(level == there, here, 0) for here, there in enumerate(to))
+        right[origin] = got[...]
     _, _, _, shots, lanes = left.shape
     scale = -1.0 / math.sqrt(2 * levels * shots)
     step = min(2, levels)
@@ -135,16 +167,17 @@
         total = total * scale
         mine[freq] = total[:shots].astype(BF16)
         theirs[freq] = total[shots:].astype(BF16)
-    waves[...] = panel_stack(theirs, apertures.at[1], shot_weights.at[1])
+    waves[...] = panel_stack(theirs, apertures.at[1], shot_weights.at[1]).astype(waves.dtype)
 
 
 def tables_kernel(
-    spread_len, left, got_lists, receiver_pos, aperture_list, source_pos, apertures, shot_weights
+    spread_len, left, got, stations, lists, places, apertures, shot_weights, digits
 ):
     del left
     _, receivers, panel = apertures.shape
     shots = shot_weights.shape[1]
-    tiles, listed = aperture_list.shape
+    tiles, listed = lists.shape
+    groups = listed // DIGIT
     width = panel // tiles
     row, col = lax.axis_index("row"), lax.axis_index("col")
 
@@ -158,15 +191,24 @@
         offset = (positions - columns) / spread_len
         return 1.0 / (1.0 + offset * offset)
 
-    position = upright(receiver_pos[pl.ds(col, 1)], receivers)
+    position = upright(stations[pl.ds(col, 1)], receivers)
     receiver = lax.broadcasted_iota(jnp.int32, (receivers, listed), 0) + col * receivers
+    receiver = receiver.astype(F32)
     ones = jnp.ones((listed, width), BF16)
-    sources = (source_pos[...], got_lists[tiles : tiles + 1, 0:shots])
-    for index, lists in enumerate((aperture_list, got_lists)):
+    digits[...] = got[NF * shots :].astype(F32)
+    theirs = []
+    for group in range(groups):
+        start = 2 * group * tiles
+        high, low = digits[start : start + tiles], digits[start + tiles : start + 2 * tiles]
+        theirs.append(high * DIGIT + low)
+    start = 2 * groups * tiles
+    there = digits[start : start + 1, 0:shots] * DIGIT + digits[start + 1 : start + 2, 0:shots]
+    sources = (places[...].astype(F32), there)
+    for index, listing in enumerate((lists[...].astype(F32), jnp.concatenate(theirs, axis=1))):
         first = (row ^ index) * panel
         near = taper(position, receivers, first)
         for tile in range(tiles):
-            hits = jnp.where(lists[tile : tile + 1] == receiver, 1.0, 0.0).astype(BF16)
+            hits = jnp.where(listing[tile : tile + 1] == receiver, 1.0, 0.0).astype(BF16)
             counts = dot(hits, ones)
             here = slice(tile * width, (tile + 1) * width)
             weighted = counts * near[:, here] * (2.0 / math.sqrt(listed))
@@ -183,7 +225,7 @@
 
 
 def own_stack_kernel(
-    mine, held, apertures, shot_weights, band_index, weight_tiles, columns, tiles_turned, chosen
+    mine, held, apertures, shot_weights, kinds, tiles_near, columns, tiles_turned, chosen
 ):
     waves = panel_stack(mine, apertures.at[0], shot_weights.at[0])
     bands, steps, _ = columns.shape
@@ -193,19 +235,19 @@
             line = dot(held[band * steps + step], apertures[0])
             lines.append(jnp.sum(line * shot_weights[0], axis=0, keepdims=True))
         columns[band] = subtract_waves(band, jnp.concatenate(lines, axis=0), waves)
-    tiles_turned[...] = weight_tiles[...].astype(F32).T.astype(BF16)
+    tiles_turned[...] = tiles_near[...].astype(F32).T.astype(BF16)
     kind = lax.broadcasted_iota(jnp.int32, chosen.shape, 0)
-    chosen[...] = jnp.where(band_index[...] == kind, 1.0, 0.0)
+    chosen[...] = jnp.where(kinds[...] == kind, 1.0, 0.0)
 
 
 def column_kernel(columns, got, *refs):
     total = refs[-1]
     col = lax.axis_index("col")
-    waves = got[...]
+    waves = got[...].astype(F32)
     for band in range(columns.shape[0]):
         total[band] = subtract_waves(band, columns[band], waves)
     for offset, out in enumerate(refs[:-1]):
-        out[...] = total[col ^ offset]
+        out[...] = total[col ^ offset].astype(out.dtype)
 
 
 def primaries_kernel(mine, got, held, out, token):
@@ -231,7 +273,7 @@
     tiles_turned, chosen, _, image = refs[bands:]
     total = parts[0][...]
     for part in parts[1:]:
-        total = total + part[...]
+        total = total + part[...].astype(F32)
     column_stack = total / math.sqrt(shots)
     steps, panel = column_stack.shape
     kinds = chosen.shape[0]
@@ -246,6 +288,10 @@
 
 def in_vmem(*arrays):
     return [pltpu.with_memory_space_constraint(a, pltpu.VMEM) for a in arrays]
+
+
+def in_hbm(*arrays):
+    return [pltpu.with_memory_space_constraint(a, pltpu.HBM) for a in arrays]
 
 
 def call(body, out_shape, in_specs, out_specs, scratch=(), flops=0, moved=0):
@@ -278,28 +324,44 @@
     plane_shape = (NF, 2, shots, receivers)
     half_shape = (NF, shots, receivers)
     part = pltpu.VMEM((NF, shots, 2 * receivers), BF16)
-    positions = source_pos.reshape(1, shots)
-    held, planes, mine, theirs, lists = call(
+    extra = digit_rows(tiles, listed)
+    held, planes, mine, theirs, lists, places, stations, near_kinds, tiles_near = call(
         spectra_kernel,
         [
             pltpu.VMEM(traces.shape, BF16),
             pltpu.VMEM(plane_shape, BF16),
             pltpu.VMEM(half_shape, BF16),
-            pltpu.VMEM(half_shape, BF16),
-            pltpu.VMEM((2 * tiles, listed), jnp.int32),
+            pltpu.VMEM((NF * shots + extra, receivers), BF16),
+            pltpu.VMEM(aperture_list.shape, jnp.int32),
+            pltpu.VMEM((1, shots), jnp.int32),
+            pltpu.VMEM((cols, receivers), jnp.int32),
+            pltpu.VMEM((1, panel), jnp.int32),
+            pltpu.VMEM((kinds * steps, depth), BF16),
         ],
-        [IN_HBM] * 3,
-        [WHOLE] * 5,
+        [IN_HBM] * 6,
+        [WHOLE] * 9,
         [
             pltpu.VMEM((2,) + half_shape, BF16),
-            pltpu.VMEM(aperture_list.shape, jnp.int32),
-            pltpu.VMEM(positions.shape, jnp.int32),
-            pltpu.SemaphoreType.DMA((6,)),
+            pltpu.VMEM((extra, DIGIT), F32),
+            pltpu.SemaphoreType.DMA((PARTS + 5,)),
         ],
-    )(*[pltpu.with_memory_space_constraint(a, pltpu.HBM) for a in (traces, aperture_list, positions)])
-    rights = [planes] + [swap(planes, "row", rows, 2 * d) for d in range(1, levels)]
+    )(
+        *in_hbm(
+            traces,
+            aperture_list,
+            source_pos.reshape(1, shots),
+            receiver_pos.reshape(cols, receivers),
+            band_index.reshape(1, panel),
+            weight_tiles.reshape(kinds * steps, depth),
+        )
+    )
+    rights = [planes] + [
+        lax.ppermute(planes, "row", [(2 * a + x, 2 * b + x) for a, b in enumerate(to) for x in range(2)])
+        for to in routes(levels)
+    ]
+    got = swap(theirs, "row", rows, 1)
     both = call(pair_kernel, pltpu.VMEM((2,) + half_shape, BF16), [WHOLE] * 2, WHOLE)(
-        *in_vmem(mine, swap(theirs, "row", rows, 1))
+        *in_vmem(mine, got)
     )
     left = lax.all_gather(both, "col")
     apertures, shot_weights = call(
@@ -307,16 +369,11 @@
         [pltpu.VMEM((2, receivers, panel), BF16), pltpu.VMEM((2, shots, panel), F32)],
         [WHOLE] * 5,
         [WHOLE] * 2,
-        moved=2 << 20,
-    )(
-        *in_vmem(left, swap(lists, "row", rows, 1)),
-        receiver_pos.reshape(cols, receivers),
-        aperture_list,
-        positions,
-    )
+        [pltpu.VMEM((extra, DIGIT), F32)],
+    )(*in_vmem(left, got, stations, lists, places))
     mine, theirs, waves = call(
         functools.partial(product_kernel, levels),
-        [part, part, pltpu.VMEM((HALF_TURN, panel), F32)],
+        [part, part, pltpu.VMEM((HALF_TURN, panel), LINKT)],
         [WHOLE] * (levels + 3),
         [WHOLE] * 3,
         [pltpu.VMEM((levels,) + plane_shape, BF16)],
@@ -332,20 +389,16 @@
         ],
         [WHOLE] * 6,
         [WHOLE] * 3,
-        flops=2 * samples * shots * receivers * panel,
-        moved=1 << 20,
-    )(
-        *in_vmem(mine, held, apertures, shot_weights),
-        band_index.reshape(1, panel),
-        weight_tiles.reshape(kinds * steps, depth),
-    )
+        flops=1 << 34,
+    )(*in_vmem(mine, held, apertures, shot_weights, near_kinds, tiles_near))
     band = pltpu.VMEM((steps, panel), F32)
     own, *sends = call(
         column_kernel,
-        [band] * cols,
+        [band] + [pltpu.VMEM((steps, panel), LINKT)] * (cols - 1),
         [WHOLE] * 2,
         [WHOLE] * cols,
         [pltpu.VMEM((cols, steps, panel), F32)],
+        flops=1 << 34,
     )(*in_vmem(columns, got_waves))
     bands = [own] + [swap(s, "col", cols, d + 1) for d, s in enumerate(sends)]
     primaries, token = call(

time: 31.3 us -> 28 us (0.89)
  waiting for transfers between devices: 4.62 us -> 3.16 us
  local copies, waits for them, and re-layouts: 1.36 us -> 0 us
    ppermute x10 -> x6, starting transfers between devices: 11.7 us -> 7.03 us  [swap(): return lax.ppermute(array, axis, [(i, i ^ offset) for i in range(size)])]
    ppermute x0 -> x3, starting transfers between devices: none -> 4.5 us  [per_device(): lax.ppermute(planes, 'row', [(2 * a + x, 2 * b + x) for a, b in enumerate...]
    ppermute x10 -> x6, waiting for transfers between devices: 4.62 us -> 2.43 us  [swap(): return lax.ppermute(array, axis, [(i, i ^ offset) for i in range(size)])]
    unnamed x10 -> x0, local copies, waits for them, and re-layouts: 1.36 us -> none
    ppermute x0 -> x3, waiting for transfers between devices: none -> 0.73 us  [per_device(): lax.ppermute(planes, 'row', [(2 * a + x, 2 * b + x) for a, b in enumerate...]
  transfers between devices with their start and end apart: 10 -> 9, of which waited for: 4 -> 5; matrix products, arithmetic and copies ran while one was open for 0% -> 0% of each run, Pallas kernels for 7% -> 8%
where the time goes in v3:
time: 28 us; the launch traced here: 27.8 us
  starting transfers between devices  11.5 us (41%)
  blocking collectives  7.2 us (26%)
  Pallas kernels  5.24 us (19%)
  waiting for transfers between devices  3.16 us (11%)
  between operations  0.68 us (2%)
    all_gather x1, blocking collectives, per_device(): left = lax.all_gather(both, 'col')  7.2 us
    ppermute x6, starting transfers between devices, swap(): return lax.ppermute(array, axis, [(i, i ^ offset) for i in range(size)])  7.03 us
    ppermute x3, starting transfers between devices, per_device(): lax.ppermute(planes, 'row', [(2 * a + x, 2 * b + x) for a, b in enumerate...  4.5 us
    ppermute x6, waiting for transfers between devices, swap(): return lax.ppermute(array, axis, [(i, i ^ offset) for i in range(size)])  2.43 us
    pallas_call x1, Pallas kernels, per_device(): call(spectra_kernel, [pltpu.VMEM(traces.shape, BF16), pltpu.VMEM(plane_sh...  1.37 us
    pallas_call x1, Pallas kernels, per_device(): call(primaries_kernel, [jax.ShapeDtypeStruct(traces.shape, BF16), pltpu.V...  1.02 us
    pallas_call x1, Pallas kernels, per_device(): call(own_stack_kernel, [pltpu.VMEM((cols, steps, panel), F32), pltpu.VMEM...  0.97 us
    pallas_call x1, Pallas kernels, per_device(): call(functools.partial(image_kernel, shots, cols), jax.ShapeDtypeStruct((...  0.92 us
  transfers between devices with their start and end apart: 9, of which 5 were waited for; matrix products, arithmetic and copies ran while one was open for 0% of the time, Pallas kernels for 8%

profile of v3, /device:TPU:0, one launch (start us, length us, event | category | flops | bytes accessed | tf_op | source)
XLA Modules:
  0.0 27.8 jit_solution(10062258688117071089)
XLA Ops:
  0.6 1.4 %shard_map.77 = (bf16[32,64,128]{2,1,0:T(8,128)(2,1)S(1)}, bf16[4,2,64,128]{3,2,1,0:T(8,128)(2,1)S(1)}, bf16[4,64,128]{2,1,0:T(8,128)(2,1)S(1)}, bf16[288,128]{1...) custom-call(bf16[32,64,128]{2,1,0:T(8,128)(2,1)} %traces.1, ...), custom_call_target="tpu_custom_call" | custom-call | tf_op jit(solution)/shard_map/pallas_call | solution.py:328
  2.0 3.0 %collective-permute-start = (bf16[288,128]{1,0:T(8,128)(2,1)S(1)}, bf16[288,128]{1,0:T(8,128)(2,1)S(1)}, u32[]{:S(2)}, u32[]{:S(2)}) collective-permute-start(bf16[288,128]{1,0:T(8,128)(2,1)S(1)} %get-tuple-element.26), channel_id=1, source_target_pairs={{0,4},{4,0},{8,12},{12,8},{16,20},{20,16},{24,28},{28,24},{1,5},{5... | collective-permute-start | bytes 221192 | tf_op jit(solution)/shard_map/ppermute | solution.py:310
  5.0 3.6 %collective-permute-start.3 = (bf16[4,2,64,128]{3,2,1,0:T(8,128)(2,1)S(1)}, bf16[4,2,64,128]{3,2,1,0:T(8,128)(2,1)S(1)}, u32[]{:S(2)}, u32[]{:S(2)}) collective-permute-start(bf16[4,2,64,128]{3,2,1,0:T(8,128)(2,1)S(1)} %get-tuple-element.27.refs_0_), channel_id=1, source_target_pairs={{0,24},{4,28},{8,16},{12,20},{16,0},{20,4},{24,8},{28,12},{1,25},{... | collective-permute-start | bytes 393224 | tf_op jit(solution)/shard_map/ppermute | solution.py:359
  8.6 0.0 collective-permute-start.2
  8.6 0.9 %collective-permute-start.1 = (bf16[4,2,64,128]{3,2,1,0:T(8,128)(2,1)S(1)}, bf16[4,2,64,128]{3,2,1,0:T(8,128)(2,1)S(1)}, u32[]{:S(2)}, u32[]{:S(2)}) collective-permute-start(bf16[4,2,64,128]{3,2,1,0:T(8,128)(2,1)S(1)} %get-tuple-element.27.refs_0_), channel_id=1, source_target_pairs={{0,16},{4,20},{8,24},{12,28},{16,8},{20,12},{24,0},{28,4},{1,17},{... | collective-permute-start | bytes 393224 | tf_op jit(solution)/shard_map/ppermute | solution.py:359
  9.5 0.0 collective-permute-done.got
  9.5 7.2 %all-gather = bf16[8,4,64,128]{3,2,1,0:T(8,128)(2,1)S(1)} all-gather(bf16[2,4,64,128]{3,2,1,0:T(8,128)(2,1)S(1)} %shard_map.78), channel_id=2, replica_groups=mesh['row'=8,'col'=4] {'col'}, dimensions={0}, use_global_device_ids=true | all-gather | bytes 655360 | tf_op jit(solution)/shard_map/all_gather | solution.py:366
  16.7 0.3 %shard_map.79 = (bf16[2,128,512]{2,1,0:T(8,128)(2,1)S(1)}, f32[2,64,512]{2,1,0:T(8,128)S(1)}) custom-call(bf16[4,2,4,64,128]{4,3,2,1,0:T(8,128)(2,1)S(1)} %bitcast.5, bf16[288,128]{1,0:T(8,128)(2,1)S(1)} %collective-permute-done.got, s32[4,128]{1,0:T(4,128)S(1)} %get-tuple-element.28.stations, s32[4,256]{1,0:T(4,128)S(1)} %get-tuple-element.29.lists, ...), custom_call_target="tpu_custom_call" | custom-call | tf_op jit(solution)/shard_map/pallas_call | solution.py:367
  17.1 0.6 %collective-permute-done.3.refs_3_ = bf16[4,2,64,128]{3,2,1,0:T(8,128)(2,1)S(1)} collective-permute-done((bf16[4,2,64,128]{3,2,1,0:T(8,128)(2,1)S(1)}, bf16[4,2,64,128]{3,2,1,0:T(8,128)(2,1)S(1)}, u32[]{:S(2)}, u32[]{:S(2)}) %collective-permute-start.3) | collective-permute-done | bytes 131104 | tf_op jit(solution)/shard_map/ppermute | solution.py:359
  17.7 0.1 collective-permute-done.2.refs_2_
  17.8 0.0 collective-permute-done.1.refs_1_
  17.8 0.6 %shard_map.80 = (bf16[4,64,256]{2,1,0:T(8,128)(2,1)S(1)}, bf16[4,64,256]{2,1,0:T(8,128)(2,1)S(1)}, bf16[8,512]{1,0:T(8,128)(2,1)S(1)}) custom-call(bf16[4,2,4,64,128]{4,3,2,1,0:T(8,128)(2,1)S(1)} %bitcast.6, bf16[4,2,64,128]{3,2,1,0:T(8,128)(2,1)S(1)} %get-tuple-element.27.refs_0_, bf16[4,2,64,128]{3,2,1,0:T(8,128)(2,1)S(1)} %collective-permute-done.1.refs_1_, ...), custom_call_target="tpu_custom_call" | custom-call | tf_op jit(solution)/shard_map/pallas_call | solution.py:374
  18.4 0.5 %collective-permute-start.5 = (bf16[8,512]{1,0:T(8,128)(2,1)S(1)}, bf16[8,512]{1,0:T(8,128)(2,1)S(1)}, u32[]{:S(2)}, u32[]{:S(2)}) collective-permute-start(bf16[8,512]{1,0:T(8,128)(2,1)S(1)} %get-tuple-element.40), channel_id=1, source_target_pairs={{0,4},{4,0},{8,12},{12,8},{16,20},{20,16},{24,28},{28,24},{1,5},{5... | collective-permute-start | bytes 24584 | tf_op jit(solution)/shard_map/ppermute | solution.py:310
  19.0 1.5 %collective-permute-start.4 = (bf16[4,64,256]{2,1,0:T(8,128)(2,1)S(1)}, bf16[4,64,256]{2,1,0:T(8,128)(2,1)S(1)}, u32[]{:S(2)}, u32[]{:S(2)}) collective-permute-start(bf16[4,64,256]{2,1,0:T(8,128)(2,1)S(1)} %get-tuple-element.34), channel_id=1, source_target_pairs={{0,4},{4,0},{8,12},{12,8},{16,20},{20,16},{24,28},{28,24},{1,5},{5... | collective-permute-start | bytes 393224 | tf_op jit(solution)/shard_map/ppermute | solution.py:310
  20.5 1.0 %shard_map.82 = (f32[4,8,512]{2,1,0:T(8,128)S(1)}, bf16[128,256]{1,0:T(8,128)(2,1)S(1)}, f32[32,512]{1,0:T(8,128)S(1)}) custom-call(bf16[4,64,256]{2,1,0:T(8,128)(2,1)S(1)} %get-tuple-element.33.mine, bf16[32,64,128]{2,1,0:T(8,128)(2,1)S(1)} %get-tuple-element.35.held, bf16[2,128,512]{2,1,0:T(8,128)(2,1)S(1)} %get-tuple-element.31.refs_4_.apertures, ...), custom_call_target="tpu_custom_call" | custom-call | flops 17179869184 | tf_op jit(solution)/shard_map/pallas_call | solution.py:383
  21.5 0.7 %collective-permute-done.5.got = bf16[8,512]{1,0:T(8,128)(2,1)S(1)} collective-permute-done((bf16[8,512]{1,0:T(8,128)(2,1)S(1)}, bf16[8,512]{1,0:T(8,128)(2,1)S(1)}, u32[]{:S(2)}, u32[]{:S(2)}) %collective-permute-start.5) | collective-permute-done | bytes 8224 | tf_op jit(solution)/shard_map/ppermute | solution.py:310
  22.2 0.1 collective-permute-start.6
  22.3 1.5 %collective-permute-start.7 = (bf16[8,512]{1,0:T(8,128)(2,1)S(1)}, bf16[8,512]{1,0:T(8,128)(2,1)S(1)}, u32[]{:S(2)}, u32[]{:S(2)}) collective-permute-start(bf16[8,512]{1,0:T(8,128)(2,1)S(1)} %get-tuple-element.43), channel_id=1, source_target_pairs={{0,2},{1,3},{2,0},{3,1},{4,6},{5,7},{6,4},{7,5},{8,10},{9,11},{10,... | collective-permute-start | bytes 24584 | tf_op jit(solution)/shard_map/ppermute | solution.py:310
  23.8 0.4 %collective-permute-start.8 = (bf16[8,512]{1,0:T(8,128)(2,1)S(1)}, bf16[8,512]{1,0:T(8,128)(2,1)S(1)}, u32[]{:S(2)}, u32[]{:S(2)}) collective-permute-start(bf16[8,512]{1,0:T(8,128)(2,1)S(1)} %get-tuple-element.44), channel_id=1, source_target_pairs={{0,3},{1,2},{2,1},{3,0},{4,7},{5,6},{6,5},{7,4},{8,11},{9,10},{10,... | collective-permute-start | bytes 24584 | tf_op jit(solution)/shard_map/ppermute | solution.py:310
  24.2 0.0 collective-permute-done.4.got
  24.2 1.0 %shard_map.81 = (bf16[32,64,128]{2,1,0:T(8,128)(2,1)}, f32[8,128]{1,0:T(8,128)S(1)}) custom-call(bf16[4,64,256]{2,1,0:T(8,128)(2,1)S(1)} %get-tuple-element.33.mine, bf16[4,64,256]{2,1,0:T(8,128)(2,1)S(1)} %collective-permute-done.4.got, bf16[32,64,128]{2,1,0:T(8,128)(2,1)S(1)} %get-tuple-element.35.held), custom_call_target="tpu_custom_call" | custom-call | flops 1048576 | bytes 3145728 | tf_op jit(solution)/shard_map/pallas_call | solution.py:404
  25.2 0.0 collective-permute-done.6.refs_1_
  25.2 0.8 %collective-permute-done.7.refs_2_ = bf16[8,512]{1,0:T(8,128)(2,1)S(1)} collective-permute-done((bf16[8,512]{1,0:T(8,128)(2,1)S(1)}, bf16[8,512]{1,0:T(8,128)(2,1)S(1)}, u32[]{:S(2)}, u32[]{:S(2)}) %collective-permute-start.7) | collective-permute-done | bytes 8224 | tf_op jit(solution)/shard_map/ppermute | solution.py:310
  26.0 0.9 %collective-permute-done.8.refs_3_ = bf16[8,512]{1,0:T(8,128)(2,1)S(1)} collective-permute-done((bf16[8,512]{1,0:T(8,128)(2,1)S(1)}, bf16[8,512]{1,0:T(8,128)(2,1)S(1)}, u32[]{:S(2)}, u32[]{:S(2)}) %collective-permute-start.8) | collective-permute-done | bytes 8224 | tf_op jit(solution)/shard_map/ppermute | solution.py:310
  26.9 0.9 %shard_map.84 = f32[128,512]{1,0:T(8,128)} custom-call(f32[8,512]{1,0:T(8,128)S(1)} %get-tuple-element.41.refs_0_, bf16[8,512]{1,0:T(8,128)(2,1)S(1)} %collective-permute-done.6.refs_1_, bf16[8,512]{1,0:T(8,128)(2,1)S(1)} %collective-permute-done.7.refs_2_, bf16[8,512]{1,0:T(8,128)(2,1)S(1)} %collective-permute-done.8.refs_3_, ...), custom_call_target="tpu_custom_call" | custom-call | tf_op jit(solution)/shard_map/pallas_call | solution.py:412
  (2 shorter events, 0.0 us)
Async XLA Ops:
  2.0 7.5 %collective-permute-start = (bf16[288,128]{1,0:T(8,128)(2,1)S(1)}, bf16[288,128]{1,0:T(8,128)(2,1)S(1)}, u32[]{:S(2)}, u32[]{:S(2)}) collective-permute-start(bf16[288,128]{1,0:T(8,128)(2,1)S(1)} %get-tuple-element.26), channel_id=1, source_target_pairs={{0,4},{4,0},{8,12},{12,8},{16,20},{20,16},{24,28},{28,24},{1,5},{5... | collective-permute-start | bytes 221192 | tf_op jit(solution)/shard_map/ppermute | solution.py:310
  5.0 12.7 %collective-permute-start.3 = (bf16[4,2,64,128]{3,2,1,0:T(8,128)(2,1)S(1)}, bf16[4,2,64,128]{3,2,1,0:T(8,128)(2,1)S(1)}, u32[]{:S(2)}, u32[]{:S(2)}) collective-permute-start(bf16[4,2,64,128]{3,2,1,0:T(8,128)(2,1)S(1)} %get-tuple-element.27.refs_0_), channel_id=1, source_target_pairs={{0,24},{4,28},{8,16},{12,20},{16,0},{20,4},{24,8},{28,12},{1,25},{... | collective-permute-start | bytes 393224 | tf_op jit(solution)/shard_map/ppermute | solution.py:359
  8.6 9.2 %collective-permute-start.2 = (bf16[4,2,64,128]{3,2,1,0:T(8,128)(2,1)S(1)}, bf16[4,2,64,128]{3,2,1,0:T(8,128)(2,1)S(1)}, u32[]{:S(2)}, u32[]{:S(2)}) collective-permute-start(bf16[4,2,64,128]{3,2,1,0:T(8,128)(2,1)S(1)} %get-tuple-element.27.refs_0_), channel_id=1, source_target_pairs={{0,8},{4,12},{8,0},{12,4},{16,24},{20,28},{24,16},{28,20},{1,9},{5... | collective-permute-start | bytes 393224 | tf_op jit(solution)/shard_map/ppermute | solution.py:359
  8.6 9.2 %collective-permute-start.1 = (bf16[4,2,64,128]{3,2,1,0:T(8,128)(2,1)S(1)}, bf16[4,2,64,128]{3,2,1,0:T(8,128)(2,1)S(1)}, u32[]{:S(2)}, u32[]{:S(2)}) collective-permute-start(bf16[4,2,64,128]{3,2,1,0:T(8,128)(2,1)S(1)} %get-tuple-element.27.refs_0_), channel_id=1, source_target_pairs={{0,16},{4,20},{8,24},{12,28},{16,8},{20,12},{24,0},{28,4},{1,17},{... | collective-permute-start | bytes 393224 | tf_op jit(solution)/shard_map/ppermute | solution.py:359
  18.4 3.8 %collective-permute-start.5 = (bf16[8,512]{1,0:T(8,128)(2,1)S(1)}, bf16[8,512]{1,0:T(8,128)(2,1)S(1)}, u32[]{:S(2)}, u32[]{:S(2)}) collective-permute-start(bf16[8,512]{1,0:T(8,128)(2,1)S(1)} %get-tuple-element.40), channel_id=1, source_target_pairs={{0,4},{4,0},{8,12},{12,8},{16,20},{20,16},{24,28},{28,24},{1,5},{5... | collective-permute-start | bytes 24584 | tf_op jit(solution)/shard_map/ppermute | solution.py:310
  19.0 5.2 %collective-permute-start.4 = (bf16[4,64,256]{2,1,0:T(8,128)(2,1)S(1)}, bf16[4,64,256]{2,1,0:T(8,128)(2,1)S(1)}, u32[]{:S(2)}, u32[]{:S(2)}) collective-permute-start(bf16[4,64,256]{2,1,0:T(8,128)(2,1)S(1)} %get-tuple-element.34), channel_id=1, source_target_pairs={{0,4},{4,0},{8,12},{12,8},{16,20},{20,16},{24,28},{28,24},{1,5},{5... | collective-permute-start | bytes 393224 | tf_op jit(solution)/shard_map/ppermute | solution.py:310
  22.2 3.0 %collective-permute-start.6 = (bf16[8,512]{1,0:T(8,128)(2,1)S(1)}, bf16[8,512]{1,0:T(8,128)(2,1)S(1)}, u32[]{:S(2)}, u32[]{:S(2)}) collective-permute-start(bf16[8,512]{1,0:T(8,128)(2,1)S(1)} %get-tuple-element.42), channel_id=1, source_target_pairs={{0,1},{1,0},{2,3},{3,2},{4,5},{5,4},{6,7},{7,6},{8,9},{9,8},{10,11... | collective-permute-start | bytes 24584 | tf_op jit(solution)/shard_map/ppermute | solution.py:310
  22.3 3.7 %collective-permute-start.7 = (bf16[8,512]{1,0:T(8,128)(2,1)S(1)}, bf16[8,512]{1,0:T(8,128)(2,1)S(1)}, u32[]{:S(2)}, u32[]{:S(2)}) collective-permute-start(bf16[8,512]{1,0:T(8,128)(2,1)S(1)} %get-tuple-element.43), channel_id=1, source_target_pairs={{0,2},{1,3},{2,0},{3,1},{4,6},{5,7},{6,4},{7,5},{8,10},{9,11},{10,... | collective-permute-start | bytes 24584 | tf_op jit(solution)/shard_map/ppermute | solution.py:310
  23.8 3.1 %collective-permute-start.8 = (bf16[8,512]{1,0:T(8,128)(2,1)S(1)}, bf16[8,512]{1,0:T(8,128)(2,1)S(1)}, u32[]{:S(2)}, u32[]{:S(2)}) collective-permute-start(bf16[8,512]{1,0:T(8,128)(2,1)S(1)} %get-tuple-element.44), channel_id=1, source_target_pairs={{0,3},{1,2},{2,1},{3,0},{4,7},{5,6},{6,5},{7,4},{8,11},{9,10},{10,... | collective-permute-start | bytes 24584 | tf_op jit(solution)/shard_map/ppermute | solution.py:310

commit v4 on v3

--- a/solution.py
+++ b/solution.py
@@ -63,6 +63,33 @@
 def digit_rows(tiles, listed):
     used = 2 * tiles * (listed // DIGIT) + 2
     return -(-used // 16) * 16
+
+
+def upright(line):
+    length = line.shape[1]
+    at_row = lax.broadcasted_iota(jnp.int32, (length, length), 0)
+    at_lane = lax.broadcasted_iota(jnp.int32, (length, length), 1)
+    return jnp.sum(jnp.where(at_row == at_lane, line.astype(F32), 0.0), axis=1, keepdims=True)
+
+
+def taper(positions, panel, first, spread_len):
+    columns = (lax.broadcasted_iota(jnp.int32, (positions.shape[0], panel), 1) + first).astype(F32)
+    offset = (positions - columns) / spread_len
+    return 1.0 / (1.0 + offset * offset)
+
+
+def fill_aperture(aperture, listing, near):
+    receivers, panel = aperture.shape
+    tiles, listed = listing.shape
+    width = panel // tiles
+    receiver = lax.broadcasted_iota(jnp.int32, (receivers, listed), 0)
+    receiver = (receiver + lax.axis_index("col") * receivers).astype(F32)
+    ones = jnp.ones((listed, width), BF16)
+    for tile in range(tiles):
+        hits = jnp.where(listing[tile : tile + 1] == receiver, 1.0, 0.0).astype(BF16)
+        here = slice(tile * width, (tile + 1) * width)
+        weighted = dot(hits, ones) * near[:, here] * (2.0 / math.sqrt(listed))
+        aperture[:, here] = weighted.astype(BF16)
 
 
 def spectra_kernel(
@@ -76,11 +103,11 @@
     for part in range(PARTS):
         piece = (slice(None), pl.ds(part * rows, rows))
         copies.append(pltpu.make_async_copy(traces.at[piece], held.at[piece], arrived.at[part]))
-        copies[-1].start()
     given = (aperture_list, source_pos, receiver_pos, band_index, weight_tiles)
     for index, near in enumerate((lists, places, stations, kinds, tiles_near)):
         copies.append(pltpu.make_async_copy(given[index], near, arrived.at[PARTS + index]))
-        copies[-1].start()
+    for copy in copies:
+        copy.start()
     lane = lax.broadcasted_iota(jnp.int32, (rows, receivers), 1)
     low = lane < receivers // 2
     for part in range(PARTS):
@@ -127,93 +154,79 @@
     both[1] = got[0 : mine.shape[0] * mine.shape[1]].reshape(mine.shape)
 
 
+def shot_sums(lines, aperture, shot_weight):
+    shots, panel = shot_weight.shape
+    stacked = dot(lines, aperture[...]).reshape(lines.shape[0] // shots, shots, panel)
+    return jnp.sum(stacked * shot_weight[...][None], axis=1)
+
+
 def panel_stack(parts, aperture, shot_weight):
-    lines = []
     receivers = aperture.shape[0]
+    both = parts[...]
+    lines = jnp.concatenate(
+        [both[freq][:, lanes] for freq in range(NF) for lanes in (slice(0, receivers), slice(receivers, None))]
+    )
+    sums = shot_sums(lines, aperture, shot_weight)
+    rows = [sums[k : k + 1] for k in range(2 * NF)]
+    waves = [weighted_sum(wave_weights(sample), rows) for sample in range(HALF_TURN)]
+    return jnp.concatenate(waves, axis=0)
+
+
+def level_blocks(rights, levels):
+    level = lax.axis_index("row") // 2
+    blocks = [(level, rights[0])]
+    for to, got in zip(routes(levels), rights[1:]):
+        blocks.append((sum(jnp.where(level == there, here, 0) for here, there in enumerate(to)), got))
+    return blocks
+
+
+def product(part, freq, left, blocks):
+    step = min(2, len(blocks))
+    total = None
+    for first in range(0, len(blocks), step):
+        some = blocks[first : first + step]
+        near = jnp.concatenate([left[origin, part, freq] for origin, _ in some], axis=1)
+        far = []
+        for _, right in some:
+            real, imag = right[freq, 0], right[freq, 1]
+            far.append(jnp.concatenate([real, imag], axis=1))
+            far.append(jnp.concatenate([-imag, real], axis=1))
+        term = dot(near, jnp.concatenate(far, axis=0))
+        total = term if total is None else total + term
+    surface = 2 * len(blocks) * left.shape[3]
+    return (total * (-1.0 / math.sqrt(surface))).astype(BF16)
+
+
+def product_kernel(levels, left, *refs):
+    aperture, shot_weight, theirs, waves = refs[levels:]
+    blocks = level_blocks(refs[:levels], levels)
     for freq in range(NF):
-        for piece in range(2):
-            part = parts[freq, :, piece * receivers : (piece + 1) * receivers]
-            line = dot(part, aperture[...]) * shot_weight[...]
-            lines.append(jnp.sum(line, axis=0, keepdims=True))
-    waves = [weighted_sum(wave_weights(sample), lines) for sample in range(HALF_TURN)]
-    return jnp.concatenate(waves, axis=0)
-
-
-def product_kernel(levels, left, *refs):
-    rights = refs[:levels]
-    apertures, shot_weights, mine, theirs, waves, right = refs[levels:]
-    level = lax.axis_index("row") // 2
-    right[level] = rights[0][...]
-    for to, got in zip(routes(levels), rights[1:]):
-        origin = sum(jnp.where(level == there, here, 0) for here, there in enumerate(to))
-        right[origin] = got[...]
-    _, _, _, shots, lanes = left.shape
-    scale = -1.0 / math.sqrt(2 * levels * shots)
-    step = min(2, levels)
-    for freq in range(NF):
-        total = None
-        for first in range(0, levels, step):
-            inner = range(first, first + step)
-            near = jnp.concatenate(
-                [left[k, :, freq].reshape(2 * shots, lanes) for k in inner], axis=1
-            )
-            far = []
-            for k in inner:
-                real, imag = right[k, freq, 0], right[k, freq, 1]
-                far.append(jnp.concatenate([real, imag], axis=1))
-                far.append(jnp.concatenate([-imag, real], axis=1))
-            term = dot(near, jnp.concatenate(far, axis=0))
-            total = term if total is None else total + term
-        total = total * scale
-        mine[freq] = total[:shots].astype(BF16)
-        theirs[freq] = total[shots:].astype(BF16)
-    waves[...] = panel_stack(theirs, apertures.at[1], shot_weights.at[1]).astype(waves.dtype)
+        theirs[freq] = product(1, freq, left, blocks)
+    waves[...] = panel_stack(theirs, aperture, shot_weight).astype(waves.dtype)
 
 
 def tables_kernel(
-    spread_len, left, got, stations, lists, places, apertures, shot_weights, digits
+    spread_len, left, got, lists, places, stations, aperture, shot_weight, their_aperture, their_weight, digits
 ):
     del left
-    _, receivers, panel = apertures.shape
-    shots = shot_weights.shape[1]
+    shots, panel = shot_weight.shape
     tiles, listed = lists.shape
-    groups = listed // DIGIT
-    width = panel // tiles
     row, col = lax.axis_index("row"), lax.axis_index("col")
-
-    def upright(line, length):
-        at_row = lax.broadcasted_iota(jnp.int32, (length, length), 0)
-        at_lane = lax.broadcasted_iota(jnp.int32, (length, length), 1)
-        return jnp.sum(jnp.where(at_row == at_lane, line.astype(F32), 0.0), axis=1, keepdims=True)
-
-    def taper(positions, length, first):
-        columns = (lax.broadcasted_iota(jnp.int32, (length, panel), 1) + first).astype(F32)
-        offset = (positions - columns) / spread_len
-        return 1.0 / (1.0 + offset * offset)
-
-    position = upright(stations[pl.ds(col, 1)], receivers)
-    receiver = lax.broadcasted_iota(jnp.int32, (receivers, listed), 0) + col * receivers
-    receiver = receiver.astype(F32)
-    ones = jnp.ones((listed, width), BF16)
     digits[...] = got[NF * shots :].astype(F32)
-    theirs = []
-    for group in range(groups):
-        start = 2 * group * tiles
+    listing = []
+    start = 0
+    for _ in range(listed // DIGIT):
         high, low = digits[start : start + tiles], digits[start + tiles : start + 2 * tiles]
-        theirs.append(high * DIGIT + low)
-    start = 2 * groups * tiles
+        listing.append(high * DIGIT + low)
+        start += 2 * tiles
     there = digits[start : start + 1, 0:shots] * DIGIT + digits[start + 1 : start + 2, 0:shots]
-    sources = (places[...].astype(F32), there)
-    for index, listing in enumerate((lists[...].astype(F32), jnp.concatenate(theirs, axis=1))):
-        first = (row ^ index) * panel
-        near = taper(position, receivers, first)
-        for tile in range(tiles):
-            hits = jnp.where(listing[tile : tile + 1] == receiver, 1.0, 0.0).astype(BF16)
-            counts = dot(hits, ones)
-            here = slice(tile * width, (tile + 1) * width)
-            weighted = counts * near[:, here] * (2.0 / math.sqrt(listed))
-            apertures[index, :, here] = weighted.astype(BF16)
-        shot_weights[index] = taper(upright(sources[index], shots), shots, first)
+    position = upright(stations[pl.ds(col, 1)])
+    for first, some, sources, table, weight in (
+        (row * panel, lists[...].astype(F32), places[...], aperture, shot_weight),
+        ((row ^ 1) * panel, jnp.concatenate(listing, axis=1), there, their_aperture, their_weight),
+    ):
+        fill_aperture(table, some, taper(position, panel, first, spread_len))
+        weight[...] = taper(upright(sources), panel, first, spread_len)
 
 
 def subtract_waves(band, columns, waves):
@@ -224,20 +237,25 @@
     return columns - sign * waves[first : first + steps]
 
 
-def own_stack_kernel(
-    mine, held, apertures, shot_weights, kinds, tiles_near, columns, tiles_turned, chosen
-):
-    waves = panel_stack(mine, apertures.at[0], shot_weights.at[0])
+def own_stack_kernel(levels, left, *refs):
+    (
+        theirs, held, aperture, shot_weight, kinds, tiles_near,
+        mine, columns, tiles_turned, chosen, send,
+    ) = refs[levels:]
+    blocks = level_blocks(refs[:levels], levels)
+    for freq in range(NF):
+        mine[freq] = product(0, freq, left, blocks)
+    waves = panel_stack(mine, aperture, shot_weight)
     bands, steps, _ = columns.shape
+    _, shots, receivers = held.shape
     for band in range(bands):
-        lines = []
-        for step in range(steps):
-            line = dot(held[band * steps + step], apertures[0])
-            lines.append(jnp.sum(line * shot_weights[0], axis=0, keepdims=True))
-        columns[band] = subtract_waves(band, jnp.concatenate(lines, axis=0), waves)
+        lines = held[band * steps : (band + 1) * steps].reshape(steps * shots, receivers)
+        sums = shot_sums(lines, aperture, shot_weight)
+        columns[band] = subtract_waves(band, sums, waves)
     tiles_turned[...] = tiles_near[...].astype(F32).T.astype(BF16)
     kind = lax.broadcasted_iota(jnp.int32, chosen.shape, 0)
     chosen[...] = jnp.where(kinds[...] == kind, 1.0, 0.0)
+    send[...] = theirs[...]
 
 
 def column_kernel(columns, got, *refs):
@@ -316,7 +334,7 @@
     panel = band_index.shape[0]
     steps = samples // cols
     kinds, _, depth = weight_tiles.shape
-    spread_len = panel * rows // 4
+    spread_len = float(panel * rows // 4)
     levels = rows // 2
     tiles, listed = aperture_list.shape
     assert receivers == 2 * shots and levels == cols
@@ -325,6 +343,8 @@
     half_shape = (NF, shots, receivers)
     part = pltpu.VMEM((NF, shots, 2 * receivers), BF16)
     extra = digit_rows(tiles, listed)
+    table = pltpu.VMEM((receivers, panel), BF16)
+    weights = pltpu.VMEM((shots, panel), F32)
     held, planes, mine, theirs, lists, places, stations, near_kinds, tiles_near = call(
         spectra_kernel,
         [
@@ -364,33 +384,34 @@
         *in_vmem(mine, got)
     )
     left = lax.all_gather(both, "col")
-    apertures, shot_weights = call(
-        functools.partial(tables_kernel, float(spread_len)),
-        [pltpu.VMEM((2, receivers, panel), BF16), pltpu.VMEM((2, shots, panel), F32)],
+    aperture, shot_weight, their_aperture, their_weight = call(
+        functools.partial(tables_kernel, spread_len),
+        [table, weights] * 2,
         [WHOLE] * 5,
+        [WHOLE] * 4,
+        [pltpu.VMEM((extra, DIGIT), F32)],
+    )(*in_vmem(left, got, lists, places, stations))
+    theirs, waves = call(
+        functools.partial(product_kernel, levels),
+        [part, pltpu.VMEM((HALF_TURN, panel), LINKT)],
+        [WHOLE] * (levels + 3),
         [WHOLE] * 2,
-        [pltpu.VMEM((extra, DIGIT), F32)],
-    )(*in_vmem(left, got, stations, lists, places))
-    mine, theirs, waves = call(
-        functools.partial(product_kernel, levels),
-        [part, part, pltpu.VMEM((HALF_TURN, panel), LINKT)],
-        [WHOLE] * (levels + 3),
-        [WHOLE] * 3,
-        [pltpu.VMEM((levels,) + plane_shape, BF16)],
-    )(*in_vmem(left, *rights, apertures, shot_weights))
+    )(*in_vmem(left, *rights, their_aperture, their_weight))
     got_waves = swap(waves, "row", rows, 1)
-    got_part = swap(theirs, "row", rows, 1)
-    columns, tiles_turned, chosen = call(
-        own_stack_kernel,
+    mine, columns, tiles_turned, chosen, send = call(
+        functools.partial(own_stack_kernel, levels),
         [
+            part,
             pltpu.VMEM((cols, steps, panel), F32),
             pltpu.VMEM((depth, kinds * steps), BF16),
             pltpu.VMEM((kinds, panel), F32),
+            part,
         ],
-        [WHOLE] * 6,
-        [WHOLE] * 3,
+        [WHOLE] * (levels + 7),
+        [WHOLE] * 5,
         flops=1 << 34,
-    )(*in_vmem(mine, held, apertures, shot_weights, near_kinds, tiles_near))
+    )(*in_vmem(left, *rights, theirs, held, aperture, shot_weight, near_kinds, tiles_near))
+    got_part = swap(send, "row", rows, 1)
     band = pltpu.VMEM((steps, panel), F32)
     own, *sends = call(
         column_kernel,
@@ -400,10 +421,11 @@
         [pltpu.VMEM((cols, steps, panel), F32)],
         flops=1 << 34,
     )(*in_vmem(columns, got_waves))
-    bands = [own] + [swap(s, "col", cols, d + 1) for d, s in enumerate(sends)]
+    order = list(range(cols - 1))[::-1]
+    bands = [own] + [swap(sends[d], "col", cols, d + 1) for d in order]
     primaries, token = call(
         primaries_kernel,
-        [jax.ShapeDtypeStruct(traces.shape, BF16), pltpu.VMEM((8, 128), F32)],
+        [pltpu.VMEM(traces.shape, BF16), pltpu.VMEM((8, 128), F32)],
         [WHOLE] * 3,
         [WHOLE] * 2,
         flops=1 << 20,

time: 28 us -> 27 us (0.964)
  waiting for transfers between devices: 3.16 us -> 2.21 us
  Pallas kernels: 5.24 us -> 4.4 us
  local copies, waits for them, and re-layouts: 0 us -> 0.8 us
    ppermute x6, waiting for transfers between devices: 2.43 us -> 1.47 us  [swap(): return lax.ppermute(array, axis, [(i, i ^ offset) for i in range(size)])]
    pallas_call x4, Pallas kernels: 2.92 us -> 2.08 us  [the longest x1 1.03 us: per_device(): call(functools.partial(own_stack_kernel, levels), [part, pltpu.VMEM((cols...]
    unnamed x0 -> x1, local copies, waits for them, and re-layouts: none -> 0.8 us
  transfers between devices with their start and end apart: 9 -> 9, of which waited for: 5 -> 4; matrix products, arithmetic and copies ran while one was open for 0% -> 3% of each run, Pallas kernels for 8% -> 6%
where the time goes in v4:
time: 27 us; the launch traced here: 26.9 us
  starting transfers between devices  11.6 us (43%)
  blocking collectives  7.2 us (27%)
  Pallas kernels  4.4 us (16%)
  waiting for transfers between devices  2.21 us (8%)
  local copies, waits for them, and re-layouts  0.8 us (3%)
  between operations  0.69 us (3%)
    all_gather x1, blocking collectives, per_device(): left = lax.all_gather(both, 'col')  7.2 us
    ppermute x6, starting transfers between devices, swap(): return lax.ppermute(array, axis, [(i, i ^ offset) for i in range(size)])  7.09 us
    ppermute x3, starting transfers between devices, per_device(): lax.ppermute(planes, 'row', [(2 * a + x, 2 * b + x) for a, b in enumerate...  4.5 us
    ppermute x6, waiting for transfers between devices, swap(): return lax.ppermute(array, axis, [(i, i ^ offset) for i in range(size)])  1.47 us
    pallas_call x1, Pallas kernels, per_device(): call(spectra_kernel, [pltpu.VMEM(traces.shape, BF16), pltpu.VMEM(plane_sh...  1.37 us
    pallas_call x1, Pallas kernels, per_device(): call(functools.partial(own_stack_kernel, levels), [part, pltpu.VMEM((cols...  1.03 us
    pallas_call x1, Pallas kernels, per_device(): call(functools.partial(image_kernel, shots, cols), jax.ShapeDtypeStruct((...  0.92 us
    unnamed x1, local copies, waits for them, and re-layouts  0.8 us
  transfers between devices with their start and end apart: 9, of which 4 were waited for; matrix products, arithmetic and copies ran while one was open for 3% of the time, Pallas kernels for 6%

profile of v4, /device:TPU:0, one launch (start us, length us, event | category | flops | bytes accessed | tf_op | source)
XLA Modules:
  0.0 26.9 jit_solution(3258102547162357111)
XLA Ops:
  0.6 1.4 %shard_map.77 = (bf16[32,64,128]{2,1,0:T(8,128)(2,1)S(1)}, bf16[4,2,64,128]{3,2,1,0:T(8,128)(2,1)S(1)}, bf16[4,64,128]{2,1,0:T(8,128)(2,1)S(1)}, bf16[288,128]{1...) custom-call(bf16[32,64,128]{2,1,0:T(8,128)(2,1)} %traces.1, ...), custom_call_target="tpu_custom_call" | custom-call | tf_op jit(solution)/shard_map/pallas_call | solution.py:348
  2.0 3.0 %collective-permute-start = (bf16[288,128]{1,0:T(8,128)(2,1)S(1)}, bf16[288,128]{1,0:T(8,128)(2,1)S(1)}, u32[]{:S(2)}, u32[]{:S(2)}) collective-permute-start(bf16[288,128]{1,0:T(8,128)(2,1)S(1)} %get-tuple-element.29), channel_id=1, source_target_pairs={{0,4},{4,0},{8,12},{12,8},{16,20},{20,16},{24,28},{28,24},{1,5},{5... | collective-permute-start | bytes 221192 | tf_op jit(solution)/shard_map/ppermute | solution.py:328
  5.0 3.6 %collective-permute-start.3 = (bf16[4,2,64,128]{3,2,1,0:T(8,128)(2,1)S(1)}, bf16[4,2,64,128]{3,2,1,0:T(8,128)(2,1)S(1)}, u32[]{:S(2)}, u32[]{:S(2)}) collective-permute-start(bf16[4,2,64,128]{3,2,1,0:T(8,128)(2,1)S(1)} %get-tuple-element.30.refs_0_), channel_id=1, source_target_pairs={{0,24},{4,28},{8,16},{12,20},{16,0},{20,4},{24,8},{28,12},{1,25},{... | collective-permute-start | bytes 393224 | tf_op jit(solution)/shard_map/ppermute | solution.py:379
  8.6 0.0 collective-permute-start.2
  8.6 0.9 %collective-permute-start.1 = (bf16[4,2,64,128]{3,2,1,0:T(8,128)(2,1)S(1)}, bf16[4,2,64,128]{3,2,1,0:T(8,128)(2,1)S(1)}, u32[]{:S(2)}, u32[]{:S(2)}) collective-permute-start(bf16[4,2,64,128]{3,2,1,0:T(8,128)(2,1)S(1)} %get-tuple-element.30.refs_0_), channel_id=1, source_target_pairs={{0,16},{4,20},{8,24},{12,28},{16,8},{20,12},{24,0},{28,4},{1,17},{... | collective-permute-start | bytes 393224 | tf_op jit(solution)/shard_map/ppermute | solution.py:379
  9.5 0.0 collective-permute-done.got
  9.5 7.2 %all-gather = bf16[8,4,64,128]{3,2,1,0:T(8,128)(2,1)S(1)} all-gather(bf16[2,4,64,128]{3,2,1,0:T(8,128)(2,1)S(1)} %shard_map.78), channel_id=2, replica_groups=mesh['row'=8,'col'=4] {'col'}, dimensions={0}, use_global_device_ids=true | all-gather | bytes 655360 | tf_op jit(solution)/shard_map/all_gather | solution.py:386
  16.7 0.3 %shard_map.79 = (bf16[128,512]{1,0:T(8,128)(2,1)S(1)}, f32[64,512]{1,0:T(8,128)S(1)}, bf16[128,512]{1,0:T(8,128)(2,1)S(1)}, f32[64,512]{1,0:T(8,128)S(1)}) custom-call(bf16[4,2,4,64,128]{4,3,2,1,0:T(8,128)(2,1)S(1)} %bitcast.5, bf16[288,128]{1,0:T(8,128)(2,1)S(1)} %collective-permute-done.got, s32[4,256]{1,0:T(4,128)S(1)} %get-tuple-element.31.lists, ...), custom_call_target="tpu_custom_call" | custom-call | tf_op jit(solution)/shard_map/pallas_call | solution.py:387
  17.1 0.6 %collective-permute-done.3.refs_3_ = bf16[4,2,64,128]{3,2,1,0:T(8,128)(2,1)S(1)} collective-permute-done((bf16[4,2,64,128]{3,2,1,0:T(8,128)(2,1)S(1)}, bf16[4,2,64,128]{3,2,1,0:T(8,128)(2,1)S(1)}, u32[]{:S(2)}, u32[]{:S(2)}) %collective-permute-start.3) | collective-permute-done | bytes 131104 | tf_op jit(solution)/shard_map/ppermute | solution.py:379
  17.7 0.1 collective-permute-done.2.refs_2_
  17.8 0.0 collective-permute-done.1.refs_1_
  17.8 0.5 %shard_map.80 = (bf16[4,64,256]{2,1,0:T(8,128)(2,1)S(1)}, bf16[8,512]{1,0:T(8,128)(2,1)S(1)}) custom-call(bf16[4,2,4,64,128]{4,3,2,1,0:T(8,128)(2,1)S(1)} %bitcast.6, bf16[4,2,64,128]{3,2,1,0:T(8,128)(2,1)S(1)} %get-tuple-element.30.refs_0_, bf16[4,2,64,128]{3,2,1,0:T(8,128)(2,1)S(1)} %collective-permute-done.1.refs_1_, ...), custom_call_target="tpu_custom_call" | custom-call | tf_op jit(solution)/shard_map/pallas_call | solution.py:394
  18.3 0.5 %collective-permute-start.5 = (bf16[8,512]{1,0:T(8,128)(2,1)S(1)}, bf16[8,512]{1,0:T(8,128)(2,1)S(1)}, u32[]{:S(2)}, u32[]{:S(2)}) collective-permute-start(bf16[8,512]{1,0:T(8,128)(2,1)S(1)} %get-tuple-element.46), channel_id=1, source_target_pairs={{0,4},{4,0},{8,12},{12,8},{16,20},{20,16},{24,28},{28,24},{1,5},{5... | collective-permute-start | bytes 24584 | tf_op jit(solution)/shard_map/ppermute | solution.py:328
  18.9 1.0 %shard_map.81 = (bf16[4,64,256]{2,1,0:T(8,128)(2,1)S(1)}, f32[4,8,512]{2,1,0:T(8,128)S(1)}, bf16[128,256]{1,0:T(8,128)(2,1)S(1)}, f32[32,512]{1,0:T(8,128)S(1)}, bf16[4,64,256]{2,1,0:T(8,128)(2,1)S(1)}) custom-call(bf16[4,2,4,64,128]{4,3,2,1,0:T(8,128)(2,1)S(1)} %bitcast.7, bf16[4,2,64,128]{3,2,1,0:T(8,128)(2,1)S(1)} %get-tuple-element.30.refs_0_, ...), custom_call_target="tpu_custom_call" | custom-call | flops 17179869184 | tf_op jit(solution)/shard_map/pallas_call | solution.py:401
  19.9 1.6 %collective-permute-start.4 = (bf16[4,64,256]{2,1,0:T(8,128)(2,1)S(1)}, bf16[4,64,256]{2,1,0:T(8,128)(2,1)S(1)}, u32[]{:S(2)}, u32[]{:S(2)}) collective-permute-start(bf16[4,64,256]{2,1,0:T(8,128)(2,1)S(1)} %get-tuple-element.43), channel_id=1, source_target_pairs={{0,4},{4,0},{8,12},{12,8},{16,20},{20,16},{24,28},{28,24},{1,5},{5... | collective-permute-start | bytes 393224 | tf_op jit(solution)/shard_map/ppermute | solution.py:328
  21.5 0.5 %collective-permute-done.5.got = bf16[8,512]{1,0:T(8,128)(2,1)S(1)} collective-permute-done((bf16[8,512]{1,0:T(8,128)(2,1)S(1)}, bf16[8,512]{1,0:T(8,128)(2,1)S(1)}, u32[]{:S(2)}, u32[]{:S(2)}) %collective-permute-start.5) | collective-permute-done | bytes 8224 | tf_op jit(solution)/shard_map/ppermute | solution.py:328
  22.1 0.1 collective-permute-start.6
  22.1 1.6 %collective-permute-start.7 = (bf16[8,512]{1,0:T(8,128)(2,1)S(1)}, bf16[8,512]{1,0:T(8,128)(2,1)S(1)}, u32[]{:S(2)}, u32[]{:S(2)}) collective-permute-start(bf16[8,512]{1,0:T(8,128)(2,1)S(1)} %get-tuple-element.49), channel_id=1, source_target_pairs={{0,2},{1,3},{2,0},{3,1},{4,6},{5,7},{6,4},{7,5},{8,10},{9,11},{10,... | collective-permute-start | bytes 24584 | tf_op jit(solution)/shard_map/ppermute | solution.py:328
  23.7 0.3 collective-permute-start.8
  24.0 0.9 %collective-permute-done.4.got = bf16[4,64,256]{2,1,0:T(8,128)(2,1)S(1)} collective-permute-done((bf16[4,64,256]{2,1,0:T(8,128)(2,1)S(1)}, bf16[4,64,256]{2,1,0:T(8,128)(2,1)S(1)}, u32[]{:S(2)}, u32[]{:S(2)}) %collective-permute-start.4) | collective-permute-done | bytes 131104 | tf_op jit(solution)/shard_map/ppermute | solution.py:328
  24.9 0.2 shard_map.82
  25.2 0.8 %copy.8 = bf16[32,64,128]{2,1,0:T(8,128)(2,1)} copy(bf16[32,64,128]{2,1,0:T(8,128)(2,1)S(1)} %get-tuple-element.54) | data formatting | bytes 1048576
  25.9 0.0 collective-permute-done.6.refs_1_
  26.0 0.0 collective-permute-done.7.refs_2_
  26.0 0.0 collective-permute-done.8.refs_3_
  26.0 0.9 %shard_map.84 = f32[128,512]{1,0:T(8,128)} custom-call(f32[8,512]{1,0:T(8,128)S(1)} %get-tuple-element.47.refs_0_, bf16[8,512]{1,0:T(8,128)(2,1)S(1)} %collective-permute-done.6.refs_1_, bf16[8,512]{1,0:T(8,128)(2,1)S(1)} %collective-permute-done.7.refs_2_, bf16[8,512]{1,0:T(8,128)(2,1)S(1)} %collective-permute-done.8.refs_3_, ...), custom_call_target="tpu_custom_call" | custom-call | tf_op jit(solution)/shard_map/pallas_call | solution.py:434
  (2 shorter events, 0.0 us)
Async XLA Ops:
  2.0 7.5 %collective-permute-start = (bf16[288,128]{1,0:T(8,128)(2,1)S(1)}, bf16[288,128]{1,0:T(8,128)(2,1)S(1)}, u32[]{:S(2)}, u32[]{:S(2)}) collective-permute-start(bf16[288,128]{1,0:T(8,128)(2,1)S(1)} %get-tuple-element.29), channel_id=1, source_target_pairs={{0,4},{4,0},{8,12},{12,8},{16,20},{20,16},{24,28},{28,24},{1,5},{5... | collective-permute-start | bytes 221192 | tf_op jit(solution)/shard_map/ppermute | solution.py:328
  5.0 12.7 %collective-permute-start.3 = (bf16[4,2,64,128]{3,2,1,0:T(8,128)(2,1)S(1)}, bf16[4,2,64,128]{3,2,1,0:T(8,128)(2,1)S(1)}, u32[]{:S(2)}, u32[]{:S(2)}) collective-permute-start(bf16[4,2,64,128]{3,2,1,0:T(8,128)(2,1)S(1)} %get-tuple-element.30.refs_0_), channel_id=1, source_target_pairs={{0,24},{4,28},{8,16},{12,20},{16,0},{20,4},{24,8},{28,12},{1,25},{... | collective-permute-start | bytes 393224 | tf_op jit(solution)/shard_map/ppermute | solution.py:379
  8.6 9.2 %collective-permute-start.2 = (bf16[4,2,64,128]{3,2,1,0:T(8,128)(2,1)S(1)}, bf16[4,2,64,128]{3,2,1,0:T(8,128)(2,1)S(1)}, u32[]{:S(2)}, u32[]{:S(2)}) collective-permute-start(bf16[4,2,64,128]{3,2,1,0:T(8,128)(2,1)S(1)} %get-tuple-element.30.refs_0_), channel_id=1, source_target_pairs={{0,8},{4,12},{8,0},{12,4},{16,24},{20,28},{24,16},{28,20},{1,9},{5... | collective-permute-start | bytes 393224 | tf_op jit(solution)/shard_map/ppermute | solution.py:379
  8.6 9.2 %collective-permute-start.1 = (bf16[4,2,64,128]{3,2,1,0:T(8,128)(2,1)S(1)}, bf16[4,2,64,128]{3,2,1,0:T(8,128)(2,1)S(1)}, u32[]{:S(2)}, u32[]{:S(2)}) collective-permute-start(bf16[4,2,64,128]{3,2,1,0:T(8,128)(2,1)S(1)} %get-tuple-element.30.refs_0_), channel_id=1, source_target_pairs={{0,16},{4,20},{8,24},{12,28},{16,8},{20,12},{24,0},{28,4},{1,17},{... | collective-permute-start | bytes 393224 | tf_op jit(solution)/shard_map/ppermute | solution.py:379
  18.3 3.7 %collective-permute-start.5 = (bf16[8,512]{1,0:T(8,128)(2,1)S(1)}, bf16[8,512]{1,0:T(8,128)(2,1)S(1)}, u32[]{:S(2)}, u32[]{:S(2)}) collective-permute-start(bf16[8,512]{1,0:T(8,128)(2,1)S(1)} %get-tuple-element.46), channel_id=1, source_target_pairs={{0,4},{4,0},{8,12},{12,8},{16,20},{20,16},{24,28},{28,24},{1,5},{5... | collective-permute-start | bytes 24584 | tf_op jit(solution)/shard_map/ppermute | solution.py:328
  19.9 5.0 %collective-permute-start.4 = (bf16[4,64,256]{2,1,0:T(8,128)(2,1)S(1)}, bf16[4,64,256]{2,1,0:T(8,128)(2,1)S(1)}, u32[]{:S(2)}, u32[]{:S(2)}) collective-permute-start(bf16[4,64,256]{2,1,0:T(8,128)(2,1)S(1)} %get-tuple-element.43), channel_id=1, source_target_pairs={{0,4},{4,0},{8,12},{12,8},{16,20},{20,16},{24,28},{28,24},{1,5},{5... | collective-permute-start | bytes 393224 | tf_op jit(solution)/shard_map/ppermute | solution.py:328
  22.1 3.9 %collective-permute-start.6 = (bf16[8,512]{1,0:T(8,128)(2,1)S(1)}, bf16[8,512]{1,0:T(8,128)(2,1)S(1)}, u32[]{:S(2)}, u32[]{:S(2)}) collective-permute-start(bf16[8,512]{1,0:T(8,128)(2,1)S(1)} %get-tuple-element.48), channel_id=1, source_target_pairs={{0,3},{1,2},{2,1},{3,0},{4,7},{5,6},{6,5},{7,4},{8,11},{9,10},{10,... | collective-permute-start | bytes 24584 | tf_op jit(solution)/shard_map/ppermute | solution.py:328
  22.1 3.8 %collective-permute-start.7 = (bf16[8,512]{1,0:T(8,128)(2,1)S(1)}, bf16[8,512]{1,0:T(8,128)(2,1)S(1)}, u32[]{:S(2)}, u32[]{:S(2)}) collective-permute-start(bf16[8,512]{1,0:T(8,128)(2,1)S(1)} %get-tuple-element.49), channel_id=1, source_target_pairs={{0,2},{1,3},{2,0},{3,1},{4,6},{5,7},{6,4},{7,5},{8,10},{9,11},{10,... | collective-permute-start | bytes 24584 | tf_op jit(solution)/shard_map/ppermute | solution.py:328
  23.7 2.2 %collective-permute-start.8 = (bf16[8,512]{1,0:T(8,128)(2,1)S(1)}, bf16[8,512]{1,0:T(8,128)(2,1)S(1)}, u32[]{:S(2)}, u32[]{:S(2)}) collective-permute-start(bf16[8,512]{1,0:T(8,128)(2,1)S(1)} %get-tuple-element.50), channel_id=1, source_target_pairs={{0,1},{1,0},{2,3},{3,2},{4,5},{5,4},{6,7},{7,6},{8,9},{9,8},{10,11... | collective-permute-start | bytes 24584 | tf_op jit(solution)/shard_map/ppermute | solution.py:328

commit v5 on v4

--- a/solution.py
+++ b/solution.py
@@ -239,8 +239,8 @@
 
 def own_stack_kernel(levels, left, *refs):
     (
-        theirs, held, aperture, shot_weight, kinds, tiles_near,
-        mine, columns, tiles_turned, chosen, send,
+        held, aperture, shot_weight, kinds, tiles_near,
+        mine, columns, tiles_turned, chosen,
     ) = refs[levels:]
     blocks = level_blocks(refs[:levels], levels)
     for freq in range(NF):
@@ -254,8 +254,7 @@
         columns[band] = subtract_waves(band, sums, waves)
     tiles_turned[...] = tiles_near[...].astype(F32).T.astype(BF16)
     kind = lax.broadcasted_iota(jnp.int32, chosen.shape, 0)
-    chosen[...] = jnp.where(kinds[...] == kind, 1.0, 0.0)
-    send[...] = theirs[...]
+    chosen[...] = jnp.where(kinds[...][:, None, :] == kind, 1.0, 0.0)
 
 
 def column_kernel(columns, got, *refs):
@@ -296,7 +295,7 @@
     steps, panel = column_stack.shape
     kinds = chosen.shape[0]
     rounded = column_stack.astype(BF16).astype(F32)
-    widened = jnp.where(chosen[...][:, None, :] > 0.5, rounded[None], 0.0)
+    widened = jnp.where(chosen[...] > 0.5, rounded[None], 0.0)
     image[...] = dot(tiles_turned[...], widened.reshape(kinds * steps, panel).astype(BF16))
 
 
@@ -398,20 +397,19 @@
         [WHOLE] * 2,
     )(*in_vmem(left, *rights, their_aperture, their_weight))
     got_waves = swap(waves, "row", rows, 1)
-    mine, columns, tiles_turned, chosen, send = call(
+    mine, columns, tiles_turned, chosen = call(
         functools.partial(own_stack_kernel, levels),
         [
             part,
             pltpu.VMEM((cols, steps, panel), F32),
             pltpu.VMEM((depth, kinds * steps), BF16),
-            pltpu.VMEM((kinds, panel), F32),
-            part,
+            pltpu.VMEM((kinds, steps, panel), F32),
         ],
-        [WHOLE] * (levels + 7),
-        [WHOLE] * 5,
+        [WHOLE] * (levels + 6),
+        [WHOLE] * 4,
         flops=1 << 34,
-    )(*in_vmem(left, *rights, theirs, held, aperture, shot_weight, near_kinds, tiles_near))
-    got_part = swap(send, "row", rows, 1)
+    )(*in_vmem(left, *rights, held, aperture, shot_weight, near_kinds, tiles_near))
+    got_part = swap(theirs, "row", rows, 1)
     band = pltpu.VMEM((steps, panel), F32)
     own, *sends = call(
         column_kernel,

time: 27 us -> 27 us (level)
  transfers between devices with their start and end apart: 9 -> 9, of which waited for: 4 -> 5; matrix products, arithmetic and copies ran while one was open for 3% -> 3% of each run, Pallas kernels for 6% -> 6%
where the time goes in v5:
time: 27 us; the launch traced here: 26.8 us
  starting transfers between devices  11.5 us (43%)
  blocking collectives  7.2 us (27%)
  Pallas kernels  4.41 us (16%)
  waiting for transfers between devices  2.22 us (8%)
  local copies, waits for them, and re-layouts  0.8 us (3%)
  between operations  0.69 us (3%)
    all_gather x1, blocking collectives, per_device(): left = lax.all_gather(both, 'col')  7.2 us
    ppermute x6, starting transfers between devices, swap(): return lax.ppermute(array, axis, [(i, i ^ offset) for i in range(size)])  7.01 us
    ppermute x3, starting transfers between devices, per_device(): lax.ppermute(planes, 'row', [(2 * a + x, 2 * b + x) for a, b in enumerate...  4.5 us
    ppermute x6, waiting for transfers between devices, swap(): return lax.ppermute(array, axis, [(i, i ^ offset) for i in range(size)])  1.49 us
    pallas_call x1, Pallas kernels, per_device(): call(spectra_kernel, [pltpu.VMEM(traces.shape, BF16), pltpu.VMEM(plane_sh...  1.37 us
    pallas_call x1, Pallas kernels, per_device(): call(functools.partial(own_stack_kernel, levels), [part, pltpu.VMEM((cols...  1.07 us
    pallas_call x1, Pallas kernels, per_device(): call(functools.partial(image_kernel, shots, cols), jax.ShapeDtypeStruct((...  0.9 us
    unnamed x1, local copies, waits for them, and re-layouts  0.8 us
  transfers between devices with their start and end apart: 9, of which 5 were waited for; matrix products, arithmetic and copies ran while one was open for 3% of the time, Pallas kernels for 6%

profile of v5, /device:TPU:0, one launch (start us, length us, event | category | flops | bytes accessed | tf_op | source)
XLA Modules:
  0.0 26.8 jit_solution(14878961549831790363)
XLA Ops:
  0.6 1.4 %shard_map.77 = (bf16[32,64,128]{2,1,0:T(8,128)(2,1)S(1)}, bf16[4,2,64,128]{3,2,1,0:T(8,128)(2,1)S(1)}, bf16[4,64,128]{2,1,0:T(8,128)(2,1)S(1)}, bf16[288,128]{1...) custom-call(bf16[32,64,128]{2,1,0:T(8,128)(2,1)} %traces.1, ...), custom_call_target="tpu_custom_call" | custom-call | tf_op jit(solution)/shard_map/pallas_call | solution.py:347
  2.0 3.0 %collective-permute-start = (bf16[288,128]{1,0:T(8,128)(2,1)S(1)}, bf16[288,128]{1,0:T(8,128)(2,1)S(1)}, u32[]{:S(2)}, u32[]{:S(2)}) collective-permute-start(bf16[288,128]{1,0:T(8,128)(2,1)S(1)} %get-tuple-element.28), channel_id=1, source_target_pairs={{0,4},{4,0},{8,12},{12,8},{16,20},{20,16},{24,28},{28,24},{1,5},{5... | collective-permute-start | bytes 221192 | tf_op jit(solution)/shard_map/ppermute | solution.py:327
  5.0 3.6 %collective-permute-start.3 = (bf16[4,2,64,128]{3,2,1,0:T(8,128)(2,1)S(1)}, bf16[4,2,64,128]{3,2,1,0:T(8,128)(2,1)S(1)}, u32[]{:S(2)}, u32[]{:S(2)}) collective-permute-start(bf16[4,2,64,128]{3,2,1,0:T(8,128)(2,1)S(1)} %get-tuple-element.29.refs_0_), channel_id=1, source_target_pairs={{0,24},{4,28},{8,16},{12,20},{16,0},{20,4},{24,8},{28,12},{1,25},{... | collective-permute-start | bytes 393224 | tf_op jit(solution)/shard_map/ppermute | solution.py:378
  8.6 0.0 collective-permute-start.2
  8.6 0.9 %collective-permute-start.1 = (bf16[4,2,64,128]{3,2,1,0:T(8,128)(2,1)S(1)}, bf16[4,2,64,128]{3,2,1,0:T(8,128)(2,1)S(1)}, u32[]{:S(2)}, u32[]{:S(2)}) collective-permute-start(bf16[4,2,64,128]{3,2,1,0:T(8,128)(2,1)S(1)} %get-tuple-element.29.refs_0_), channel_id=1, source_target_pairs={{0,16},{4,20},{8,24},{12,28},{16,8},{20,12},{24,0},{28,4},{1,17},{... | collective-permute-start | bytes 393224 | tf_op jit(solution)/shard_map/ppermute | solution.py:378
  9.5 0.0 collective-permute-done.got
  9.5 7.2 %all-gather = bf16[8,4,64,128]{3,2,1,0:T(8,128)(2,1)S(1)} all-gather(bf16[2,4,64,128]{3,2,1,0:T(8,128)(2,1)S(1)} %shard_map.78), channel_id=2, replica_groups=mesh['row'=8,'col'=4] {'col'}, dimensions={0}, use_global_device_ids=true | all-gather | bytes 655360 | tf_op jit(solution)/shard_map/all_gather | solution.py:385
  16.7 0.3 %shard_map.79 = (bf16[128,512]{1,0:T(8,128)(2,1)S(1)}, f32[64,512]{1,0:T(8,128)S(1)}, bf16[128,512]{1,0:T(8,128)(2,1)S(1)}, f32[64,512]{1,0:T(8,128)S(1)}) custom-call(bf16[4,2,4,64,128]{4,3,2,1,0:T(8,128)(2,1)S(1)} %bitcast.5, bf16[288,128]{1,0:T(8,128)(2,1)S(1)} %collective-permute-done.got, s32[4,256]{1,0:T(4,128)S(1)} %get-tuple-element.31.lists, ...), custom_call_target="tpu_custom_call" | custom-call | tf_op jit(solution)/shard_map/pallas_call | solution.py:386
  17.1 0.6 %collective-permute-done.3.refs_3_ = bf16[4,2,64,128]{3,2,1,0:T(8,128)(2,1)S(1)} collective-permute-done((bf16[4,2,64,128]{3,2,1,0:T(8,128)(2,1)S(1)}, bf16[4,2,64,128]{3,2,1,0:T(8,128)(2,1)S(1)}, u32[]{:S(2)}, u32[]{:S(2)}) %collective-permute-start.3) | collective-permute-done | bytes 131104 | tf_op jit(solution)/shard_map/ppermute | solution.py:378
  17.7 0.1 collective-permute-done.2.refs_2_
  17.8 0.0 collective-permute-done.1.refs_1_
  17.8 0.5 %shard_map.81 = (bf16[4,64,256]{2,1,0:T(8,128)(2,1)S(1)}, bf16[8,512]{1,0:T(8,128)(2,1)S(1)}) custom-call(bf16[4,2,4,64,128]{4,3,2,1,0:T(8,128)(2,1)S(1)} %bitcast.6, bf16[4,2,64,128]{3,2,1,0:T(8,128)(2,1)S(1)} %get-tuple-element.29.refs_0_, bf16[4,2,64,128]{3,2,1,0:T(8,128)(2,1)S(1)} %collective-permute-done.1.refs_1_, ...), custom_call_target="tpu_custom_call" | custom-call | tf_op jit(solution)/shard_map/pallas_call | solution.py:393
  18.3 0.5 %collective-permute-start.5 = (bf16[8,512]{1,0:T(8,128)(2,1)S(1)}, bf16[8,512]{1,0:T(8,128)(2,1)S(1)}, u32[]{:S(2)}, u32[]{:S(2)}) collective-permute-start(bf16[8,512]{1,0:T(8,128)(2,1)S(1)} %get-tuple-element.44), channel_id=1, source_target_pairs={{0,4},{4,0},{8,12},{12,8},{16,20},{20,16},{24,28},{28,24},{1,5},{5... | collective-permute-start | bytes 24584 | tf_op jit(solution)/shard_map/ppermute | solution.py:327
  18.9 1.5 %collective-permute-start.4 = (bf16[4,64,256]{2,1,0:T(8,128)(2,1)S(1)}, bf16[4,64,256]{2,1,0:T(8,128)(2,1)S(1)}, u32[]{:S(2)}, u32[]{:S(2)}) collective-permute-start(bf16[4,64,256]{2,1,0:T(8,128)(2,1)S(1)} %get-tuple-element.41), channel_id=1, source_target_pairs={{0,4},{4,0},{8,12},{12,8},{16,20},{20,16},{24,28},{28,24},{1,5},{5... | collective-permute-start | bytes 393224 | tf_op jit(solution)/shard_map/ppermute | solution.py:327
  20.4 1.1 %shard_map.80 = (bf16[4,64,256]{2,1,0:T(8,128)(2,1)S(1)}, f32[4,8,512]{2,1,0:T(8,128)S(1)}, bf16[128,256]{1,0:T(8,128)(2,1)S(1)}, f32[32,8,512]{2,1,0:T(8,128)S(1)}) custom-call(bf16[4,2,4,64,128]{4,3,2,1,0:T(8,128)(2,1)S(1)} %bitcast.7, bf16[4,2,64,128]{3,2,1,0:T(8,128)(2,1)S(1)} %get-tuple-element.29.refs_0_, ...), custom_call_target="tpu_custom_call" | custom-call | flops 17179869184 | tf_op jit(solution)/shard_map/pallas_call | solution.py:400
  21.5 0.6 %collective-permute-done.5.got = bf16[8,512]{1,0:T(8,128)(2,1)S(1)} collective-permute-done((bf16[8,512]{1,0:T(8,128)(2,1)S(1)}, bf16[8,512]{1,0:T(8,128)(2,1)S(1)}, u32[]{:S(2)}, u32[]{:S(2)}) %collective-permute-start.5) | collective-permute-done | bytes 8224 | tf_op jit(solution)/shard_map/ppermute | solution.py:327
  22.1 0.1 collective-permute-start.6
  22.2 1.5 %collective-permute-start.7 = (bf16[8,512]{1,0:T(8,128)(2,1)S(1)}, bf16[8,512]{1,0:T(8,128)(2,1)S(1)}, u32[]{:S(2)}, u32[]{:S(2)}) collective-permute-start(bf16[8,512]{1,0:T(8,128)(2,1)S(1)} %get-tuple-element.47), channel_id=1, source_target_pairs={{0,2},{1,3},{2,0},{3,1},{4,6},{5,7},{6,4},{7,5},{8,10},{9,11},{10,... | collective-permute-start | bytes 24584 | tf_op jit(solution)/shard_map/ppermute | solution.py:327
  23.7 0.4 %collective-permute-start.8 = (bf16[8,512]{1,0:T(8,128)(2,1)S(1)}, bf16[8,512]{1,0:T(8,128)(2,1)S(1)}, u32[]{:S(2)}, u32[]{:S(2)}) collective-permute-start(bf16[8,512]{1,0:T(8,128)(2,1)S(1)} %get-tuple-element.48), channel_id=1, source_target_pairs={{0,1},{1,0},{2,3},{3,2},{4,5},{5,4},{6,7},{7,6},{8,9},{9,8},{10,11... | collective-permute-start | bytes 24584 | tf_op jit(solution)/shard_map/ppermute | solution.py:327
  24.1 0.0 collective-permute-done.4.got
  24.1 0.2 shard_map.82
  24.3 0.8 %copy.8 = bf16[32,64,128]{2,1,0:T(8,128)(2,1)} copy(bf16[32,64,128]{2,1,0:T(8,128)(2,1)S(1)} %get-tuple-element.52) | data formatting | bytes 1048576
  25.1 0.3 collective-permute-done.6.refs_1_
  25.3 0.6 %collective-permute-done.7.refs_2_ = bf16[8,512]{1,0:T(8,128)(2,1)S(1)} collective-permute-done((bf16[8,512]{1,0:T(8,128)(2,1)S(1)}, bf16[8,512]{1,0:T(8,128)(2,1)S(1)}, u32[]{:S(2)}, u32[]{:S(2)}) %collective-permute-start.7) | collective-permute-done | bytes 8224 | tf_op jit(solution)/shard_map/ppermute | solution.py:327
  25.9 0.0 collective-permute-done.8.refs_3_
  25.9 0.9 %shard_map.84 = f32[128,512]{1,0:T(8,128)} custom-call(f32[8,512]{1,0:T(8,128)S(1)} %get-tuple-element.45.refs_0_, bf16[8,512]{1,0:T(8,128)(2,1)S(1)} %collective-permute-done.6.refs_1_, bf16[8,512]{1,0:T(8,128)(2,1)S(1)} %collective-permute-done.7.refs_2_, bf16[8,512]{1,0:T(8,128)(2,1)S(1)} %collective-permute-done.8.refs_3_, ...), custom_call_target="tpu_custom_call" | custom-call | tf_op jit(solution)/shard_map/pallas_call | solution.py:432
  (2 shorter events, 0.0 us)
Async XLA Ops:
  2.0 7.5 %collective-permute-start = (bf16[288,128]{1,0:T(8,128)(2,1)S(1)}, bf16[288,128]{1,0:T(8,128)(2,1)S(1)}, u32[]{:S(2)}, u32[]{:S(2)}) collective-permute-start(bf16[288,128]{1,0:T(8,128)(2,1)S(1)} %get-tuple-element.28), channel_id=1, source_target_pairs={{0,4},{4,0},{8,12},{12,8},{16,20},{20,16},{24,28},{28,24},{1,5},{5... | collective-permute-start | bytes 221192 | tf_op jit(solution)/shard_map/ppermute | solution.py:327
  5.0 12.7 %collective-permute-start.3 = (bf16[4,2,64,128]{3,2,1,0:T(8,128)(2,1)S(1)}, bf16[4,2,64,128]{3,2,1,0:T(8,128)(2,1)S(1)}, u32[]{:S(2)}, u32[]{:S(2)}) collective-permute-start(bf16[4,2,64,128]{3,2,1,0:T(8,128)(2,1)S(1)} %get-tuple-element.29.refs_0_), channel_id=1, source_target_pairs={{0,24},{4,28},{8,16},{12,20},{16,0},{20,4},{24,8},{28,12},{1,25},{... | collective-permute-start | bytes 393224 | tf_op jit(solution)/shard_map/ppermute | solution.py:378
  8.6 9.2 %collective-permute-start.2 = (bf16[4,2,64,128]{3,2,1,0:T(8,128)(2,1)S(1)}, bf16[4,2,64,128]{3,2,1,0:T(8,128)(2,1)S(1)}, u32[]{:S(2)}, u32[]{:S(2)}) collective-permute-start(bf16[4,2,64,128]{3,2,1,0:T(8,128)(2,1)S(1)} %get-tuple-element.29.refs_0_), channel_id=1, source_target_pairs={{0,8},{4,12},{8,0},{12,4},{16,24},{20,28},{24,16},{28,20},{1,9},{5... | collective-permute-start | bytes 393224 | tf_op jit(solution)/shard_map/ppermute | solution.py:378
  8.6 9.2 %collective-permute-start.1 = (bf16[4,2,64,128]{3,2,1,0:T(8,128)(2,1)S(1)}, bf16[4,2,64,128]{3,2,1,0:T(8,128)(2,1)S(1)}, u32[]{:S(2)}, u32[]{:S(2)}) collective-permute-start(bf16[4,2,64,128]{3,2,1,0:T(8,128)(2,1)S(1)} %get-tuple-element.29.refs_0_), channel_id=1, source_target_pairs={{0,16},{4,20},{8,24},{12,28},{16,8},{20,12},{24,0},{28,4},{1,17},{... | collective-permute-start | bytes 393224 | tf_op jit(solution)/shard_map/ppermute | solution.py:378
  18.3 3.8 %collective-permute-start.5 = (bf16[8,512]{1,0:T(8,128)(2,1)S(1)}, bf16[8,512]{1,0:T(8,128)(2,1)S(1)}, u32[]{:S(2)}, u32[]{:S(2)}) collective-permute-start(bf16[8,512]{1,0:T(8,128)(2,1)S(1)} %get-tuple-element.44), channel_id=1, source_target_pairs={{0,4},{4,0},{8,12},{12,8},{16,20},{20,16},{24,28},{28,24},{1,5},{5... | collective-permute-start | bytes 24584 | tf_op jit(solution)/shard_map/ppermute | solution.py:327
  18.9 5.2 %collective-permute-start.4 = (bf16[4,64,256]{2,1,0:T(8,128)(2,1)S(1)}, bf16[4,64,256]{2,1,0:T(8,128)(2,1)S(1)}, u32[]{:S(2)}, u32[]{:S(2)}) collective-permute-start(bf16[4,64,256]{2,1,0:T(8,128)(2,1)S(1)} %get-tuple-element.41), channel_id=1, source_target_pairs={{0,4},{4,0},{8,12},{12,8},{16,20},{20,16},{24,28},{28,24},{1,5},{5... | collective-permute-start | bytes 393224 | tf_op jit(solution)/shard_map/ppermute | solution.py:327
  22.1 3.2 %collective-permute-start.6 = (bf16[8,512]{1,0:T(8,128)(2,1)S(1)}, bf16[8,512]{1,0:T(8,128)(2,1)S(1)}, u32[]{:S(2)}, u32[]{:S(2)}) collective-permute-start(bf16[8,512]{1,0:T(8,128)(2,1)S(1)} %get-tuple-element.46), channel_id=1, source_target_pairs={{0,3},{1,2},{2,1},{3,0},{4,7},{5,6},{6,5},{7,4},{8,11},{9,10},{10,... | collective-permute-start | bytes 24584 | tf_op jit(solution)/shard_map/ppermute | solution.py:327
  22.2 3.7 %collective-permute-start.7 = (bf16[8,512]{1,0:T(8,128)(2,1)S(1)}, bf16[8,512]{1,0:T(8,128)(2,1)S(1)}, u32[]{:S(2)}, u32[]{:S(2)}) collective-permute-start(bf16[8,512]{1,0:T(8,128)(2,1)S(1)} %get-tuple-element.47), channel_id=1, source_target_pairs={{0,2},{1,3},{2,0},{3,1},{4,6},{5,7},{6,4},{7,5},{8,10},{9,11},{10,... | collective-permute-start | bytes 24584 | tf_op jit(solution)/shard_map/ppermute | solution.py:327
  23.7 2.2 %collective-permute-start.8 = (bf16[8,512]{1,0:T(8,128)(2,1)S(1)}, bf16[8,512]{1,0:T(8,128)(2,1)S(1)}, u32[]{:S(2)}, u32[]{:S(2)}) collective-permute-start(bf16[8,512]{1,0:T(8,128)(2,1)S(1)} %get-tuple-element.48), channel_id=1, source_target_pairs={{0,1},{1,0},{2,3},{3,2},{4,5},{5,4},{6,7},{7,6},{8,9},{9,8},{10,11... | collective-permute-start | bytes 24584 | tf_op jit(solution)/shard_map/ppermute | solution.py:327

commit v6 on v5

--- a/solution.py
+++ b/solution.py
@@ -120,11 +120,17 @@
                 term = held[sample + turn * HALF_TURN, here].astype(F32)
                 total = total - term if turn % 2 else total + term
             folded.append(total)
-        for freq in range(NF):
-            pair = []
+        pairs = [[None, None] for _ in range(NF)]
+        for freq in range(NF // 2):
             for piece in range(2):
                 weights = [forward_weight(freq, piece, t, samples) for t in range(HALF_TURN)]
-                pair.append(weighted_sum(weights, folded))
+                even = weighted_sum(weights[0::2], folded[0::2])
+                odd = weighted_sum(weights[1::2], folded[1::2])
+                pairs[freq][piece] = even + odd
+                pairs[NF - 1 - freq][piece] = odd - even if piece else even - odd
+        for freq in range(NF):
+            pair = pairs[freq]
+            for piece in range(2):
                 planes[freq, piece, here] = pair[piece].astype(BF16)
             real, imag = pair
             turned = [pltpu.roll(p, receivers // 2, 1) for p in pair]

time: 27 us -> 27 us (level)
  no operation moved by 1% of the time
where the time goes in v6:
time: 27 us; the launch traced here: 26.8 us
  starting transfers between devices  11.5 us (43%)
  blocking collectives  7.2 us (27%)
  Pallas kernels  4.38 us (16%)
  waiting for transfers between devices  2.21 us (8%)
  local copies, waits for them, and re-layouts  0.8 us (3%)
  between operations  0.69 us (3%)
    all_gather x1, blocking collectives, per_device(): left = lax.all_gather(both, 'col')  7.2 us
    ppermute x6, starting transfers between devices, swap(): return lax.ppermute(array, axis, [(i, i ^ offset) for i in range(size)])  7.01 us
    ppermute x3, starting transfers between devices, per_device(): lax.ppermute(planes, 'row', [(2 * a + x, 2 * b + x) for a, b in enumerate...  4.5 us
    ppermute x6, waiting for transfers between devices, swap(): return lax.ppermute(array, axis, [(i, i ^ offset) for i in range(size)])  1.49 us
    pallas_call x1, Pallas kernels, per_device(): call(spectra_kernel, [pltpu.VMEM(traces.shape, BF16), pltpu.VMEM(plane_sh...  1.33 us
    pallas_call x1, Pallas kernels, per_device(): call(functools.partial(own_stack_kernel, levels), [part, pltpu.VMEM((cols...  1.07 us
    pallas_call x1, Pallas kernels, per_device(): call(functools.partial(image_kernel, shots, cols), jax.ShapeDtypeStruct((...  0.9 us
    unnamed x1, local copies, waits for them, and re-layouts  0.8 us
  transfers between devices with their start and end apart: 9, of which 5 were waited for; matrix products, arithmetic and copies ran while one was open for 3% of the time, Pallas kernels for 6%

profile of v6, /device:TPU:0, one launch (start us, length us, event | category | flops | bytes accessed | tf_op | source)
XLA Modules:
  0.0 26.8 jit_solution(13358176889440492234)
XLA Ops:
  0.6 1.3 %shard_map.77 = (bf16[32,64,128]{2,1,0:T(8,128)(2,1)S(1)}, bf16[4,2,64,128]{3,2,1,0:T(8,128)(2,1)S(1)}, bf16[4,64,128]{2,1,0:T(8,128)(2,1)S(1)}, bf16[288,128]{1...) custom-call(bf16[32,64,128]{2,1,0:T(8,128)(2,1)} %traces.1, ...), custom_call_target="tpu_custom_call" | custom-call | tf_op jit(solution)/shard_map/pallas_call | solution.py:353
  2.0 3.0 %collective-permute-start = (bf16[288,128]{1,0:T(8,128)(2,1)S(1)}, bf16[288,128]{1,0:T(8,128)(2,1)S(1)}, u32[]{:S(2)}, u32[]{:S(2)}) collective-permute-start(bf16[288,128]{1,0:T(8,128)(2,1)S(1)} %get-tuple-element.28), channel_id=1, source_target_pairs={{0,4},{4,0},{8,12},{12,8},{16,20},{20,16},{24,28},{28,24},{1,5},{5... | collective-permute-start | bytes 221192 | tf_op jit(solution)/shard_map/ppermute | solution.py:333
  5.0 3.6 %collective-permute-start.3 = (bf16[4,2,64,128]{3,2,1,0:T(8,128)(2,1)S(1)}, bf16[4,2,64,128]{3,2,1,0:T(8,128)(2,1)S(1)}, u32[]{:S(2)}, u32[]{:S(2)}) collective-permute-start(bf16[4,2,64,128]{3,2,1,0:T(8,128)(2,1)S(1)} %get-tuple-element.29.refs_0_), channel_id=1, source_target_pairs={{0,24},{4,28},{8,16},{12,20},{16,0},{20,4},{24,8},{28,12},{1,25},{... | collective-permute-start | bytes 393224 | tf_op jit(solution)/shard_map/ppermute | solution.py:384
  8.6 0.0 collective-permute-start.2
  8.6 0.9 %collective-permute-start.1 = (bf16[4,2,64,128]{3,2,1,0:T(8,128)(2,1)S(1)}, bf16[4,2,64,128]{3,2,1,0:T(8,128)(2,1)S(1)}, u32[]{:S(2)}, u32[]{:S(2)}) collective-permute-start(bf16[4,2,64,128]{3,2,1,0:T(8,128)(2,1)S(1)} %get-tuple-element.29.refs_0_), channel_id=1, source_target_pairs={{0,16},{4,20},{8,24},{12,28},{16,8},{20,12},{24,0},{28,4},{1,17},{... | collective-permute-start | bytes 393224 | tf_op jit(solution)/shard_map/ppermute | solution.py:384
  9.5 0.0 collective-permute-done.got
  9.5 7.2 %all-gather = bf16[8,4,64,128]{3,2,1,0:T(8,128)(2,1)S(1)} all-gather(bf16[2,4,64,128]{3,2,1,0:T(8,128)(2,1)S(1)} %shard_map.78), channel_id=2, replica_groups=mesh['row'=8,'col'=4] {'col'}, dimensions={0}, use_global_device_ids=true | all-gather | bytes 655360 | tf_op jit(solution)/shard_map/all_gather | solution.py:391
  16.7 0.3 %shard_map.79 = (bf16[128,512]{1,0:T(8,128)(2,1)S(1)}, f32[64,512]{1,0:T(8,128)S(1)}, bf16[128,512]{1,0:T(8,128)(2,1)S(1)}, f32[64,512]{1,0:T(8,128)S(1)}) custom-call(bf16[4,2,4,64,128]{4,3,2,1,0:T(8,128)(2,1)S(1)} %bitcast.5, bf16[288,128]{1,0:T(8,128)(2,1)S(1)} %collective-permute-done.got, s32[4,256]{1,0:T(4,128)S(1)} %get-tuple-element.31.lists, ...), custom_call_target="tpu_custom_call" | custom-call | tf_op jit(solution)/shard_map/pallas_call | solution.py:392
  17.0 0.6 %collective-permute-done.3.refs_3_ = bf16[4,2,64,128]{3,2,1,0:T(8,128)(2,1)S(1)} collective-permute-done((bf16[4,2,64,128]{3,2,1,0:T(8,128)(2,1)S(1)}, bf16[4,2,64,128]{3,2,1,0:T(8,128)(2,1)S(1)}, u32[]{:S(2)}, u32[]{:S(2)}) %collective-permute-start.3) | collective-permute-done | bytes 131104 | tf_op jit(solution)/shard_map/ppermute | solution.py:384
  17.6 0.1 collective-permute-done.2.refs_2_
  17.8 0.0 collective-permute-done.1.refs_1_
  17.8 0.5 %shard_map.81 = (bf16[4,64,256]{2,1,0:T(8,128)(2,1)S(1)}, bf16[8,512]{1,0:T(8,128)(2,1)S(1)}) custom-call(bf16[4,2,4,64,128]{4,3,2,1,0:T(8,128)(2,1)S(1)} %bitcast.6, bf16[4,2,64,128]{3,2,1,0:T(8,128)(2,1)S(1)} %get-tuple-element.29.refs_0_, bf16[4,2,64,128]{3,2,1,0:T(8,128)(2,1)S(1)} %collective-permute-done.1.refs_1_, ...), custom_call_target="tpu_custom_call" | custom-call | tf_op jit(solution)/shard_map/pallas_call | solution.py:399
  18.3 0.5 %collective-permute-start.5 = (bf16[8,512]{1,0:T(8,128)(2,1)S(1)}, bf16[8,512]{1,0:T(8,128)(2,1)S(1)}, u32[]{:S(2)}, u32[]{:S(2)}) collective-permute-start(bf16[8,512]{1,0:T(8,128)(2,1)S(1)} %get-tuple-element.44), channel_id=1, source_target_pairs={{0,4},{4,0},{8,12},{12,8},{16,20},{20,16},{24,28},{28,24},{1,5},{5... | collective-permute-start | bytes 24584 | tf_op jit(solution)/shard_map/ppermute | solution.py:333
  18.8 1.5 %collective-permute-start.4 = (bf16[4,64,256]{2,1,0:T(8,128)(2,1)S(1)}, bf16[4,64,256]{2,1,0:T(8,128)(2,1)S(1)}, u32[]{:S(2)}, u32[]{:S(2)}) collective-permute-start(bf16[4,64,256]{2,1,0:T(8,128)(2,1)S(1)} %get-tuple-element.41), channel_id=1, source_target_pairs={{0,4},{4,0},{8,12},{12,8},{16,20},{20,16},{24,28},{28,24},{1,5},{5... | collective-permute-start | bytes 393224 | tf_op jit(solution)/shard_map/ppermute | solution.py:333
  20.4 1.1 %shard_map.80 = (bf16[4,64,256]{2,1,0:T(8,128)(2,1)S(1)}, f32[4,8,512]{2,1,0:T(8,128)S(1)}, bf16[128,256]{1,0:T(8,128)(2,1)S(1)}, f32[32,8,512]{2,1,0:T(8,128)S(1)}) custom-call(bf16[4,2,4,64,128]{4,3,2,1,0:T(8,128)(2,1)S(1)} %bitcast.7, bf16[4,2,64,128]{3,2,1,0:T(8,128)(2,1)S(1)} %get-tuple-element.29.refs_0_, ...), custom_call_target="tpu_custom_call" | custom-call | flops 17179869184 | tf_op jit(solution)/shard_map/pallas_call | solution.py:406
  21.4 0.6 %collective-permute-done.5.got = bf16[8,512]{1,0:T(8,128)(2,1)S(1)} collective-permute-done((bf16[8,512]{1,0:T(8,128)(2,1)S(1)}, bf16[8,512]{1,0:T(8,128)(2,1)S(1)}, u32[]{:S(2)}, u32[]{:S(2)}) %collective-permute-start.5) | collective-permute-done | bytes 8224 | tf_op jit(solution)/shard_map/ppermute | solution.py:333
  22.1 0.1 collective-permute-start.6
  22.2 1.5 %collective-permute-start.7 = (bf16[8,512]{1,0:T(8,128)(2,1)S(1)}, bf16[8,512]{1,0:T(8,128)(2,1)S(1)}, u32[]{:S(2)}, u32[]{:S(2)}) collective-permute-start(bf16[8,512]{1,0:T(8,128)(2,1)S(1)} %get-tuple-element.47), channel_id=1, source_target_pairs={{0,2},{1,3},{2,0},{3,1},{4,6},{5,7},{6,4},{7,5},{8,10},{9,11},{10,... | collective-permute-start | bytes 24584 | tf_op jit(solution)/shard_map/ppermute | solution.py:333
  23.7 0.4 %collective-permute-start.8 = (bf16[8,512]{1,0:T(8,128)(2,1)S(1)}, bf16[8,512]{1,0:T(8,128)(2,1)S(1)}, u32[]{:S(2)}, u32[]{:S(2)}) collective-permute-start(bf16[8,512]{1,0:T(8,128)(2,1)S(1)} %get-tuple-element.48), channel_id=1, source_target_pairs={{0,1},{1,0},{2,3},{3,2},{4,5},{5,4},{6,7},{7,6},{8,9},{9,8},{10,11... | collective-permute-start | bytes 24584 | tf_op jit(solution)/shard_map/ppermute | solution.py:333
  24.0 0.0 collective-permute-done.4.got
  24.0 0.2 shard_map.82
  24.2 0.8 %copy.8 = bf16[32,64,128]{2,1,0:T(8,128)(2,1)} copy(bf16[32,64,128]{2,1,0:T(8,128)(2,1)S(1)} %get-tuple-element.52) | data formatting | bytes 1048576
  25.0 0.3 collective-permute-done.6.refs_1_
  25.3 0.6 %collective-permute-done.7.refs_2_ = bf16[8,512]{1,0:T(8,128)(2,1)S(1)} collective-permute-done((bf16[8,512]{1,0:T(8,128)(2,1)S(1)}, bf16[8,512]{1,0:T(8,128)(2,1)S(1)}, u32[]{:S(2)}, u32[]{:S(2)}) %collective-permute-start.7) | collective-permute-done | bytes 8224 | tf_op jit(solution)/shard_map/ppermute | solution.py:333
  25.9 0.0 collective-permute-done.8.refs_3_
  25.9 0.9 %shard_map.84 = f32[128,512]{1,0:T(8,128)} custom-call(f32[8,512]{1,0:T(8,128)S(1)} %get-tuple-element.45.refs_0_, bf16[8,512]{1,0:T(8,128)(2,1)S(1)} %collective-permute-done.6.refs_1_, bf16[8,512]{1,0:T(8,128)(2,1)S(1)} %collective-permute-done.7.refs_2_, bf16[8,512]{1,0:T(8,128)(2,1)S(1)} %collective-permute-done.8.refs_3_, ...), custom_call_target="tpu_custom_call" | custom-call | tf_op jit(solution)/shard_map/pallas_call | solution.py:438
  (2 shorter events, 0.0 us)
Async XLA Ops:
  2.0 7.5 %collective-permute-start = (bf16[288,128]{1,0:T(8,128)(2,1)S(1)}, bf16[288,128]{1,0:T(8,128)(2,1)S(1)}, u32[]{:S(2)}, u32[]{:S(2)}) collective-permute-start(bf16[288,128]{1,0:T(8,128)(2,1)S(1)} %get-tuple-element.28), channel_id=1, source_target_pairs={{0,4},{4,0},{8,12},{12,8},{16,20},{20,16},{24,28},{28,24},{1,5},{5... | collective-permute-start | bytes 221192 | tf_op jit(solution)/shard_map/ppermute | solution.py:333
  5.0 12.7 %collective-permute-start.3 = (bf16[4,2,64,128]{3,2,1,0:T(8,128)(2,1)S(1)}, bf16[4,2,64,128]{3,2,1,0:T(8,128)(2,1)S(1)}, u32[]{:S(2)}, u32[]{:S(2)}) collective-permute-start(bf16[4,2,64,128]{3,2,1,0:T(8,128)(2,1)S(1)} %get-tuple-element.29.refs_0_), channel_id=1, source_target_pairs={{0,24},{4,28},{8,16},{12,20},{16,0},{20,4},{24,8},{28,12},{1,25},{... | collective-permute-start | bytes 393224 | tf_op jit(solution)/shard_map/ppermute | solution.py:384
  8.6 9.2 %collective-permute-start.2 = (bf16[4,2,64,128]{3,2,1,0:T(8,128)(2,1)S(1)}, bf16[4,2,64,128]{3,2,1,0:T(8,128)(2,1)S(1)}, u32[]{:S(2)}, u32[]{:S(2)}) collective-permute-start(bf16[4,2,64,128]{3,2,1,0:T(8,128)(2,1)S(1)} %get-tuple-element.29.refs_0_), channel_id=1, source_target_pairs={{0,8},{4,12},{8,0},{12,4},{16,24},{20,28},{24,16},{28,20},{1,9},{5... | collective-permute-start | bytes 393224 | tf_op jit(solution)/shard_map/ppermute | solution.py:384
  8.6 9.2 %collective-permute-start.1 = (bf16[4,2,64,128]{3,2,1,0:T(8,128)(2,1)S(1)}, bf16[4,2,64,128]{3,2,1,0:T(8,128)(2,1)S(1)}, u32[]{:S(2)}, u32[]{:S(2)}) collective-permute-start(bf16[4,2,64,128]{3,2,1,0:T(8,128)(2,1)S(1)} %get-tuple-element.29.refs_0_), channel_id=1, source_target_pairs={{0,16},{4,20},{8,24},{12,28},{16,8},{20,12},{24,0},{28,4},{1,17},{... | collective-permute-start | bytes 393224 | tf_op jit(solution)/shard_map/ppermute | solution.py:384
  18.3 3.8 %collective-permute-start.5 = (bf16[8,512]{1,0:T(8,128)(2,1)S(1)}, bf16[8,512]{1,0:T(8,128)(2,1)S(1)}, u32[]{:S(2)}, u32[]{:S(2)}) collective-permute-start(bf16[8,512]{1,0:T(8,128)(2,1)S(1)} %get-tuple-element.44), channel_id=1, source_target_pairs={{0,4},{4,0},{8,12},{12,8},{16,20},{20,16},{24,28},{28,24},{1,5},{5... | collective-permute-start | bytes 24584 | tf_op jit(solution)/shard_map/ppermute | solution.py:333
  18.8 5.2 %collective-permute-start.4 = (bf16[4,64,256]{2,1,0:T(8,128)(2,1)S(1)}, bf16[4,64,256]{2,1,0:T(8,128)(2,1)S(1)}, u32[]{:S(2)}, u32[]{:S(2)}) collective-permute-start(bf16[4,64,256]{2,1,0:T(8,128)(2,1)S(1)} %get-tuple-element.41), channel_id=1, source_target_pairs={{0,4},{4,0},{8,12},{12,8},{16,20},{20,16},{24,28},{28,24},{1,5},{5... | collective-permute-start | bytes 393224 | tf_op jit(solution)/shard_map/ppermute | solution.py:333
  22.1 3.2 %collective-permute-start.6 = (bf16[8,512]{1,0:T(8,128)(2,1)S(1)}, bf16[8,512]{1,0:T(8,128)(2,1)S(1)}, u32[]{:S(2)}, u32[]{:S(2)}) collective-permute-start(bf16[8,512]{1,0:T(8,128)(2,1)S(1)} %get-tuple-element.46), channel_id=1, source_target_pairs={{0,3},{1,2},{2,1},{3,0},{4,7},{5,6},{6,5},{7,4},{8,11},{9,10},{10,... | collective-permute-start | bytes 24584 | tf_op jit(solution)/shard_map/ppermute | solution.py:333
  22.2 3.7 %collective-permute-start.7 = (bf16[8,512]{1,0:T(8,128)(2,1)S(1)}, bf16[8,512]{1,0:T(8,128)(2,1)S(1)}, u32[]{:S(2)}, u32[]{:S(2)}) collective-permute-start(bf16[8,512]{1,0:T(8,128)(2,1)S(1)} %get-tuple-element.47), channel_id=1, source_target_pairs={{0,2},{1,3},{2,0},{3,1},{4,6},{5,7},{6,4},{7,5},{8,10},{9,11},{10,... | collective-permute-start | bytes 24584 | tf_op jit(solution)/shard_map/ppermute | solution.py:333
  23.7 2.2 %collective-permute-start.8 = (bf16[8,512]{1,0:T(8,128)(2,1)S(1)}, bf16[8,512]{1,0:T(8,128)(2,1)S(1)}, u32[]{:S(2)}, u32[]{:S(2)}) collective-permute-start(bf16[8,512]{1,0:T(8,128)(2,1)S(1)} %get-tuple-element.48), channel_id=1, source_target_pairs={{0,1},{1,0},{2,3},{3,2},{4,5},{5,4},{6,7},{7,6},{8,9},{9,8},{10,11... | collective-permute-start | bytes 24584 | tf_op jit(solution)/shard_map/ppermute | solution.py:333
